TPU v7x, 512 devices: a whole 4x4x16 slice. The times are simulated.
512 devices in a mesh: dp: 4 (over z_lo), expert: 128 (over y, x, z_hi, core).
Axes of the slice: x: 4, y: 4, z: 16 (z_hi: 4, z_lo: 4; z = z_hi * 4 + z_lo), core: 2. Of those that a mesh axis runs over, the one named last changes fastest.
Arguments:
- hidden_in: bfloat16 [2, 8192, 2048], P(None, ('dp', 'expert')), may hold values from -6 to 6
- cotangent: bfloat16 [2, 8192, 2048], P(None, ('dp', 'expert')), may hold values from -6 to 6
- expert_ids: int32 [2, 8192, 8], P(None, ('dp', 'expert')), may hold values from 0 to 127, all different within a row; in each aligned block of 16 rows (0 to 15, 16 to 31, ..., all dimensions but the last counted through in order) at most 2 rows name the same one
- route_prob: float32 [2, 8192, 8], P(None, ('dp', 'expert')), may hold values from 0.05 to 1
- swap_flags: int32 [64], replicated, may hold values 0 or 1
- gate_up: bfloat16 [128, 2048, 2, 384], P('expert', 'dp'), may hold values from -0.125 to 0.125
- down_t: bfloat16 [128, 2048, 384], P('expert', 'dp'), may hold values from -0.3125 to 0.3125
Outputs:
- hidden_out: bfloat16 [2, 8192, 2048], P(None, ('dp', 'expert'))
- input_grad: bfloat16 [2, 8192, 2048], P(None, ('dp', 'expert'))
- resident_gate_up: bfloat16 [128, 2048, 2, 384], P('expert', 'dp')
- resident_down: bfloat16 [128, 2048, 384], P('expert', 'dp')
Inputs may be any that keep to these rules, and one draw needn't show every extreme that they name: `expert_ids`: within one microbatch the 16 tokens of one device name any one expert at most 2 times, a bound that some block reaches.
All inputs are finite; a program needn't handle non-finite values.
Results may differ from a plain program's by a relative error of at most 0.0064.
Values may be sent and summed in bfloat16 or wider, within the bound.
No kernel may reach another device: no remote copies, remote signals or barrier semaphores. Data moves between devices by JAX's collectives and lax.ppermute only.
A program may use at most 64 MiB of HBM per device.

v0:
```python
import jax
import jax.numpy as jnp
from jax import lax
from jax.sharding import PartitionSpec as P


def from_partner(value, axis, stride):
    mask = 2**stride
    pairs = [(source, source ^ mask) for source in range(lax.axis_size(axis))]
    return lax.ppermute(value, axis, pairs)


def expert_forward(row_block, gate_matrix, down_matrix):
    hidden_width = down_matrix.shape[1]
    projected = jnp.dot(row_block, gate_matrix, preferred_element_type=jnp.float32)
    gate_part = projected[:, :hidden_width]
    upper_part = projected[:, hidden_width:]
    hidden = (jax.nn.silu(gate_part) * upper_part).astype(jnp.bfloat16)
    output = lax.dot_general(
        hidden, down_matrix, (((1,), (1,)), ((), ())), preferred_element_type=jnp.float32
    )
    return (output.astype(jnp.bfloat16), projected)


def expert_backward(grad_block, projected, gate_matrix, down_matrix):
    hidden_width = down_matrix.shape[1]
    gate_part = projected[:, :hidden_width]
    upper_part = projected[:, hidden_width:]
    d_hidden = jnp.dot(grad_block, down_matrix, preferred_element_type=jnp.float32)
    sigmoid_gate = jax.nn.sigmoid(gate_part)
    d_gate = (
        d_hidden * upper_part * sigmoid_gate * (1.0 + gate_part * (1.0 - sigmoid_gate))
    ).astype(jnp.bfloat16)
    d_upper = (d_hidden * gate_part * sigmoid_gate).astype(jnp.bfloat16)
    d_joined = jnp.concatenate([d_gate, d_upper], axis=1)
    d_rows = lax.dot_general(
        d_joined, gate_matrix, (((1,), (1,)), ((), ())), preferred_element_type=jnp.float32
    )
    return d_rows.astype(jnp.bfloat16)


def route_matrix(ids_now, swap_flags, experts, slots, moved):
    token_count, top_count = ids_now.shape
    target = ids_now
    if moved:
        half_axis = experts // 2
        hit_mask = (ids_now % half_axis)[:, :, None] == jnp.arange(half_axis, dtype=jnp.int32)[
            None, None, :
        ]
        flipped = jnp.sum(jnp.where(hit_mask, swap_flags[None, None, :], 0), axis=2)
        target = jnp.where(flipped == 1, ids_now ^ half_axis, ids_now)
    flat_ids = target.reshape(token_count * top_count)
    one_hot = (flat_ids[:, None] == jnp.arange(experts, dtype=jnp.int32)[None, :]).astype(jnp.int32)
    earlier = jnp.cumsum(one_hot, axis=0) - one_hot
    slot_index = jnp.sum(earlier * one_hot, axis=1)
    slot_place = flat_ids * slots + slot_index
    picked = slot_place[:, None] == jnp.arange(experts * slots, dtype=jnp.int32)[None, :]
    return picked.astype(jnp.bfloat16)


def run_micro(tokens_now, grads_now, ids_now, weights_now, swap_flags, gate_full, down_full, moved):
    experts = lax.axis_size("expert")
    token_count, top_count = ids_now.shape
    model_width = tokens_now.shape[1]
    slots = 2 * token_count * top_count // experts
    picked = route_matrix(ids_now, swap_flags, experts, slots, moved)
    by_token = jnp.sum(picked.reshape(token_count, top_count, experts * slots), axis=1)
    first_axis = (((0,), (0,)), ((), ()))
    send_tokens = lax.dot_general(
        by_token, tokens_now, first_axis, preferred_element_type=jnp.float32
    )
    send_tokens = send_tokens.astype(jnp.bfloat16).reshape(experts, slots, model_width)
    row_grads = (weights_now[:, :, None] * grads_now[:, None, :].astype(jnp.float32)).astype(
        jnp.bfloat16
    )
    row_grads = row_grads.reshape(token_count * top_count, model_width)
    send_grads = lax.dot_general(picked, row_grads, first_axis, preferred_element_type=jnp.float32)
    send_grads = send_grads.astype(jnp.bfloat16).reshape(experts, slots, model_width)
    gate_matrix = gate_full.reshape(model_width, -1)
    down_matrix = down_full.reshape(model_width, -1)
    pieces = lax.all_to_all(send_tokens, "expert", split_axis=0, concat_axis=0, tiled=True)
    item_count = pieces.shape[1]
    expert_out, projected = expert_forward(
        pieces.reshape(experts * item_count, model_width), gate_matrix, down_matrix
    )
    returned = lax.all_to_all(
        expert_out.reshape(experts, item_count, model_width),
        "expert",
        split_axis=0,
        concat_axis=0,
        tiled=True,
    )
    saved = projected.reshape(experts, item_count, projected.shape[1])
    arrived = lax.all_to_all(send_grads, "expert", split_axis=0, concat_axis=0, tiled=True)
    row_input = expert_backward(
        arrived.reshape(experts * slots, model_width),
        saved.reshape(experts * slots, saved.shape[2]),
        gate_matrix,
        down_matrix,
    )
    back_grad = lax.all_to_all(
        row_input.reshape(experts, slots, model_width),
        "expert",
        split_axis=0,
        concat_axis=0,
        tiled=True,
    )
    back_rows = jnp.dot(
        picked, returned.reshape(experts * slots, model_width), preferred_element_type=jnp.float32
    )
    back_rows = back_rows.reshape(token_count, top_count, model_width)
    hidden_out = jnp.sum(weights_now[:, :, None] * back_rows, axis=1).astype(jnp.bfloat16)
    back_input = jnp.dot(
        picked, back_grad.reshape(experts * slots, model_width), preferred_element_type=jnp.float32
    )
    input_grad = jnp.sum(back_input.reshape(token_count, top_count, model_width), axis=1).astype(
        jnp.bfloat16
    )
    return (hidden_out, input_grad)


def local(hidden_in, cotangent, expert_ids, route_prob, swap_flags, gate_up, down_t):
    experts = lax.axis_size("expert")
    swap_bit = experts.bit_length() - 2
    half_axis = experts // 2
    my_index = lax.axis_index("expert")
    flag_mine = jnp.sum(
        jnp.where(jnp.arange(half_axis, dtype=jnp.int32) == my_index % half_axis, swap_flags, 0)
    )
    gate_full, down_full = (
        lax.all_gather(gate_up, "dp", axis=1, tiled=True),
        lax.all_gather(down_t, "dp", axis=1, tiled=True),
    )
    out_first, grad_first = run_micro(
        hidden_in[0],
        cotangent[0],
        expert_ids[0],
        route_prob[0],
        swap_flags,
        gate_full,
        down_full,
        False,
    )
    other_gate, other_down = from_partner((gate_up, down_t), "expert", swap_bit)
    resident_gate_up = jnp.where(flag_mine == 1, other_gate, gate_up)
    resident_down = jnp.where(flag_mine == 1, other_down, down_t)
    gate_full, down_full = (
        lax.all_gather(resident_gate_up, "dp", axis=1, tiled=True),
        lax.all_gather(resident_down, "dp", axis=1, tiled=True),
    )
    out_second, grad_second = run_micro(
        hidden_in[1],
        cotangent[1],
        expert_ids[1],
        route_prob[1],
        swap_flags,
        gate_full,
        down_full,
        True,
    )
    return (
        jnp.stack([out_first, out_second]),
        jnp.stack([grad_first, grad_second]),
        resident_gate_up,
        resident_down,
    )


def solution(mesh):
    placed = (
        P(None, ("dp", "expert"), None),
        P(None, ("dp", "expert"), None),
        P(None, ("dp", "expert"), None),
        P(None, ("dp", "expert"), None),
        P(),
        P("expert", "dp", None, None),
        P("expert", "dp", None),
    )
    return jax.shard_map(
        local,
        mesh=mesh,
        in_specs=placed,
        out_specs=(
            P(None, ("dp", "expert"), None),
            P(None, ("dp", "expert"), None),
            P("expert", "dp", None, None),
            P("expert", "dp", None),
        ),
        check_vma=False,
    )
```

profile of v0, /device:TPU:1, one launch (start us, length us, event | category | flops | bytes accessed | tf_op | source)
XLA Modules:
  0.0 722.0 jit_solution(1986401625468098576)
XLA Ops:
  12.8 23.0 %all-to-all-start.2 = ((bf16[128,2,2048]{2,1,0:T(2,128)(2,1)}), bf16[128,2,2048]{2,1,0:T(2,128)(2,1)S(1)}, u32[]{:S(2)}, u32[]{:S(2)}) async-start(bf16[128,2,2048]{2,1,0:T(2,128)(2,1)} %reshape.299), calls=%async_computation.2 | async-start | bytes 2097152 | tf_op jit(solution)/shard_map/all_to_all | solution.py:81
  39.4 50.2 %all-to-all-done.2 = bf16[128,2,2048]{2,1,0:T(2,128)(2,1)S(1)} async-done(((bf16[128,2,2048]{2,1,0:T(2,128)(2,1)}), bf16[128,2,2048]{2,1,0:T(2,128)(2,1)S(1)}, u32[]{:S(2)}, u32[]{:S(2)}) %all-to-all-start.2) | async-done | bytes 1048608 | tf_op jit(solution)/shard_map/all_to_all | solution.py:81
  89.5 10.7 %all-to-all-start.4 = ((bf16[128,2,2048]{2,1,0:T(2,128)(2,1)}), bf16[128,2,2048]{2,1,0:T(2,128)(2,1)S(1)}, u32[]{:S(2)}, u32[]{:S(2)}) async-start(bf16[128,2,2048]{2,1,0:T(2,128)(2,1)} %reshape.305), calls=%async_computation.4 | async-start | bytes 2097152 | tf_op jit(solution)/shard_map/all_to_all | solution.py:94
  102.6 34.1 %all-to-all-done.4 = bf16[128,2,2048]{2,1,0:T(2,128)(2,1)S(1)} async-done(((bf16[128,2,2048]{2,1,0:T(2,128)(2,1)}), bf16[128,2,2048]{2,1,0:T(2,128)(2,1)S(1)}, u32[]{:S(2)}, u32[]{:S(2)}) %all-to-all-start.4) | async-done | bytes 1048608 | tf_op jit(solution)/shard_map/all_to_all | solution.py:94
  136.8 28.5 %all-to-all-start = ((bf16[128,2,2048]{2,1,0:T(2,128)(2,1)}), bf16[128,2,2048]{2,1,0:T(2,128)(2,1)S(1)}, u32[]{:S(2)}, u32[]{:S(2)}) async-start(bf16[128,2,2048]{2,1,0:T(2,128)(2,1)} %reshape.293), calls=%async_computation | async-start | bytes 2097152 | tf_op jit(solution)/shard_map/all_to_all | solution.py:81
  170.3 31.9 %all-to-all-done = bf16[128,2,2048]{2,1,0:T(2,128)(2,1)S(1)} async-done(((bf16[128,2,2048]{2,1,0:T(2,128)(2,1)}), bf16[128,2,2048]{2,1,0:T(2,128)(2,1)S(1)}, u32[]{:S(2)}, u32[]{:S(2)}) %all-to-all-start) | async-done | bytes 1048608 | tf_op jit(solution)/shard_map/all_to_all | solution.py:81
  203.2 6.4 all-to-all-start.6
  210.4 5.4 collective-permute-start
  219.3 75.4 %all-gather.5.cloned.1.call-done = bf16[1,2048,2,384]{3,2,0,1:T(2,128)(2,1)} async-done(((bf16[1,512,2,384]{3,2,0,1:T(2,128)(2,1)}), bf16[1,2048,2,384]{3,2,0,1:T(2,128)(2,1)}) %all-gather.5.cloned.1.call-update) | async-done | bytes 3145744 | tf_op jit(solution)/shard_map/all_gather | solution.py:131
  294.6 2.6 copy.75
  300.9 54.5 %all-gather.7.cloned.1.call-done = bf16[1,2048,384]{2,1,0:T(8,128)(2,1)} async-done(((bf16[1,512,384]{2,1,0:T(8,128)(2,1)}), bf16[1,2048,384]{2,1,0:T(8,128)(2,1)}) %all-gather.7.cloned.1.call-update) | async-done | bytes 1572880 | tf_op jit(solution)/shard_map/all_gather | solution.py:132
  360.5 17.4 %all-to-all-start.5 = ((bf16[128,2,2048]{2,1,0:T(2,128)(2,1)}), bf16[128,2,2048]{2,1,0:T(2,128)(2,1)S(1)}, u32[]{:S(2)}, u32[]{:S(2)}) async-start(bf16[128,2,2048]{2,1,0:T(2,128)(2,1)} %reshape.307), calls=%async_computation.5 | async-start | bytes 2097152 | tf_op jit(solution)/shard_map/all_to_all | solution.py:101
  379.3 2.8 broadcast_select_fusion
  382.2 3.4 convolution_convert_fusion.3
  388.2 40.3 %all-to-all-done.5 = bf16[128,2,2048]{2,1,0:T(2,128)(2,1)S(1)} async-done(((bf16[128,2,2048]{2,1,0:T(2,128)(2,1)}), bf16[128,2,2048]{2,1,0:T(2,128)(2,1)S(1)}, u32[]{:S(2)}, u32[]{:S(2)}) %all-to-all-start.5) | async-done | bytes 1048608 | tf_op jit(solution)/shard_map/all_to_all | solution.py:101
  428.4 8.2 %all-to-all-start.1 = ((bf16[128,2,2048]{2,1,0:T(2,128)(2,1)}), bf16[128,2,2048]{2,1,0:T(2,128)(2,1)}, u32[]{:S(2)}, u32[]{:S(2)}) async-start(bf16[128,2,2048]{2,1,0:T(2,128)(2,1)} %reshape.297), calls=%async_computation.1 | async-start | bytes 2097152 | tf_op jit(solution)/shard_map/all_to_all | solution.py:86
  436.8 5.4 collective-permute-start.1
  442.2 14.4 %collective-permute-done.1 = bf16[1,512,384]{2,1,0:T(8,128)(2,1)S(1)} collective-permute-done((bf16[1,512,384]{2,1,0:T(8,128)(2,1)S(1)}, bf16[1,512,384]{2,1,0:T(8,128)(2,1)S(1)}, u32[]{:S(2)}, u32[]{:S(2)}) %collective-permute-start.1) | collective-permute-done | bytes 393248 | tf_op jit(solution)/shard_map/ppermute | solution.py:10
  459.1 60.1 %all-gather.9.cloned.1.call-done = bf16[1,2048,2,384]{3,2,0,1:T(2,128)(2,1)} async-done(((bf16[1,512,2,384]{3,2,0,1:T(2,128)(2,1)}), bf16[1,2048,2,384]{3,2,0,1:T(2,128)(2,1)}) %all-gather.9.cloned.1.call-update) | async-done | bytes 3145744 | tf_op jit(solution)/shard_map/all_gather | solution.py:148
  524.4 45.2 %all-gather.11.cloned.1.call-done = bf16[1,2048,384]{2,1,0:T(8,128)(2,1)} async-done(((bf16[1,512,384]{2,1,0:T(8,128)(2,1)}), bf16[1,2048,384]{2,1,0:T(8,128)(2,1)}) %all-gather.11.cloned.1.call-update) | async-done | bytes 1572880 | tf_op jit(solution)/shard_map/all_gather | solution.py:149
  574.6 17.4 %all-to-all-start.7 = ((bf16[128,2,2048]{2,1,0:T(2,128)(2,1)}), bf16[128,2,2048]{2,1,0:T(2,128)(2,1)S(1)}, u32[]{:S(2)}, u32[]{:S(2)}) async-start(bf16[128,2,2048]{2,1,0:T(2,128)(2,1)} %reshape.311), calls=%async_computation.7 | async-start | bytes 2097152 | tf_op jit(solution)/shard_map/all_to_all | solution.py:101
  596.0 51.1 %all-to-all-done.7 = bf16[128,2,2048]{2,1,0:T(2,128)(2,1)S(1)} async-done(((bf16[128,2,2048]{2,1,0:T(2,128)(2,1)}), bf16[128,2,2048]{2,1,0:T(2,128)(2,1)S(1)}, u32[]{:S(2)}, u32[]{:S(2)}) %all-to-all-start.7) | async-done | bytes 1048608 | tf_op jit(solution)/shard_map/all_to_all | solution.py:101
  647.0 10.4 %all-to-all-start.3 = ((bf16[128,2,2048]{2,1,0:T(2,128)(2,1)}), bf16[128,2,2048]{2,1,0:T(2,128)(2,1)S(1)}, u32[]{:S(2)}, u32[]{:S(2)}) async-start(bf16[128,2,2048]{2,1,0:T(2,128)(2,1)} %reshape.303), calls=%async_computation.3 | async-start | bytes 2097152 | tf_op jit(solution)/shard_map/all_to_all | solution.py:86
  664.3 49.5 %all-to-all-done.3 = bf16[128,2,2048]{2,1,0:T(2,128)(2,1)S(1)} async-done(((bf16[128,2,2048]{2,1,0:T(2,128)(2,1)}), bf16[128,2,2048]{2,1,0:T(2,128)(2,1)S(1)}, u32[]{:S(2)}, u32[]{:S(2)}) %all-to-all-start.3) | async-done | bytes 1048608 | tf_op jit(solution)/shard_map/all_to_all | solution.py:86
  (117 shorter events, 58.6 us)
Async XLA Ops:
  11.3 25.0 %copy-start.15 = (f32[2,16,8]{1,2,0:T(8,128)S(1)}, f32[2,16,8]{1,2,0:T(8,128)}, u32[]{:S(2)}) copy-start(f32[2,16,8]{1,2,0:T(8,128)} %param.10) | copy-start | bytes 3076
  11.3 25.9 %copy-start.10 = (bf16[2,16,2048]{2,1,0:T(8,128)(2,1)S(1)}, bf16[2,16,2048]{2,1,0:T(8,128)(2,1)}, u32[]{:S(2)}) copy-start(bf16[2,16,2048]{2,1,0:T(8,128)(2,1)} %param.8) | copy-start | bytes 393220
  12.8 76.7 %all-to-all-start.2 = ((bf16[128,2,2048]{2,1,0:T(2,128)(2,1)}), bf16[128,2,2048]{2,1,0:T(2,128)(2,1)S(1)}, u32[]{:S(2)}, u32[]{:S(2)}) async-start(bf16[128,2,2048]{2,1,0:T(2,128)(2,1)} %reshape.299), calls=%async_computation.2 | async-start | bytes 2097152 | tf_op jit(solution)/shard_map/all_to_all | solution.py:81
  37.8 62.6 %copy-start.12 = (s32[2,16,8]{1,2,0:T(8,128)S(1)}, s32[2,16,8]{1,2,0:T(8,128)}, u32[]{:S(2)}) copy-start(s32[2,16,8]{1,2,0:T(8,128)} %param.9) | copy-start | bytes 3076
  37.9 62.8 %copy-start.11 = (bf16[2,16,2048]{2,1,0:T(8,128)(2,1)S(1)}, bf16[2,16,2048]{2,1,0:T(8,128)(2,1)}, u32[]{:S(2)}) copy-start(bf16[2,16,2048]{2,1,0:T(8,128)(2,1)} %param.7) | copy-start | bytes 393220
  89.5 47.2 %all-to-all-start.4 = ((bf16[128,2,2048]{2,1,0:T(2,128)(2,1)}), bf16[128,2,2048]{2,1,0:T(2,128)(2,1)S(1)}, u32[]{:S(2)}, u32[]{:S(2)}) async-start(bf16[128,2,2048]{2,1,0:T(2,128)(2,1)} %reshape.305), calls=%async_computation.4 | async-start | bytes 2097152 | tf_op jit(solution)/shard_map/all_to_all | solution.py:94
  136.8 65.5 %all-to-all-start = ((bf16[128,2,2048]{2,1,0:T(2,128)(2,1)}), bf16[128,2,2048]{2,1,0:T(2,128)(2,1)S(1)}, u32[]{:S(2)}, u32[]{:S(2)}) async-start(bf16[128,2,2048]{2,1,0:T(2,128)(2,1)} %reshape.293), calls=%async_computation | async-start | bytes 2097152 | tf_op jit(solution)/shard_map/all_to_all | solution.py:81
  165.3 129.3 %all-gather.5.cloned.1.call-start = ((), (), s32[]{:S(2)}) async-start(), calls=%async_computation.8 | async-start | bytes 3932160 | tf_op jit(solution)/shard_map/all_gather | solution.py:131
  203.2 157.3 %all-to-all-start.6 = ((bf16[128,2,2048]{2,1,0:T(2,128)(2,1)}), bf16[128,2,2048]{2,1,0:T(2,128)(2,1)S(1)}, u32[]{:S(2)}, u32[]{:S(2)}) async-start(bf16[128,2,2048]{2,1,0:T(2,128)(2,1)} %reshape.309), calls=%async_computation.6 | async-start | bytes 2097152 | tf_op jit(solution)/shard_map/all_to_all | solution.py:94
  209.6 145.8 %all-gather.7.cloned.1.call-start = ((), (), s32[]{:S(2)}) async-start(), calls=%async_computation.9 | async-start | bytes 1966080 | tf_op jit(solution)/shard_map/all_gather | solution.py:132
  210.4 168.9 %collective-permute-start = (bf16[1,512,2,384]{3,2,0,1:T(2,128)(2,1)}, bf16[1,512,2,384]{3,2,0,1:T(2,128)(2,1)}, u32[]{:S(2)}, u32[]{:S(2)}) collective-permute-start(bf16[1,512,2,384]{3,2,0,1:T(2,128)(2,1)} %bitcast.92), channel_id=1, source_target_pairs={{0,64},{1,65},{2,66},{3,67},{4,68},{5,69},{6,70},{7,71},{8,72},{9,... | collective-permute-start | bytes 2359304 | tf_op jit(solution)/shard_map/ppermute | solution.py:10
  298.9 56.5 %copy-start.7 = (bf16[256,2048]{1,0:T(8,128)(2,1)S(1)}, bf16[256,2048]{1,0:T(8,128)(2,1)}, u32[]{:S(2)}) copy-start(bf16[256,2048]{1,0:T(8,128)(2,1)} %reshape.306) | copy-start | bytes 3145732
  359.0 19.0 %copy-start.16 = (s32[64]{0:T(128)S(1)}, s32[64]{0:T(128)}, u32[]{:S(2)}) copy-start(s32[64]{0:T(128)} %param.11) | copy-start | bytes 772
  360.5 67.9 %all-to-all-start.5 = ((bf16[128,2,2048]{2,1,0:T(2,128)(2,1)}), bf16[128,2,2048]{2,1,0:T(2,128)(2,1)S(1)}, u32[]{:S(2)}, u32[]{:S(2)}) async-start(bf16[128,2,2048]{2,1,0:T(2,128)(2,1)} %reshape.307), calls=%async_computation.5 | async-start | bytes 2097152 | tf_op jit(solution)/shard_map/all_to_all | solution.py:101
  377.9 141.2 %all-gather.9.cloned.1.call-start = ((), (), s32[]{:S(2)}) async-start(), calls=%async_computation.10 | async-start | bytes 3932160 | tf_op jit(solution)/shard_map/all_gather | solution.py:148
  385.6 51.2 %copy-start.6 = (bf16[1,512,384]{2,1,0:T(8,128)(2,1)S(1)}, bf16[1,512,384]{2,1,0:T(8,128)(2,1)}, u32[]{:S(2)}) copy-start(bf16[1,512,384]{2,1,0:T(8,128)(2,1)} %param.13) | copy-start | bytes 1179652
  428.4 146.1 %all-to-all-start.1 = ((bf16[128,2,2048]{2,1,0:T(2,128)(2,1)}), bf16[128,2,2048]{2,1,0:T(2,128)(2,1)}, u32[]{:S(2)}, u32[]{:S(2)}) async-start(bf16[128,2,2048]{2,1,0:T(2,128)(2,1)} %reshape.297), calls=%async_computation.1 | async-start | bytes 2097152 | tf_op jit(solution)/shard_map/all_to_all | solution.py:86
  436.7 133.0 %all-gather.11.cloned.1.call-start = ((), (), s32[]{:S(2)}) async-start(), calls=%async_computation.11 | async-start | bytes 1966080 | tf_op jit(solution)/shard_map/all_gather | solution.py:149
  436.8 19.9 %collective-permute-start.1 = (bf16[1,512,384]{2,1,0:T(8,128)(2,1)S(1)}, bf16[1,512,384]{2,1,0:T(8,128)(2,1)S(1)}, u32[]{:S(2)}, u32[]{:S(2)}) collective-permute-start(bf16[1,512,384]{2,1,0:T(8,128)(2,1)S(1)} %copy-done.6), channel_id=1, source_target_pairs={{0,64},{1,65},{2,66},{3,67},{4,68},{5,69},{6,70},{7,71},{8,72},{9,... | collective-permute-start | bytes 1179656 | tf_op jit(solution)/shard_map/ppermute | solution.py:10
  524.4 47.6 %copy-start.17 = (f32[256,768]{1,0:T(8,128)}, f32[256,768]{1,0:T(8,128)S(1)}, u32[]{:S(2)}) copy-start(f32[256,768]{1,0:T(8,128)S(1)} %fusion.57) | copy-start | bytes 2359300
  574.6 72.4 %all-to-all-start.7 = ((bf16[128,2,2048]{2,1,0:T(2,128)(2,1)}), bf16[128,2,2048]{2,1,0:T(2,128)(2,1)S(1)}, u32[]{:S(2)}, u32[]{:S(2)}) async-start(bf16[128,2,2048]{2,1,0:T(2,128)(2,1)} %reshape.311), calls=%async_computation.7 | async-start | bytes 2097152 | tf_op jit(solution)/shard_map/all_to_all | solution.py:101
  594.4 63.0 %copy-start.14 = (f32[16,8]{0,1:T(8,128)S(1)}, f32[16,8]{0,1:T(8,128)}, u32[]{:S(2)}) copy-start(f32[16,8]{0,1:T(8,128)} %get-tuple-element.20) | copy-start | bytes 1540
  594.4 63.1 %copy-start.13 = (f32[16,8]{0,1:T(8,128)S(1)}, f32[16,8]{0,1:T(8,128)}, u32[]{:S(2)}) copy-start(f32[16,8]{0,1:T(8,128)} %get-tuple-element.19) | copy-start | bytes 1540
  647.0 66.8 %all-to-all-start.3 = ((bf16[128,2,2048]{2,1,0:T(2,128)(2,1)}), bf16[128,2,2048]{2,1,0:T(2,128)(2,1)S(1)}, u32[]{:S(2)}, u32[]{:S(2)}) async-start(bf16[128,2,2048]{2,1,0:T(2,128)(2,1)} %reshape.303), calls=%async_computation.3 | async-start | bytes 2097152 | tf_op jit(solution)/shard_map/all_to_all | solution.py:86
  (8 other events, 20.1 us)
Sparse Core Ops, SparseCore 0:
  168.2 126.3 all-gather.4
  296.7 58.5 all-gather.6
  382.3 136.8 all-gather.8
  521.7 47.9 all-gather.10
where the time goes:
time: 723 us; the launch traced here: 722 us
  waiting for transfers between devices  508 us (70%)
  starting transfers between devices  133 us (18%)
  local copies, waits for them, and re-layouts  36 us (5%)
  matrix products  22.6 us (3%)
  between operations  14.9 us (2%)
  other arithmetic  7.25 us (1%)
    all_to_all x2, waiting for transfers between devices, run_micro(): lax.all_to_all(row_input.reshape(experts, slots, model_width), 'expert',...  91.3 us
    all_to_all x2, waiting for transfers between devices, run_micro(): lax.all_to_all(send_tokens, 'expert', split_axis=0, concat_axis=0, tiled=...  82.1 us
    all_gather x1, waiting for transfers between devices, local(): lax.all_gather(gate_up, 'dp', axis=1, tiled=True)  75.4 us
    all_gather x1, waiting for transfers between devices, local(): lax.all_gather(resident_gate_up, 'dp', axis=1, tiled=True)  60.1 us
    all_gather x1, waiting for transfers between devices, local(): lax.all_gather(down_t, 'dp', axis=1, tiled=True)  54.5 us
    all_to_all x2, starting transfers between devices, run_micro(): lax.all_to_all(send_tokens, 'expert', split_axis=0, concat_axis=0, tiled=...  51.5 us
    all_to_all x2, waiting for transfers between devices, run_micro(): lax.all_to_all(expert_out.reshape(experts, item_count, model_width), 'exp...  49.5 us
    all_gather x1, waiting for transfers between devices, local(): lax.all_gather(resident_down, 'dp', axis=1, tiled=True)  45.2 us
  transfers between devices with their start and end apart: 14, of which 11 were waited for; matrix products, arithmetic and copies ran while one was open for 8% of the time, Pallas kernels for 0%

commit v1 on v0

v1 whole, which is shorter than its diff:
```python
import jax
import jax.numpy as jnp
from jax import lax
from jax.sharding import Mesh, PartitionSpec as P

EXPERT = ("y", "x", "z", "c")
PLANE = ("y", "x", "c")
BF = jnp.bfloat16
F32 = jnp.float32


def along_z(value, shift):
    count = lax.axis_size("z")
    return lax.ppermute(value, "z", [(i, (i + shift) % count) for i in range(count)])


def local(hidden_in, cotangent, expert_ids, route_prob, swap_flags, gate_up, down_t):
    micro, tok, width = hidden_in.shape
    top = expert_ids.shape[2]
    hid = down_t.shape[2]
    nz = lax.axis_size("z")
    ny = lax.axis_size("y")
    plane = ny * lax.axis_size("x") * 2
    my_z = lax.axis_index("z")
    my_y = lax.axis_index("y")
    half = ny * lax.axis_size("x") * nz
    my_index = lax.axis_index(EXPERT)

    flag = jnp.sum(jnp.where(jnp.arange(half, dtype=jnp.int32) == my_index % half, swap_flags, 0))
    pairs = [(i, i ^ (ny // 2)) for i in range(ny)]
    other_gate = lax.ppermute(gate_up, "y", pairs)
    other_down = lax.ppermute(down_t, "y", pairs)
    resident_gate = jnp.where(flag == 1, other_gate, gate_up)
    resident_down = jnp.where(flag == 1, other_down, down_t)

    mine = jnp.stack([hidden_in, cotangent])
    facts = jnp.concatenate([expert_ids.astype(F32), route_prob], axis=2)
    facts = jnp.stack([facts] + [along_z(facts, s) for s in range(1, nz)])
    column = jnp.stack([mine] + [along_z(mine, s) for s in range(1, nz)])

    weights = jnp.concatenate([gate_up.reshape(-1, 2 * hid), down_t.reshape(-1, hid)], axis=1)
    weights = lax.all_gather(weights, "dp", axis=0, tiled=True)
    gate_matrix = weights[:, : 2 * hid]
    down_matrix = weights[:, 2 * hid :]

    ids = facts[..., :top].astype(jnp.int32)
    prob = facts[..., top:]
    core = ids % 2
    place = (ids // (2 * nz)) * 2 + core
    place = jnp.where((ids // 2) % nz == my_z, place, -1)
    hit = place[..., None] == jnp.arange(plane, dtype=jnp.int32)
    member = jnp.any(hit, axis=3)
    weight = jnp.sum(jnp.where(hit, prob[..., None], 0.0), axis=3)
    below = jnp.tril(jnp.ones((tok, tok), F32), -1)
    earlier = jnp.einsum("ut,smtd->smud", below, member.astype(F32))
    rank = jnp.arange(2, dtype=jnp.int32).astype(F32)
    pick = member[..., None] & (earlier[..., None] == rank)
    pick = pick.astype(F32)
    slot_weight = jnp.einsum("smtdr,smtd->dmsr", pick, weight)

    pick_b = pick.astype(BF)
    rows_x = jnp.einsum("smtdr,smtw->dmsrw", pick_b, column[:, 0], preferred_element_type=F32).astype(BF)
    rows_g = jnp.einsum("smtdr,smtw->dmsrw", pick_b, column[:, 1], preferred_element_type=F32)
    rows_g = (rows_g * slot_weight[..., None]).astype(BF)
    count = micro * nz * 2
    rows = jnp.concatenate(
        [rows_x.reshape(plane, count, width), rows_g.reshape(plane, count, width)], axis=1
    )
    rows = lax.all_to_all(rows, PLANE, 0, 0, tiled=True)
    tokens_now = rows[:, :count].reshape(plane * count, width)
    grads_now = rows[:, count:].reshape(plane * count, width)

    projected = jnp.dot(tokens_now, gate_matrix, preferred_element_type=F32)
    gate_part = projected[:, :hid]
    upper_part = projected[:, hid:]
    sig = jax.nn.sigmoid(gate_part)
    hidden = (gate_part * sig * upper_part).astype(BF)
    last = (((1,), (1,)), ((), ()))
    expert_out = lax.dot_general(hidden, down_matrix, last, preferred_element_type=F32).astype(BF)
    d_hidden = jnp.dot(grads_now, down_matrix, preferred_element_type=F32)
    d_gate = (d_hidden * upper_part * sig * (1.0 + gate_part * (1.0 - sig))).astype(BF)
    d_upper = (d_hidden * gate_part * sig).astype(BF)
    d_joined = jnp.concatenate([d_gate, d_upper], axis=1)
    row_input = lax.dot_general(d_joined, gate_matrix, last, preferred_element_type=F32).astype(BF)

    back = jnp.concatenate(
        [expert_out.reshape(plane, count, width), row_input.reshape(plane, count, width)], axis=1
    )
    back = lax.all_to_all(back, PLANE, 0, 0, tiled=True)
    back_out = back[:, :count].reshape(plane, micro, nz, 2, width)
    back_grad = back[:, count:].reshape(plane, micro, nz, 2, width)

    scaled = pick * weight[..., None]
    scaled_high = scaled.astype(BF)
    scaled_low = (scaled - scaled_high.astype(F32)).astype(BF)
    form = "smtdr,dmsrw->smtw"
    part_out = jnp.einsum(form, scaled_high, back_out, preferred_element_type=F32) + jnp.einsum(
        form, scaled_low, back_out, preferred_element_type=F32
    )
    part_grad = jnp.einsum(form, pick_b, back_grad, preferred_element_type=F32)
    part = jnp.stack([part_out, part_grad], axis=1)
    total = part[0]
    for s in range(1, nz):
        total = total + along_z(part[s].astype(BF), -s).astype(F32)
    total = total.astype(BF)
    return (total[0], total[1], resident_gate, resident_down)


def solution(mesh):
    devices = mesh.devices.reshape(4, 4, 4, 4, 2)
    fine = Mesh(devices, ("dp", "y", "x", "z", "c"))
    tokens = P(None, ("dp",) + EXPERT, None)
    placed = (
        tokens,
        tokens,
        tokens,
        tokens,
        P(),
        P(EXPERT, "dp", None, None),
        P(EXPERT, "dp", None),
    )
    return jax.shard_map(
        local,
        mesh=fine,
        in_specs=placed,
        out_specs=(tokens, tokens, P(EXPERT, "dp", None, None), P(EXPERT, "dp", None)),
        check_vma=False,
    )
```

time: 723 us -> 334 us (0.46)
  the two profiles are of different devices: /device:TPU:1 before, /device:TPU:117 now
where the time goes in v1:
time: 334 us
  waiting for transfers between devices  160 us (48%)
  starting transfers between devices  65.4 us (20%)
  blocking collectives  59 us (18%)
  between operations  15.1 us (5%)
  matrix products  12.4 us (4%)
  local copies, waits for them, and re-layouts  11.4 us (3%)
  other arithmetic  10.4 us (3%)
    ppermute x9, waiting for transfers between devices, along_z(): lax.ppermute(value, 'z', [(i, (i + shift) % count) for i in range(count)])  87.1 us
    all_to_all x1, blocking collectives, local(): rows = lax.all_to_all(rows, PLANE, 0, 0, tiled=True)  59 us
    ppermute x9, starting transfers between devices, along_z(): lax.ppermute(value, 'z', [(i, (i + shift) % count) for i in range(count)])  50.8 us
    ppermute x1, waiting for transfers between devices, local(): other_down = lax.ppermute(down_t, 'y', pairs)  46.3 us
    all_to_all x1, waiting for transfers between devices, local(): back = lax.all_to_all(back, PLANE, 0, 0, tiled=True)  16.6 us
    all_gather x1, waiting for transfers between devices, local(): weights = lax.all_gather(weights, 'dp', axis=0, tiled=True)  10.1 us
    all_to_all x1, starting transfers between devices, local(): back = lax.all_to_all(back, PLANE, 0, 0, tiled=True)  7.81 us
  transfers between devices with their start and end apart: 13, of which 8 were waited for; matrix products, arithmetic and copies ran while one was open for 6% of the time, Pallas kernels for 0%

profile of v1, /device:TPU:117, one launch (start us, length us, event | category | flops | bytes accessed | tf_op | source)
XLA Modules:
  0.0 333.7 jit_solution(6145874898485073797)
XLA Ops:
  8.6 8.8 %collective-permute-start = (f32[2,16,16]{1,2,0:T(8,128)S(1)}, f32[2,16,16]{1,2,0:T(8,128)S(1)}, u32[]{:S(2)}, u32[]{:S(2)}) collective-permute-start(f32[2,16,16]{1,2,0:T(8,128)S(1)} %get-tuple-element.18), channel_id=1, source_target_pairs={{0,2},{2,4},{4,6},{6,0},{1,3},{3,5},{5,7},{7,1},{8,10},{10,12},{12... | collective-permute-start | bytes 6152 | tf_op jit(solution)/shard_map/ppermute | solution.py:14
  17.4 7.9 %collective-permute-start.1 = (f32[2,16,16]{1,2,0:T(8,128)S(1)}, f32[2,16,16]{1,2,0:T(8,128)S(1)}, u32[]{:S(2)}, u32[]{:S(2)}) collective-permute-start(f32[2,16,16]{1,2,0:T(8,128)S(1)} %get-tuple-element.18), channel_id=1, source_target_pairs={{0,4},{2,6},{4,0},{6,2},{1,5},{3,7},{5,1},{7,3},{8,12},{10,14},{12... | collective-permute-start | bytes 6152 | tf_op jit(solution)/shard_map/ppermute | solution.py:14
  25.4 5.2 %collective-permute-start.2 = (f32[2,16,16]{1,2,0:T(8,128)S(1)}, f32[2,16,16]{1,2,0:T(8,128)S(1)}, u32[]{:S(2)}, u32[]{:S(2)}) collective-permute-start(f32[2,16,16]{1,2,0:T(8,128)S(1)} %get-tuple-element.18), channel_id=1, source_target_pairs={{0,6},{2,0},{4,2},{6,4},{1,7},{3,1},{5,3},{7,5},{8,14},{10,8},{12,... | collective-permute-start | bytes 6152 | tf_op jit(solution)/shard_map/ppermute | solution.py:14
  34.1 4.0 %collective-permute-start.3 = (bf16[2,2,16,2048]{3,2,1,0:T(8,128)(2,1)S(1)}, bf16[2,2,16,2048]{3,2,1,0:T(8,128)(2,1)S(1)}, u32[]{:S(2)}, u32[]{:S(2)}) collective-permute-start(bf16[2,2,16,2048]{3,2,1,0:T(8,128)(2,1)S(1)} %get-tuple-element.16), channel_id=1, source_target_pairs={{0,2},{2,4},{4,6},{6,0},{1,3},{3,5},{5,7},{7,1},{8,10},{10,12},{12... | collective-permute-start | bytes 786440 | tf_op jit(solution)/shard_map/ppermute | solution.py:14
  38.1 6.1 %collective-permute-start.4 = (bf16[2,2,16,2048]{3,2,1,0:T(8,128)(2,1)S(1)}, bf16[2,2,16,2048]{3,2,1,0:T(8,128)(2,1)S(1)}, u32[]{:S(2)}, u32[]{:S(2)}) collective-permute-start(bf16[2,2,16,2048]{3,2,1,0:T(8,128)(2,1)S(1)} %get-tuple-element.16), channel_id=1, source_target_pairs={{0,4},{2,6},{4,0},{6,2},{1,5},{3,7},{5,1},{7,3},{8,12},{10,14},{12... | collective-permute-start | bytes 786440 | tf_op jit(solution)/shard_map/ppermute | solution.py:14
  44.2 2.9 collective-permute-start.5
  48.3 14.5 %collective-permute-done.3 = bf16[2,2,16,2048]{3,2,1,0:T(8,128)(2,1)S(1)} collective-permute-done((bf16[2,2,16,2048]{3,2,1,0:T(8,128)(2,1)S(1)}, bf16[2,2,16,2048]{3,2,1,0:T(8,128)(2,1)S(1)}, u32[]{:S(2)}, u32[]{:S(2)}) %collective-permute-start.3) | collective-permute-done | bytes 262176 | tf_op jit(solution)/shard_map/ppermute | solution.py:14
  62.8 11.7 %collective-permute-done.4 = bf16[2,2,16,2048]{3,2,1,0:T(8,128)(2,1)S(1)} collective-permute-done((bf16[2,2,16,2048]{3,2,1,0:T(8,128)(2,1)S(1)}, bf16[2,2,16,2048]{3,2,1,0:T(8,128)(2,1)S(1)}, u32[]{:S(2)}, u32[]{:S(2)}) %collective-permute-start.4) | collective-permute-done | bytes 262176 | tf_op jit(solution)/shard_map/ppermute | solution.py:14
  74.5 16.0 %collective-permute-done.5 = bf16[2,2,16,2048]{3,2,1,0:T(8,128)(2,1)S(1)} collective-permute-done((bf16[2,2,16,2048]{3,2,1,0:T(8,128)(2,1)S(1)}, bf16[2,2,16,2048]{3,2,1,0:T(8,128)(2,1)S(1)}, u32[]{:S(2)}, u32[]{:S(2)}) %collective-permute-start.5) | collective-permute-done | bytes 262176 | tf_op jit(solution)/shard_map/ppermute | solution.py:14
  95.2 59.0 %all_to_all.10 = bf16[32,32,2048]{2,1,0:T(8,128)(2,1)S(1)} all-to-all(bf16[32,32,2048]{2,1,0:T(8,128)(2,1)S(1)} %pad_maximum_fusion), channel_id=1, replica_groups=mesh['dp'=4,'y'=4,'x'=4,'z'=4,'c'=2] {'y','x','c'}, dimensions={0} | all-to-all | bytes 8388608 | tf_op jit(solution)/shard_map/all_to_all | solution.py:69
  155.9 10.1 %all-gather.2.cloned.1.call-done = bf16[2048,1152]{1,0:T(8,128)(2,1)} async-done(((bf16[512,1152]{1,0:T(8,128)(2,1)}), bf16[2048,1152]{1,0:T(8,128)(2,1)}) %all-gather.2.cloned.1.call-update) | async-done | bytes 4718608 | tf_op jit(solution)/shard_map/all_gather | solution.py:42
  166.0 4.5 %fusion.2 = f32[512,768]{1,0:T(8,128)S(1)} fusion(bf16[512,2048]{1,0:T(8,128)(2,1)} %bitcast.117, bf16[2048,1152]{1,0:T(8,128)(2,1)} %all-gather.2.cloned.1.call-done), kind=kOutput, calls=%fused_computation.8 | convolution fusion | flops 1610612736 | bytes 6815744 | tf_op jit(solution)/shard_map/dot_general | solution.py:73
  175.1 2.6 pad_maximum_fusion.1
  177.7 7.8 %all-to-all-start.1 = ((bf16[32,32,2048]{2,1,0:T(8,128)(2,1)}), bf16[32,32,2048]{2,1,0:T(8,128)(2,1)}, u32[]{:S(2)}, u32[]{:S(2)}) async-start(bf16[32,32,2048]{2,1,0:T(8,128)(2,1)} %pad_maximum_fusion.1), calls=%async_computation.1 | async-start | bytes 8388608 | tf_op jit(solution)/shard_map/all_to_all | solution.py:89
  185.5 2.2 collective-permute-start.10
  187.7 4.6 %collective-permute-start.9 = (bf16[1,512,2,384]{3,2,1,0:T(2,128)(2,1)S(1)}, bf16[1,512,2,384]{3,2,1,0:T(2,128)(2,1)S(1)}, u32[]{:S(2)}, u32[]{:S(2)}) collective-permute-start(bf16[1,512,2,384]{3,2,1,0:T(2,128)(2,1)S(1)} %copy-done), channel_id=1, source_target_pairs={{0,64},{32,96},{64,0},{96,32},{1,65},{33,97},{65,1},{97,33},{2,66}... | collective-permute-start | bytes 2359304 | tf_op jit(solution)/shard_map/ppermute | solution.py:31
  193.6 46.3 %collective-permute-done.10 = bf16[1,512,384]{2,1,0:T(8,128)(2,1)S(1)} collective-permute-done((bf16[1,512,384]{2,1,0:T(8,128)(2,1)S(1)}, bf16[1,512,384]{2,1,0:T(8,128)(2,1)S(1)}, u32[]{:S(2)}, u32[]{:S(2)}) %collective-permute-start.10) | collective-permute-done | bytes 393248 | tf_op jit(solution)/shard_map/ppermute | solution.py:32
  240.7 16.6 %all-to-all-done.1 = bf16[32,32,2048]{2,1,0:T(8,128)(2,1)} async-done(((bf16[32,32,2048]{2,1,0:T(8,128)(2,1)}), bf16[32,32,2048]{2,1,0:T(8,128)(2,1)}, u32[]{:S(2)}, u32[]{:S(2)}) %all-to-all-start.1) | async-done | bytes 4194336 | tf_op jit(solution)/shard_map/all_to_all | solution.py:89
  257.3 2.7 fusion.62
  264.2 2.7 collective-permute-start.6
  266.9 10.3 %collective-permute-start.7 = (bf16[2,2,16,2048]{3,2,1,0:T(8,128)(2,1)S(1)}, bf16[2,2,16,2048]{3,2,1,0:T(8,128)(2,1)S(1)}, u32[]{:S(2)}, u32[]{:S(2)}) collective-permute-start(bf16[2,2,16,2048]{3,2,1,0:T(8,128)(2,1)S(1)} %get-tuple-element.12), channel_id=1, source_target_pairs={{0,4},{2,6},{4,0},{6,2},{1,5},{3,7},{5,1},{7,3},{8,12},{10,14},{12... | collective-permute-start | bytes 786440 | tf_op jit(solution)/shard_map/ppermute | solution.py:14
  277.2 2.9 collective-permute-start.8
  281.1 39.5 %collective-permute-done.7 = bf16[2,2,16,2048]{3,2,1,0:T(8,128)(2,1)S(1)} collective-permute-done((bf16[2,2,16,2048]{3,2,1,0:T(8,128)(2,1)S(1)}, bf16[2,2,16,2048]{3,2,1,0:T(8,128)(2,1)S(1)}, u32[]{:S(2)}, u32[]{:S(2)}) %collective-permute-start.7) | collective-permute-done | bytes 262176 | tf_op jit(solution)/shard_map/ppermute | solution.py:14
  320.6 5.4 %collective-permute-done.8 = bf16[2,2,16,2048]{3,2,1,0:T(8,128)(2,1)S(1)} collective-permute-done((bf16[2,2,16,2048]{3,2,1,0:T(8,128)(2,1)S(1)}, bf16[2,2,16,2048]{3,2,1,0:T(8,128)(2,1)S(1)}, u32[]{:S(2)}, u32[]{:S(2)}) %collective-permute-start.8) | collective-permute-done | bytes 262176 | tf_op jit(solution)/shard_map/ppermute | solution.py:14
  (57 shorter events, 24.5 us)
Async XLA Ops:
  7.2 158.9 %all-gather.2.cloned.1.call-start = ((), (), s32[]{:S(2)}) async-start(), calls=%async_computation.2 | async-start | bytes 5898240 | tf_op jit(solution)/shard_map/all_gather | solution.py:42
  8.6 35.6 %collective-permute-start = (f32[2,16,16]{1,2,0:T(8,128)S(1)}, f32[2,16,16]{1,2,0:T(8,128)S(1)}, u32[]{:S(2)}, u32[]{:S(2)}) collective-permute-start(f32[2,16,16]{1,2,0:T(8,128)S(1)} %get-tuple-element.18), channel_id=1, source_target_pairs={{0,2},{2,4},{4,6},{6,0},{1,3},{3,5},{5,7},{7,1},{8,10},{10,12},{12... | collective-permute-start | bytes 6152 | tf_op jit(solution)/shard_map/ppermute | solution.py:14
  17.4 29.7 %collective-permute-start.1 = (f32[2,16,16]{1,2,0:T(8,128)S(1)}, f32[2,16,16]{1,2,0:T(8,128)S(1)}, u32[]{:S(2)}, u32[]{:S(2)}) collective-permute-start(f32[2,16,16]{1,2,0:T(8,128)S(1)} %get-tuple-element.18), channel_id=1, source_target_pairs={{0,4},{2,6},{4,0},{6,2},{1,5},{3,7},{5,1},{7,3},{8,12},{10,14},{12... | collective-permute-start | bytes 6152 | tf_op jit(solution)/shard_map/ppermute | solution.py:14
  25.4 21.7 %collective-permute-start.2 = (f32[2,16,16]{1,2,0:T(8,128)S(1)}, f32[2,16,16]{1,2,0:T(8,128)S(1)}, u32[]{:S(2)}, u32[]{:S(2)}) collective-permute-start(f32[2,16,16]{1,2,0:T(8,128)S(1)} %get-tuple-element.18), channel_id=1, source_target_pairs={{0,6},{2,0},{4,2},{6,4},{1,7},{3,1},{5,3},{7,5},{8,14},{10,8},{12,... | collective-permute-start | bytes 6152 | tf_op jit(solution)/shard_map/ppermute | solution.py:14
  31.8 2.2 copy-start.2
  31.8 2.2 copy-start.3
  34.1 28.8 %collective-permute-start.3 = (bf16[2,2,16,2048]{3,2,1,0:T(8,128)(2,1)S(1)}, bf16[2,2,16,2048]{3,2,1,0:T(8,128)(2,1)S(1)}, u32[]{:S(2)}, u32[]{:S(2)}) collective-permute-start(bf16[2,2,16,2048]{3,2,1,0:T(8,128)(2,1)S(1)} %get-tuple-element.16), channel_id=1, source_target_pairs={{0,2},{2,4},{4,6},{6,0},{1,3},{3,5},{5,7},{7,1},{8,10},{10,12},{12... | collective-permute-start | bytes 786440 | tf_op jit(solution)/shard_map/ppermute | solution.py:14
  38.1 36.4 %collective-permute-start.4 = (bf16[2,2,16,2048]{3,2,1,0:T(8,128)(2,1)S(1)}, bf16[2,2,16,2048]{3,2,1,0:T(8,128)(2,1)S(1)}, u32[]{:S(2)}, u32[]{:S(2)}) collective-permute-start(bf16[2,2,16,2048]{3,2,1,0:T(8,128)(2,1)S(1)} %get-tuple-element.16), channel_id=1, source_target_pairs={{0,4},{2,6},{4,0},{6,2},{1,5},{3,7},{5,1},{7,3},{8,12},{10,14},{12... | collective-permute-start | bytes 786440 | tf_op jit(solution)/shard_map/ppermute | solution.py:14
  44.2 46.3 %collective-permute-start.5 = (bf16[2,2,16,2048]{3,2,1,0:T(8,128)(2,1)S(1)}, bf16[2,2,16,2048]{3,2,1,0:T(8,128)(2,1)S(1)}, u32[]{:S(2)}, u32[]{:S(2)}) collective-permute-start(bf16[2,2,16,2048]{3,2,1,0:T(8,128)(2,1)S(1)} %get-tuple-element.16), channel_id=1, source_target_pairs={{0,6},{2,0},{4,2},{6,4},{1,7},{3,1},{5,3},{7,5},{8,14},{10,8},{12,... | collective-permute-start | bytes 786440 | tf_op jit(solution)/shard_map/ppermute | solution.py:14
  166.0 4.5 %copy-start.4 = (bf16[2048,1152]{1,0:T(8,128)(2,1)S(1)}, bf16[2048,1152]{1,0:T(8,128)(2,1)}, u32[]{:S(2)}) copy-start(bf16[2048,1152]{1,0:T(8,128)(2,1)} %all-gather.2.cloned.1.call-done) | copy-start | bytes 14155780
  177.7 7.8 %copy-start.1 = (bf16[1,512,384]{2,1,0:T(8,128)(2,1)S(1)}, bf16[1,512,384]{2,1,0:T(8,128)(2,1)}, u32[]{:S(2)}) copy-start(bf16[1,512,384]{2,1,0:T(8,128)(2,1)} %param.13) | copy-start | bytes 1179652
  177.7 10.0 %copy-start = (bf16[1,512,2,384]{3,2,1,0:T(2,128)(2,1)S(1)}, bf16[1,512,2,384]{3,2,1,0:T(2,128)(2,1)}, u32[]{:S(2)}) copy-start(bf16[1,512,2,384]{3,2,1,0:T(2,128)(2,1)} %param.12) | copy-start | bytes 2359300
  177.7 14.7 %copy-start.5 = (s32[64]{0:T(128)S(1)}, s32[64]{0:T(128)}, u32[]{:S(2)}) copy-start(s32[64]{0:T(128)} %param.11) | copy-start | bytes 772
  177.7 79.6 %all-to-all-start.1 = ((bf16[32,32,2048]{2,1,0:T(8,128)(2,1)}), bf16[32,32,2048]{2,1,0:T(8,128)(2,1)}, u32[]{:S(2)}, u32[]{:S(2)}) async-start(bf16[32,32,2048]{2,1,0:T(8,128)(2,1)} %pad_maximum_fusion.1), calls=%async_computation.1 | async-start | bytes 8388608 | tf_op jit(solution)/shard_map/all_to_all | solution.py:89
  185.5 54.4 %collective-permute-start.10 = (bf16[1,512,384]{2,1,0:T(8,128)(2,1)S(1)}, bf16[1,512,384]{2,1,0:T(8,128)(2,1)S(1)}, u32[]{:S(2)}, u32[]{:S(2)}) collective-permute-start(bf16[1,512,384]{2,1,0:T(8,128)(2,1)S(1)} %copy-done.1), channel_id=1, source_target_pairs={{0,64},{32,96},{64,0},{96,32},{1,65},{33,97},{65,1},{97,33},{2,66}... | collective-permute-start | bytes 1179656 | tf_op jit(solution)/shard_map/ppermute | solution.py:32
  187.7 92.5 %collective-permute-start.9 = (bf16[1,512,2,384]{3,2,1,0:T(2,128)(2,1)S(1)}, bf16[1,512,2,384]{3,2,1,0:T(2,128)(2,1)S(1)}, u32[]{:S(2)}, u32[]{:S(2)}) collective-permute-start(bf16[1,512,2,384]{3,2,1,0:T(2,128)(2,1)S(1)} %copy-done), channel_id=1, source_target_pairs={{0,64},{32,96},{64,0},{96,32},{1,65},{33,97},{65,1},{97,33},{2,66}... | collective-permute-start | bytes 2359304 | tf_op jit(solution)/shard_map/ppermute | solution.py:31
  264.2 16.9 %collective-permute-start.6 = (bf16[2,2,16,2048]{3,2,1,0:T(8,128)(2,1)S(1)}, bf16[2,2,16,2048]{3,2,1,0:T(8,128)(2,1)S(1)}, u32[]{:S(2)}, u32[]{:S(2)}) collective-permute-start(bf16[2,2,16,2048]{3,2,1,0:T(8,128)(2,1)S(1)} %get-tuple-element.10), channel_id=1, source_target_pairs={{0,6},{2,0},{4,2},{6,4},{1,7},{3,1},{5,3},{7,5},{8,14},{10,8},{12,... | collective-permute-start | bytes 786440 | tf_op jit(solution)/shard_map/ppermute | solution.py:14
  266.9 53.8 %collective-permute-start.7 = (bf16[2,2,16,2048]{3,2,1,0:T(8,128)(2,1)S(1)}, bf16[2,2,16,2048]{3,2,1,0:T(8,128)(2,1)S(1)}, u32[]{:S(2)}, u32[]{:S(2)}) collective-permute-start(bf16[2,2,16,2048]{3,2,1,0:T(8,128)(2,1)S(1)} %get-tuple-element.12), channel_id=1, source_target_pairs={{0,4},{2,6},{4,0},{6,2},{1,5},{3,7},{5,1},{7,3},{8,12},{10,14},{12... | collective-permute-start | bytes 786440 | tf_op jit(solution)/shard_map/ppermute | solution.py:14
  277.2 48.8 %collective-permute-start.8 = (bf16[2,2,16,2048]{3,2,1,0:T(8,128)(2,1)S(1)}, bf16[2,2,16,2048]{3,2,1,0:T(8,128)(2,1)S(1)}, u32[]{:S(2)}, u32[]{:S(2)}) collective-permute-start(bf16[2,2,16,2048]{3,2,1,0:T(8,128)(2,1)S(1)} %get-tuple-element.11), channel_id=1, source_target_pairs={{0,2},{2,4},{4,6},{6,0},{1,3},{3,5},{5,7},{7,1},{8,10},{10,12},{12... | collective-permute-start | bytes 786440 | tf_op jit(solution)/shard_map/ppermute | solution.py:14
Sparse Core Ops, SparseCore 0:
  34.1 131.8 all-gather.1

commit v2 on v1

v2 whole, which is shorter than its diff:
```python
import functools

import jax
import jax.numpy as jnp
from jax import lax
from jax.experimental import pallas as pl
from jax.experimental.pallas import tpu as pltpu
from jax.sharding import Mesh, PartitionSpec as P

EXPERT = ("y", "x", "z", "c")
PLANE = ("y", "x", "c")
BF = jnp.bfloat16
F32 = jnp.float32
STEP = 512
MORE = 128
ROWS = 256
GRANT = 60 << 20
LAST = (((1,), (1,)), ((), ()))


def along_z(value, shift):
    count = lax.axis_size("z")
    return lax.ppermute(value, "z", [(i, (i + shift) % count) for i in range(count)])


def cost(flops, size):
    return pl.CostEstimate(flops=flops, bytes_accessed=size, transcendentals=0)


def select_body(place_ref, f0, f1, f2, f3, a0, a1, x2, g2, a3, rows_ref, back_ref, high_ref, low_ref, pick_ref, scale_ref):
    n, slots = back_ref.shape
    half = n // 4

    @pl.when(pl.program_id(0) == 0)
    def _():
        facts = jnp.concatenate([f[...] for f in (f0, f1, f2, f3)], axis=0).astype(F32)
        ids = facts[:, 0:8].astype(jnp.int32)
        prob = facts[:, 8:16] + facts[:, 16:24] + facts[:, 24:32]
        place = jnp.where(((ids >> 1) & 3) == place_ref[0], ((ids >> 3) << 1) + (ids & 1), -1)
        col = lax.broadcasted_iota(jnp.int32, (n, slots), 1)
        row = lax.broadcasted_iota(jnp.int32, (n, slots), 0)
        dest = col >> 4
        hit = jnp.zeros((n, slots), jnp.bool_)
        weight = jnp.zeros((n, slots), F32)
        for k in range(8):
            same = place[:, k : k + 1] == dest
            hit = hit | same
            weight = jnp.where(same, prob[:, k : k + 1], weight)
        r2 = lax.broadcasted_iota(jnp.int32, (n, n), 0)
        c2 = lax.broadcasted_iota(jnp.int32, (n, n), 1)
        below = ((c2 < r2) & ((c2 >> 4) == (r2 >> 4))).astype(F32).astype(BF)
        earlier = jnp.dot(below, hit.astype(F32).astype(BF), preferred_element_type=F32)
        block = ((row >> 5) == ((col >> 1) & 3)) & (((row >> 4) & 1) == ((col >> 3) & 1))
        pick = hit & block & (earlier == (col & 1).astype(F32))
        pick_f = pick.astype(F32)
        scaled = jnp.where(pick, weight, 0.0)
        back_ref[...] = pick_f.astype(BF)
        high = scaled.astype(BF)
        high_ref[...] = high
        low_ref[...] = (scaled - high.astype(F32)).astype(BF)
        pick_ref[...] = jnp.transpose(pick_f).astype(BF)
        scale_ref[...] = jnp.sum(jnp.transpose(scaled), axis=1, keepdims=True)

    pick = pick_ref[...]
    shape = (rows_ref.shape[0], rows_ref.shape[2], rows_ref.shape[3])
    tokens = jnp.concatenate([a0[:half], a1[:half], x2[...], a3[:half]], axis=0)
    rows = jnp.dot(pick, tokens, preferred_element_type=F32)
    rows_ref[:, 0] = rows.astype(BF).reshape(shape)
    tokens = jnp.concatenate([a0[half:], a1[half:], g2[...], a3[half:]], axis=0)
    rows = jnp.dot(pick, tokens, preferred_element_type=F32)
    rows_ref[:, 1] = (rows * scale_ref[...]).astype(BF).reshape(shape)


def select(place, mine, up, far, down, plane, count):
    both = mine.shape[0]
    n = both * 2
    width = mine.shape[1] - MORE
    slots = plane * count
    facts = pl.BlockSpec((both // 2, MORE), lambda j: (0, width // MORE))
    part = pl.BlockSpec((both, STEP), lambda j: (0, j))
    one = pl.BlockSpec((both // 2, STEP), lambda j: (0, j))
    whole = pl.BlockSpec((n, slots), lambda j: (0, 0))
    return pl.pallas_call(
        select_body,
        grid=(width // STEP,),
        in_specs=[pl.BlockSpec(memory_space=pltpu.SMEM)] + [facts] * 4 + [part, part, one, one, part],
        out_specs=[pl.BlockSpec((plane, 2, count, STEP), lambda j: (0, 0, 0, j))] + [whole] * 3,
        out_shape=[jax.ShapeDtypeStruct((plane, 2, count, width), BF)]
        + [jax.ShapeDtypeStruct((n, slots), BF)] * 3,
        scratch_shapes=[pltpu.VMEM((slots, n), BF), pltpu.VMEM((slots, 1), F32)],
        compiler_params=pltpu.CompilerParams(vmem_limit_bytes=GRANT),
        cost_estimate=cost(1 << 30, 6 << 20),
    )(place, mine, up, far[0], down, mine, up, *far, down)


def forward_body(x_ref, w_ref, out_ref, projected_ref):
    hid = w_ref.shape[1] // 3
    x = x_ref[...].reshape(out_ref.shape)
    projected = jnp.dot(x, w_ref[:, : 2 * hid], preferred_element_type=F32)
    projected_ref[...] = projected
    gate_part = projected[:, :hid]
    hidden = (gate_part * jax.nn.sigmoid(gate_part) * projected[:, hid:]).astype(BF)
    for j in range(0, out_ref.shape[1], STEP):
        out = lax.dot_general(hidden, w_ref[j : j + STEP, 2 * hid :], LAST, preferred_element_type=F32)
        out_ref[:, j : j + STEP] = out.astype(BF)


def backward_body(g_ref, projected_ref, w_ref, out_ref):
    hid = w_ref.shape[1] // 3
    g = g_ref[...].reshape(out_ref.shape)
    d_hidden = jnp.dot(g, w_ref[:, 2 * hid :], preferred_element_type=F32)
    gate_part = projected_ref[:, :hid]
    sig = jax.nn.sigmoid(gate_part)
    d_gate = d_hidden * projected_ref[:, hid:] * sig * (1.0 + gate_part * (1.0 - sig))
    d_upper = d_hidden * gate_part * sig
    d_joined = jnp.concatenate([d_gate.astype(BF), d_upper.astype(BF)], axis=1)
    for j in range(0, out_ref.shape[1], STEP):
        out = lax.dot_general(d_joined, w_ref[j : j + STEP, : 2 * hid], LAST, preferred_element_type=F32)
        out_ref[:, j : j + STEP] = out.astype(BF)


def expert_specs(rows, weights, which):
    plane, _, count, width = rows.shape
    hid = weights.shape[1] // 3
    taken = pl.BlockSpec((ROWS // count, None, count, width), lambda i: (i, which, 0, 0))
    row = pl.BlockSpec((ROWS, width), lambda i: (i, 0))
    middle = pl.BlockSpec((ROWS, 2 * hid), lambda i: (i, 0))
    whole = pl.BlockSpec(weights.shape, lambda i: (0, 0), pipeline_mode=pl.Buffered(1))
    total = plane * count
    out = jax.ShapeDtypeStruct((total, width), BF)
    return (total // ROWS,), taken, row, middle, whole, out, jax.ShapeDtypeStruct((total, 2 * hid), F32)


def forward(rows, weights):
    grid, taken, row, middle, whole, out, projected = expert_specs(rows, weights, 0)
    return pl.pallas_call(
        forward_body,
        grid=grid,
        in_specs=[taken, whole],
        out_specs=[row, middle],
        out_shape=[out, projected],
        compiler_params=pltpu.CompilerParams(vmem_limit_bytes=GRANT),
        cost_estimate=cost(5 << 29, 10 << 20),
    )(rows, weights)


def backward(rows, projected, weights):
    grid, taken, row, middle, whole, out, _ = expert_specs(rows, weights, 1)
    return pl.pallas_call(
        backward_body,
        grid=grid,
        in_specs=[taken, middle, whole],
        out_specs=row,
        out_shape=out,
        compiler_params=pltpu.CompilerParams(vmem_limit_bytes=GRANT),
        cost_estimate=cost(5 << 29, 10 << 20),
    )(rows, projected, weights)


def combine_body(count, *refs):
    factors, rows, own_ref = refs[:count], refs[count][...], refs[count + 1]
    total = jnp.dot(factors[0][...], rows, preferred_element_type=F32)
    for f in factors[1:]:
        total = total + jnp.dot(f[...], rows, preferred_element_type=F32)
    m = own_ref.shape[0]
    own_ref[...] = total[:m]
    for s, ref in enumerate(refs[count + 2 :], 1):
        ref[...] = total[s * m : (s + 1) * m].astype(BF)


def combine(factors, rows):
    n, slots = factors[0].shape
    width = rows.shape[1]
    part = pl.BlockSpec((n // 4, STEP), lambda j: (0, j))
    return pl.pallas_call(
        functools.partial(combine_body, len(factors)),
        grid=(width // STEP,),
        in_specs=[pl.BlockSpec((n, slots), lambda j: (0, 0))] * len(factors)
        + [pl.BlockSpec((slots, STEP), lambda j: (0, j))],
        out_specs=[part] * 4,
        out_shape=[jax.ShapeDtypeStruct((n // 4, width), F32)]
        + [jax.ShapeDtypeStruct((n // 4, width), BF)] * 3,
        compiler_params=pltpu.CompilerParams(vmem_limit_bytes=16 << 20),
        cost_estimate=cost(1 << 28, 3 << 20),
    )(*factors, rows)


def in_plane(rows):
    return lax.all_to_all(rows, PLANE, 0, 0, tiled=True)


def local(hidden_in, cotangent, expert_ids, route_prob, swap_flags, gate_up, down_t):
    micro, tok, width = hidden_in.shape
    top = expert_ids.shape[2]
    hid = down_t.shape[2]
    nz = lax.axis_size("z")
    ny = lax.axis_size("y")
    plane = ny * lax.axis_size("x") * 2
    count = micro * nz * 2
    my_z = lax.axis_index("z")
    half = ny * lax.axis_size("x") * nz
    my_index = lax.axis_index(EXPERT)

    weights = jnp.concatenate([gate_up.reshape(-1, 2 * hid), down_t.reshape(-1, hid)], axis=1)
    weights = lax.all_gather(weights, "dp", axis=0, tiled=True)

    flag = jnp.sum(jnp.where(jnp.arange(half, dtype=jnp.int32) == my_index % half, swap_flags, 0))
    pairs = [(i, i ^ (ny // 2)) for i in range(ny)]

    high = lax.reduce_precision(route_prob, 8, 7)
    middle = lax.reduce_precision(route_prob - high, 8, 7)
    low = route_prob - high - middle
    facts = jnp.concatenate([expert_ids.astype(F32), high, middle, low], axis=2).astype(BF)
    facts = jnp.pad(facts.reshape(micro * tok, 4 * top), ((0, micro * tok), (0, MORE - 4 * top)))
    mine = jnp.concatenate([hidden_in, cotangent], axis=0).reshape(2 * micro * tok, width)
    mine = jnp.concatenate([mine, facts], axis=1)
    gate_own, down_own, mine = lax.optimization_barrier((gate_up, down_t, mine))
    other_gate = lax.ppermute(gate_own, "y", pairs)
    other_down = lax.ppermute(down_own, "y", pairs)
    up, down = along_z(mine, 1), along_z(mine, -1)
    split = micro * tok
    far = (along_z(up[:split], 1), along_z(down[split:], -1))

    rows, back, w_high, w_low = select(jnp.full((1,), my_z, jnp.int32), mine, up, far, down, plane, count)
    rows, other_gate, other_down = lax.optimization_barrier((rows, other_gate, other_down))
    rows = in_plane(rows)

    expert_out, projected = forward(rows, weights)
    back_out = in_plane(expert_out.reshape(plane, count, width)).reshape(plane * count, width)
    row_input = backward(rows, projected, weights)
    back_out, row_input = lax.optimization_barrier((back_out, row_input))
    back_grad = in_plane(row_input.reshape(plane, count, width)).reshape(plane * count, width)
    resident_gate = jnp.where(flag == 1, other_gate, gate_up)
    resident_down = jnp.where(flag == 1, other_down, down_t)

    results = []
    for factors, moved in (((w_high, w_low), back_out), ((back,), back_grad)):
        own, *others = combine(factors, moved)
        for s, part in enumerate(others, 1):
            own = own + along_z(part, -s).astype(F32)
        results.append(own.astype(BF).reshape(micro, tok, width))
    return (results[0], results[1], resident_gate, resident_down)


def solution(mesh):
    devices = mesh.devices.reshape(4, 4, 4, 4, 2)
    fine = Mesh(devices, ("dp", "y", "x", "z", "c"))
    tokens = P(None, ("dp",) + EXPERT, None)
    placed = (
        tokens,
        tokens,
        tokens,
        tokens,
        P(),
        P(EXPERT, "dp", None, None),
        P(EXPERT, "dp", None),
    )
    return jax.shard_map(
        local,
        mesh=fine,
        in_specs=placed,
        out_specs=(tokens, tokens, P(EXPERT, "dp", None, None), P(EXPERT, "dp", None)),
        check_vma=False,
    )
```

time: 334 us -> 274 us (0.82)
  the two profiles are of different devices: /device:TPU:117 before, /device:TPU:35 now
where the time goes in v2:
time: 274 us; the launch traced here: 273 us
  waiting for transfers between devices  96.6 us (35%)
  starting transfers between devices  65.9 us (24%)
  blocking collectives  60.6 us (22%)
  Pallas kernels  23.9 us (9%)
  between operations  15.2 us (6%)
  other arithmetic  7.25 us (3%)
  local copies, waits for them, and re-layouts  3.93 us (1%)
    ppermute x10, waiting for transfers between devices, along_z(): lax.ppermute(value, 'z', [(i, (i + shift) % count) for i in range(count)])  66.2 us
    all_to_all x1, blocking collectives, in_plane(): return lax.all_to_all(rows, PLANE, 0, 0, tiled=True)  60.6 us
    ppermute x10, starting transfers between devices, along_z(): lax.ppermute(value, 'z', [(i, (i + shift) % count) for i in range(count)])  47.2 us
    all_to_all x2, waiting for transfers between devices, in_plane(): return lax.all_to_all(rows, PLANE, 0, 0, tiled=True)  30.4 us
    all_to_all x2, starting transfers between devices, in_plane(): return lax.all_to_all(rows, PLANE, 0, 0, tiled=True)  11.9 us
    pallas_call x1, Pallas kernels, forward(): pl.pallas_call(forward_body, grid=grid, in_specs=[taken, whole], out_spec...  8.03 us
    pallas_call x1, Pallas kernels, backward(): pl.pallas_call(backward_body, grid=grid, in_specs=[taken, middle, whole],...  7.3 us
    pallas_call x1, Pallas kernels, select(): pl.pallas_call(select_body, grid=(width // STEP,), in_specs=[pl.BlockSpec...  5.87 us
  transfers between devices with their start and end apart: 15, of which 8 were waited for; matrix products, arithmetic and copies ran while one was open for 2% of the time, Pallas kernels for 6%

profile of v2, /device:TPU:35, one launch (start us, length us, event | category | flops | bytes accessed | tf_op | source)
XLA Modules:
  0.0 273.4 jit_solution(1319029939097416894)
XLA Ops:
  8.5 2.2 pad_maximum_fusion
  11.3 4.8 %collective-permute-start.4 = (bf16[1,512,2,384]{3,2,1,0:T(2,128)(2,1)S(1)}, bf16[1,512,2,384]{3,2,1,0:T(2,128)(2,1)S(1)}, u32[]{:S(2)}, u32[]{:S(2)}) collective-permute-start(bf16[1,512,2,384]{3,2,1,0:T(2,128)(2,1)S(1)} %copy-done.5), channel_id=1, source_target_pairs={{0,64},{32,96},{64,0},{96,32},{1,65},{33,97},{65,1},{97,33},{2,66}... | collective-permute-start | bytes 2359304 | tf_op jit(solution)/shard_map/ppermute | solution.py:218
  16.2 11.6 %collective-permute-start.2 = (bf16[64,2176]{1,0:T(8,128)(2,1)S(1)}, bf16[64,2176]{1,0:T(8,128)(2,1)S(1)}, u32[]{:S(2)}, u32[]{:S(2)}) collective-permute-start(bf16[64,2176]{1,0:T(8,128)(2,1)S(1)} %pad_maximum_fusion.1.f0.a0), channel_id=1, source_target_pairs={{0,6},{2,0},{4,2},{6,4},{1,7},{3,1},{5,3},{7,5},{8,14},{10,8},{12,... | collective-permute-start | bytes 835592 | tf_op jit(solution)/shard_map/ppermute | solution.py:23
  29.7 2.0 collective-permute-start.5
  31.6 33.1 %collective-permute-done.2.f3.a3 = bf16[64,2176]{1,0:T(8,128)(2,1)S(1)} collective-permute-done((bf16[64,2176]{1,0:T(8,128)(2,1)S(1)}, bf16[64,2176]{1,0:T(8,128)(2,1)S(1)}, u32[]{:S(2)}, u32[]{:S(2)}) %collective-permute-start.2) | collective-permute-done | bytes 278560 | tf_op jit(solution)/shard_map/ppermute | solution.py:23
  64.7 9.2 %collective-permute-start.3 = (bf16[32,2176]{1,0:T(8,128)(2,1)S(1)}, bf16[32,2176]{1,0:T(8,128)(2,1)}, u32[]{:S(2)}, u32[]{:S(2)}) collective-permute-start(bf16[32,2176]{1,0:T(8,128)(2,1)S(1)} %slice.9), channel_id=1, source_target_pairs={{0,6},{2,0},{4,2},{6,4},{1,7},{3,1},{5,3},{7,5},{8,14},{10,8},{12,... | collective-permute-start | bytes 417800 | tf_op jit(solution)/shard_map/ppermute | solution.py:23
  74.0 1.9 collective-permute-start.1
  75.9 8.2 %collective-permute-done.3.g2 = bf16[32,2176]{1,0:T(8,128)(2,1)} collective-permute-done((bf16[32,2176]{1,0:T(8,128)(2,1)S(1)}, bf16[32,2176]{1,0:T(8,128)(2,1)}, u32[]{:S(2)}, u32[]{:S(2)}) %collective-permute-start.3) | collective-permute-done | bytes 139296 | tf_op jit(solution)/shard_map/ppermute | solution.py:23
  84.2 9.0 %collective-permute-done.1.f2.x2 = bf16[32,2176]{1,0:T(8,128)(2,1)} collective-permute-done((bf16[32,2176]{1,0:T(8,128)(2,1)S(1)}, bf16[32,2176]{1,0:T(8,128)(2,1)}, u32[]{:S(2)}, u32[]{:S(2)}) %collective-permute-start.1) | collective-permute-done | bytes 139296 | tf_op jit(solution)/shard_map/ppermute | solution.py:23
  93.1 5.9 %shard_map.102 = (bf16[32,2,16,2048]{3,2,1,0:T(8,128)(2,1)}, bf16[128,512]{1,0:T(8,128)(2,1)}, bf16[128,512]{1,0:T(8,128)(2,1)}, bf16[128,512]{1,0:T(8,128)(2,1)}) custom-call(s32[1]{0:T(128)} %bitcast.place_ref, bf16[64,2176]{1,0:T(8,128)(2,1)} %copy-done.11, bf16[64,2176]{1,0:T(8,128)(2,1)} %copy-done.15, bf16[32,2176]{1,0:T(8,128)(2,1)} %collective-permute-done.1.f2.x2, ...), custom_call_target="tpu_custom_call" | custom-call | flops 1073741824 | bytes 6291456 | tf_op jit(solution)/shard_map/pallas_call | solution.py:83
  99.1 60.6 %all_to_all.15.x_ref.g_ref = bf16[32,2,16,2048]{3,2,1,0:T(8,128)(2,1)} all-to-all(bf16[32,2,16,2048]{3,2,1,0:T(8,128)(2,1)} %get-tuple-element.32), channel_id=1, replica_groups=mesh['dp'=4,'y'=4,'x'=4,'z'=4,'c'=2] {'y','x','c'}, dimensions={0} | all-to-all | bytes 8388608 | tf_op jit(solution)/shard_map/all_to_all | solution.py:189
  159.7 8.0 %shard_map.103 = (bf16[512,2048]{1,0:T(8,128)(2,1)}, f32[512,768]{1,0:T(8,128)}) custom-call(bf16[32,2,16,2048]{3,2,1,0:T(8,128)(2,1)} %all_to_all.15.x_ref.g_ref, bf16[2048,1152]{1,0:T(8,128)(2,1)} %all-gather.2.cloned.1.call-done.w_ref), custom_call_target="tpu_custom_call" | custom-call | flops 2684354560 | bytes 10485760 | tf_op jit(solution)/shard_map/pallas_call | solution.py:136
  167.7 5.1 %all-to-all-start.1 = ((bf16[32,16,2048]{2,1,0:T(8,128)(2,1)}), bf16[32,16,2048]{2,1,0:T(8,128)(2,1)S(1)}, u32[]{:S(2)}, u32[]{:S(2)}) async-start(bf16[32,16,2048]{2,1,0:T(8,128)(2,1)} %bitcast.25), calls=%async_computation.1 | async-start | bytes 4194304 | tf_op jit(solution)/shard_map/all_to_all | solution.py:189
  172.8 7.3 %shard_map.104 = bf16[512,2048]{1,0:T(8,128)(2,1)} custom-call(bf16[32,2,16,2048]{3,2,1,0:T(8,128)(2,1)} %all_to_all.15.x_ref.g_ref, f32[512,768]{1,0:T(8,128)} %get-tuple-element.34.projected_ref, bf16[2048,1152]{1,0:T(8,128)(2,1)} %all-gather.2.cloned.1.call-done.w_ref), custom_call_target="tpu_custom_call" | custom-call | flops 2684354560 | bytes 10485760 | tf_op jit(solution)/shard_map/pallas_call | solution.py:149
  180.1 20.0 %all-to-all-done.1 = bf16[32,16,2048]{2,1,0:T(8,128)(2,1)S(1)} async-done(((bf16[32,16,2048]{2,1,0:T(8,128)(2,1)}), bf16[32,16,2048]{2,1,0:T(8,128)(2,1)S(1)}, u32[]{:S(2)}, u32[]{:S(2)}) %all-to-all-start.1) | async-done | bytes 2097184 | tf_op jit(solution)/shard_map/all_to_all | solution.py:189
  201.4 6.8 %all-to-all-start.2 = ((bf16[32,16,2048]{2,1,0:T(8,128)(2,1)}), bf16[32,16,2048]{2,1,0:T(8,128)(2,1)S(1)}, u32[]{:S(2)}, u32[]{:S(2)}) async-start(bf16[32,16,2048]{2,1,0:T(8,128)(2,1)} %bitcast.21), calls=%async_computation.2 | async-start | bytes 4194304 | tf_op jit(solution)/shard_map/all_to_all | solution.py:189
  215.1 7.2 %collective-permute-start.7 = (bf16[32,2048]{1,0:T(8,128)(2,1)S(1)}, bf16[32,2048]{1,0:T(8,128)(2,1)}, u32[]{:S(2)}, u32[]{:S(2)}) collective-permute-start(bf16[32,2048]{1,0:T(8,128)(2,1)S(1)} %get-tuple-element.38), channel_id=1, source_target_pairs={{0,4},{2,6},{4,0},{6,2},{1,5},{3,7},{5,1},{7,3},{8,12},{10,14},{12... | collective-permute-start | bytes 393224 | tf_op jit(solution)/shard_map/ppermute | solution.py:23
  222.2 2.4 collective-permute-start.8
  225.5 10.4 %all-to-all-done.2 = bf16[32,16,2048]{2,1,0:T(8,128)(2,1)S(1)} async-done(((bf16[32,16,2048]{2,1,0:T(8,128)(2,1)}), bf16[32,16,2048]{2,1,0:T(8,128)(2,1)S(1)}, u32[]{:S(2)}, u32[]{:S(2)}) %all-to-all-start.2) | async-done | bytes 2097184 | tf_op jit(solution)/shard_map/all_to_all | solution.py:189
  239.0 6.7 %collective-permute-start.10 = (bf16[32,2048]{1,0:T(8,128)(2,1)S(1)}, bf16[32,2048]{1,0:T(8,128)(2,1)S(1)}, u32[]{:S(2)}, u32[]{:S(2)}) collective-permute-start(bf16[32,2048]{1,0:T(8,128)(2,1)S(1)} %get-tuple-element.44), channel_id=1, source_target_pairs={{0,4},{2,6},{4,0},{6,2},{1,5},{3,7},{5,1},{7,3},{8,12},{10,14},{12... | collective-permute-start | bytes 393224 | tf_op jit(solution)/shard_map/ppermute | solution.py:23
  245.7 2.5 collective-permute-start.11
  249.9 3.9 %collective-permute-done.9 = bf16[32,2048]{1,0:T(8,128)(2,1)S(1)} collective-permute-done((bf16[32,2048]{1,0:T(8,128)(2,1)S(1)}, bf16[32,2048]{1,0:T(8,128)(2,1)S(1)}, u32[]{:S(2)}, u32[]{:S(2)}) %collective-permute-start.9) | collective-permute-done | bytes 131104 | tf_op jit(solution)/shard_map/ppermute | solution.py:23
  253.8 7.7 %collective-permute-done.10 = bf16[32,2048]{1,0:T(8,128)(2,1)S(1)} collective-permute-done((bf16[32,2048]{1,0:T(8,128)(2,1)S(1)}, bf16[32,2048]{1,0:T(8,128)(2,1)S(1)}, u32[]{:S(2)}, u32[]{:S(2)}) %collective-permute-start.10) | collective-permute-done | bytes 131104 | tf_op jit(solution)/shard_map/ppermute | solution.py:23
  261.5 4.3 %collective-permute-done.11 = bf16[32,2048]{1,0:T(8,128)(2,1)S(1)} collective-permute-done((bf16[32,2048]{1,0:T(8,128)(2,1)S(1)}, bf16[32,2048]{1,0:T(8,128)(2,1)S(1)}, u32[]{:S(2)}, u32[]{:S(2)}) %collective-permute-start.11) | collective-permute-done | bytes 131104 | tf_op jit(solution)/shard_map/ppermute | solution.py:23
  (69 shorter events, 17.5 us)
Async XLA Ops:
  7.2 152.5 %all-gather.2.cloned.1.call-start = ((), (), s32[]{:S(2)}) async-start(), calls=%async_computation.3 | async-start | bytes 5898240 | tf_op jit(solution)/shard_map/all_gather | solution.py:205
  8.5 21.1 %copy-start.6 = (bf16[1,512,384]{2,1,0:T(8,128)(2,1)S(1)}, bf16[1,512,384]{2,1,0:T(8,128)(2,1)}, u32[]{:S(2)}) copy-start(bf16[1,512,384]{2,1,0:T(8,128)(2,1)} %param.13) | copy-start | bytes 1179652
  11.3 81.8 %copy-start.11 = (bf16[64,2176]{1,0:T(8,128)(2,1)}, bf16[64,2176]{1,0:T(8,128)(2,1)S(1)}, u32[]{:S(2)}) copy-start(bf16[64,2176]{1,0:T(8,128)(2,1)S(1)} %pad_maximum_fusion.1.f0.a0) | copy-start | bytes 835588
  11.3 87.7 %collective-permute-start.4 = (bf16[1,512,2,384]{3,2,1,0:T(2,128)(2,1)S(1)}, bf16[1,512,2,384]{3,2,1,0:T(2,128)(2,1)S(1)}, u32[]{:S(2)}, u32[]{:S(2)}) collective-permute-start(bf16[1,512,2,384]{3,2,1,0:T(2,128)(2,1)S(1)} %copy-done.5), channel_id=1, source_target_pairs={{0,64},{32,96},{64,0},{96,32},{1,65},{33,97},{65,1},{97,33},{2,66}... | collective-permute-start | bytes 2359304 | tf_op jit(solution)/shard_map/ppermute | solution.py:218
  16.2 48.5 %collective-permute-start.2 = (bf16[64,2176]{1,0:T(8,128)(2,1)S(1)}, bf16[64,2176]{1,0:T(8,128)(2,1)S(1)}, u32[]{:S(2)}, u32[]{:S(2)}) collective-permute-start(bf16[64,2176]{1,0:T(8,128)(2,1)S(1)} %pad_maximum_fusion.1.f0.a0), channel_id=1, source_target_pairs={{0,6},{2,0},{4,2},{6,4},{1,7},{3,1},{5,3},{7,5},{8,14},{10,8},{12,... | collective-permute-start | bytes 835592 | tf_op jit(solution)/shard_map/ppermute | solution.py:23
  27.7 46.2 %collective-permute-start = (bf16[64,2176]{1,0:T(8,128)(2,1)S(1)}, bf16[64,2176]{1,0:T(8,128)(2,1)S(1)}, u32[]{:S(2)}, u32[]{:S(2)}) collective-permute-start(bf16[64,2176]{1,0:T(8,128)(2,1)S(1)} %pad_maximum_fusion.1.f0.a0), channel_id=1, source_target_pairs={{0,2},{2,4},{4,6},{6,0},{1,3},{3,5},{5,7},{7,1},{8,10},{10,12},{12... | collective-permute-start | bytes 835592 | tf_op jit(solution)/shard_map/ppermute | solution.py:23
  29.7 69.3 %collective-permute-start.5 = (bf16[1,512,384]{2,1,0:T(8,128)(2,1)S(1)}, bf16[1,512,384]{2,1,0:T(8,128)(2,1)S(1)}, u32[]{:S(2)}, u32[]{:S(2)}) collective-permute-start(bf16[1,512,384]{2,1,0:T(8,128)(2,1)S(1)} %copy-done.6), channel_id=1, source_target_pairs={{0,64},{32,96},{64,0},{96,32},{1,65},{33,97},{65,1},{97,33},{2,66}... | collective-permute-start | bytes 1179656 | tf_op jit(solution)/shard_map/ppermute | solution.py:219
  64.7 28.4 %copy-start.14 = (bf16[64,2176]{1,0:T(8,128)(2,1)}, bf16[64,2176]{1,0:T(8,128)(2,1)S(1)}, u32[]{:S(2)}) copy-start(bf16[64,2176]{1,0:T(8,128)(2,1)S(1)} %collective-permute-done.2.f3.a3) | copy-start | bytes 835588
  64.7 19.4 %collective-permute-start.3 = (bf16[32,2176]{1,0:T(8,128)(2,1)S(1)}, bf16[32,2176]{1,0:T(8,128)(2,1)}, u32[]{:S(2)}, u32[]{:S(2)}) collective-permute-start(bf16[32,2176]{1,0:T(8,128)(2,1)S(1)} %slice.9), channel_id=1, source_target_pairs={{0,6},{2,0},{4,2},{6,4},{1,7},{3,1},{5,3},{7,5},{8,14},{10,8},{12,... | collective-permute-start | bytes 417800 | tf_op jit(solution)/shard_map/ppermute | solution.py:23
  73.9 19.2 %copy-start.15 = (bf16[64,2176]{1,0:T(8,128)(2,1)}, bf16[64,2176]{1,0:T(8,128)(2,1)S(1)}, u32[]{:S(2)}) copy-start(bf16[64,2176]{1,0:T(8,128)(2,1)S(1)} %collective-permute-done.f1.a1) | copy-start | bytes 835588
  74.0 19.2 %collective-permute-start.1 = (bf16[32,2176]{1,0:T(8,128)(2,1)S(1)}, bf16[32,2176]{1,0:T(8,128)(2,1)}, u32[]{:S(2)}, u32[]{:S(2)}) collective-permute-start(bf16[32,2176]{1,0:T(8,128)(2,1)S(1)} %slice.8), channel_id=1, source_target_pairs={{0,2},{2,4},{4,6},{6,0},{1,3},{3,5},{5,7},{7,1},{8,10},{10,12},{12... | collective-permute-start | bytes 417800 | tf_op jit(solution)/shard_map/ppermute | solution.py:23
  99.0 60.6 %copy-start.9 = (bf16[1,512,384]{2,1,0:T(8,128)(2,1)}, bf16[1,512,384]{2,1,0:T(8,128)(2,1)S(1)}, u32[]{:S(2)}) copy-start(bf16[1,512,384]{2,1,0:T(8,128)(2,1)S(1)} %collective-permute-done.5) | copy-start | bytes 1179652
  99.0 60.6 %copy-start.8 = (bf16[1,512,2,384]{3,2,1,0:T(2,128)(2,1)}, bf16[1,512,2,384]{3,2,1,0:T(2,128)(2,1)S(1)}, u32[]{:S(2)}) copy-start(bf16[1,512,2,384]{3,2,1,0:T(2,128)(2,1)S(1)} %collective-permute-done.4) | copy-start | bytes 2359300
  167.7 32.4 %all-to-all-start.1 = ((bf16[32,16,2048]{2,1,0:T(8,128)(2,1)}), bf16[32,16,2048]{2,1,0:T(8,128)(2,1)S(1)}, u32[]{:S(2)}, u32[]{:S(2)}) async-start(bf16[32,16,2048]{2,1,0:T(8,128)(2,1)} %bitcast.25), calls=%async_computation.1 | async-start | bytes 4194304 | tf_op jit(solution)/shard_map/all_to_all | solution.py:189
  201.4 34.4 %all-to-all-start.2 = ((bf16[32,16,2048]{2,1,0:T(8,128)(2,1)}), bf16[32,16,2048]{2,1,0:T(8,128)(2,1)S(1)}, u32[]{:S(2)}, u32[]{:S(2)}) async-start(bf16[32,16,2048]{2,1,0:T(8,128)(2,1)} %bitcast.21), calls=%async_computation.2 | async-start | bytes 4194304 | tf_op jit(solution)/shard_map/all_to_all | solution.py:189
  209.8 14.9 %copy-start.7 = (bf16[1,512,384]{2,1,0:T(8,128)(2,1)S(1)}, bf16[1,512,384]{2,1,0:T(8,128)(2,1)}, u32[]{:S(2)}) copy-start(bf16[1,512,384]{2,1,0:T(8,128)(2,1)} %param.13) | copy-start | bytes 1179652
  209.8 14.9 %copy-start.10 = (bf16[1,512,384]{2,1,0:T(8,128)(2,1)S(1)}, bf16[1,512,384]{2,1,0:T(8,128)(2,1)}, u32[]{:S(2)}) copy-start(bf16[1,512,384]{2,1,0:T(8,128)(2,1)} %copy-done.9) | copy-start | bytes 1179652
  210.8 25.1 %copy-start.2 = (bf16[128,512]{1,0:T(8,128)(2,1)S(1)}, bf16[128,512]{1,0:T(8,128)(2,1)}, u32[]{:S(2)}) copy-start(bf16[128,512]{1,0:T(8,128)(2,1)} %get-tuple-element.40.refs_0_) | copy-start | bytes 393220
  213.1 32.6 %collective-permute-start.6 = (bf16[32,2048]{1,0:T(8,128)(2,1)S(1)}, bf16[32,2048]{1,0:T(8,128)(2,1)S(1)}, u32[]{:S(2)}, u32[]{:S(2)}) collective-permute-start(bf16[32,2048]{1,0:T(8,128)(2,1)S(1)} %get-tuple-element.37), channel_id=1, source_target_pairs={{0,6},{2,0},{4,2},{6,4},{1,7},{3,1},{5,3},{7,5},{8,14},{10,8},{12,... | collective-permute-start | bytes 393224 | tf_op jit(solution)/shard_map/ppermute | solution.py:23
  215.1 33.2 %collective-permute-start.7 = (bf16[32,2048]{1,0:T(8,128)(2,1)S(1)}, bf16[32,2048]{1,0:T(8,128)(2,1)}, u32[]{:S(2)}, u32[]{:S(2)}) collective-permute-start(bf16[32,2048]{1,0:T(8,128)(2,1)S(1)} %get-tuple-element.38), channel_id=1, source_target_pairs={{0,4},{2,6},{4,0},{6,2},{1,5},{3,7},{5,1},{7,3},{8,12},{10,14},{12... | collective-permute-start | bytes 393224 | tf_op jit(solution)/shard_map/ppermute | solution.py:23
  222.2 26.0 %collective-permute-start.8 = (bf16[32,2048]{1,0:T(8,128)(2,1)S(1)}, bf16[32,2048]{1,0:T(8,128)(2,1)}, u32[]{:S(2)}, u32[]{:S(2)}) collective-permute-start(bf16[32,2048]{1,0:T(8,128)(2,1)S(1)} %get-tuple-element.39), channel_id=1, source_target_pairs={{0,2},{2,4},{4,6},{6,0},{1,3},{3,5},{5,7},{7,1},{8,10},{10,12},{12... | collective-permute-start | bytes 393224 | tf_op jit(solution)/shard_map/ppermute | solution.py:23
  237.1 16.7 %collective-permute-start.9 = (bf16[32,2048]{1,0:T(8,128)(2,1)S(1)}, bf16[32,2048]{1,0:T(8,128)(2,1)S(1)}, u32[]{:S(2)}, u32[]{:S(2)}) collective-permute-start(bf16[32,2048]{1,0:T(8,128)(2,1)S(1)} %get-tuple-element.43), channel_id=1, source_target_pairs={{0,6},{2,0},{4,2},{6,4},{1,7},{3,1},{5,3},{7,5},{8,14},{10,8},{12,... | collective-permute-start | bytes 393224 | tf_op jit(solution)/shard_map/ppermute | solution.py:23
  239.0 22.5 %collective-permute-start.10 = (bf16[32,2048]{1,0:T(8,128)(2,1)S(1)}, bf16[32,2048]{1,0:T(8,128)(2,1)S(1)}, u32[]{:S(2)}, u32[]{:S(2)}) collective-permute-start(bf16[32,2048]{1,0:T(8,128)(2,1)S(1)} %get-tuple-element.44), channel_id=1, source_target_pairs={{0,4},{2,6},{4,0},{6,2},{1,5},{3,7},{5,1},{7,3},{8,12},{10,14},{12... | collective-permute-start | bytes 393224 | tf_op jit(solution)/shard_map/ppermute | solution.py:23
  245.7 20.1 %collective-permute-start.11 = (bf16[32,2048]{1,0:T(8,128)(2,1)S(1)}, bf16[32,2048]{1,0:T(8,128)(2,1)S(1)}, u32[]{:S(2)}, u32[]{:S(2)}) collective-permute-start(bf16[32,2048]{1,0:T(8,128)(2,1)S(1)} %get-tuple-element.45), channel_id=1, source_target_pairs={{0,2},{2,4},{4,6},{6,0},{1,3},{3,5},{5,7},{7,1},{8,10},{10,12},{12... | collective-permute-start | bytes 393224 | tf_op jit(solution)/shard_map/ppermute | solution.py:23
  (10 other events, 28.1 us)
Sparse Core Ops, SparseCore 0:
  10.9 129.9 all-gather.1

commit v3 on v2

v3 whole, which is shorter than its diff:
```python
import functools

import jax
import jax.numpy as jnp
from jax import lax
from jax.experimental import pallas as pl
from jax.experimental.pallas import tpu as pltpu
from jax.sharding import Mesh, PartitionSpec as P

EXPERT = ("y", "x", "z", "c")
PLANE = ("y", "x", "c")
BF = jnp.bfloat16
F32 = jnp.float32
STEP = 512
MORE = 128
ROWS = 256
GRANT = 60 << 20
LAST = (((1,), (1,)), ((), ()))


def along_z(value, shift):
    count = lax.axis_size("z")
    return lax.ppermute(value, "z", [(i, (i + shift) % count) for i in range(count)])


def cost(flops, size):
    return pl.CostEstimate(flops=flops, bytes_accessed=size, transcendentals=0)


def route_body(place_ref, f0, f1, f2, f3, pick_ref, scale_ref, back_ref, high_ref, low_ref):
    n, slots = back_ref.shape
    facts = jnp.concatenate([f[...] for f in (f0, f1, f2, f3)], axis=0).astype(F32)
    ids = facts[:, 0:8].astype(jnp.int32)
    prob = facts[:, 8:16] + facts[:, 16:24] + facts[:, 24:32]
    place = jnp.where(((ids >> 1) & 3) == place_ref[0], ((ids >> 3) << 1) + (ids & 1), -1)
    col = lax.broadcasted_iota(jnp.int32, (n, slots), 1)
    row = lax.broadcasted_iota(jnp.int32, (n, slots), 0)
    dest = col >> 4
    hit = jnp.zeros((n, slots), jnp.bool_)
    weight = jnp.zeros((n, slots), F32)
    for k in range(8):
        same = place[:, k : k + 1] == dest
        hit = hit | same
        weight = jnp.where(same, prob[:, k : k + 1], weight)
    r2 = lax.broadcasted_iota(jnp.int32, (n, n), 0)
    c2 = lax.broadcasted_iota(jnp.int32, (n, n), 1)
    below = ((c2 < r2) & ((c2 >> 4) == (r2 >> 4))).astype(F32).astype(BF)
    earlier = jnp.dot(below, hit.astype(F32).astype(BF), preferred_element_type=F32)
    block = ((row >> 5) == ((col >> 1) & 3)) & (((row >> 4) & 1) == ((col >> 3) & 1))
    pick = hit & block & (earlier == (col & 1).astype(F32))
    pick_f = pick.astype(F32)
    scaled = jnp.where(pick, weight, 0.0)
    back_ref[...] = pick_f.astype(BF)
    high = scaled.astype(BF)
    high_ref[...] = high
    low_ref[...] = (scaled - high.astype(F32)).astype(BF)
    pick_ref[...] = jnp.transpose(pick_f).astype(BF)
    scale_ref[...] = jnp.sum(jnp.transpose(scaled), axis=1, keepdims=True)


def route(place, mine, up, far, down, slots):
    tokens = mine.shape[0] // 2
    n = tokens * 4
    last = mine.shape[1] // MORE - 1
    facts = pl.BlockSpec((tokens, MORE), lambda i: (0, last))

    def whole(a, b):
        return pl.BlockSpec((a, b), lambda i: (0, 0))

    return pl.pallas_call(
        route_body,
        grid=(1,),
        in_specs=[pl.BlockSpec(memory_space=pltpu.SMEM)] + [facts] * 4,
        out_specs=[whole(slots, n), whole(slots, 1)] + [whole(n, slots)] * 3,
        out_shape=[jax.ShapeDtypeStruct((slots, n), BF), jax.ShapeDtypeStruct((slots, 1), F32)]
        + [jax.ShapeDtypeStruct((n, slots), BF)] * 3,
        compiler_params=pltpu.CompilerParams(vmem_limit_bytes=16 << 20),
        cost_estimate=cost(1 << 26, 1 << 20),
    )(place, mine, up, far, down)


def select_tokens_body(pick_ref, a0, a1, a2, a3, rows_ref):
    tokens = jnp.concatenate([a[...] for a in (a0, a1, a2, a3)], axis=0)
    rows = jnp.dot(pick_ref[...], tokens, preferred_element_type=F32)
    rows_ref[...] = rows.astype(BF).reshape(rows_ref.shape)


def select_grads_body(pick_ref, scale_ref, a0, a1, a2, a3, _, rows_ref):
    tokens = jnp.concatenate([a[...] for a in (a0, a1, a2, a3)], axis=0)
    rows = jnp.dot(pick_ref[...], tokens, preferred_element_type=F32)
    rows_ref[...] = (rows * scale_ref[...]).astype(BF).reshape(rows_ref.shape)


def select(pick, mine, up, far, down, plane, scale=None, rows=None):
    slots, n = pick.shape
    part, width = n // 4, mine.shape[1] - MORE
    which = 0 if rows is None else 1
    step = 2 * STEP
    near = pl.BlockSpec((part, step), lambda j: (which, j))
    distant = pl.BlockSpec((part, step), lambda j: (0, j))
    whole = pl.BlockSpec((slots, n), lambda j: (0, 0))
    specs = [near, near, distant, near]
    if which:
        specs = [whole, pl.BlockSpec((slots, 1), lambda j: (0, 0)), *specs, pl.BlockSpec(memory_space=pl.ANY)]
        operands = (pick, scale, mine, up, far, down, rows)
    else:
        specs = [whole, *specs]
        operands = (pick, mine, up, far, down)
    return pl.pallas_call(
        select_grads_body if which else select_tokens_body,
        grid=(width // step,),
        in_specs=specs,
        out_specs=pl.BlockSpec((plane, None, slots // plane, step), lambda j: (0, which, 0, j)),
        out_shape=jax.ShapeDtypeStruct((plane, 2, slots // plane, width), BF),
        input_output_aliases={len(operands) - 1: 0} if which else {},
        compiler_params=pltpu.CompilerParams(vmem_limit_bytes=GRANT),
        cost_estimate=cost(1 << 29, 3 << 20),
    )(*operands)


def forward_body(rows_hbm, weights_hbm, out_hbm, x_ref, w_ref, out_ref, came, went):
    plane, _, count, width = rows_hbm.shape
    hid = w_ref.shape[2] // 3
    steps = width // STEP

    def taken(k):
        columns = pl.ds(k * STEP, STEP)
        return (
            pltpu.make_async_copy(rows_hbm.at[:, 0, :, columns], x_ref.at[k], came.at[2 * k]),
            pltpu.make_async_copy(weights_hbm.at[columns], w_ref.at[k], came.at[2 * k + 1]),
        )

    def given(k):
        return pltpu.make_async_copy(out_ref.at[k], out_hbm.at[:, pl.ds(k * STEP, STEP)], went.at[k])

    for k in range(steps):
        for copy in taken(k):
            copy.start()
    projected = None
    for k in range(steps):
        for copy in taken(k):
            copy.wait()
        x = x_ref[k].reshape(plane * count, STEP)
        term = jnp.dot(x, w_ref[k, :, : 2 * hid], preferred_element_type=F32)
        projected = term if projected is None else projected + term
    gate_part = projected[:, :hid]
    hidden = (gate_part * jax.nn.sigmoid(gate_part) * projected[:, hid:]).astype(BF)
    for k in range(steps):
        out = lax.dot_general(hidden, w_ref[k, :, 2 * hid :], LAST, preferred_element_type=F32)
        out_ref[k] = out.astype(BF)
        given(k).start()
    for k in range(steps):
        given(k).wait()


def forward(rows, weights):
    plane, _, count, width = rows.shape
    total, steps = plane * count, width // STEP
    anywhere = pl.BlockSpec(memory_space=pl.ANY)
    return pl.pallas_call(
        forward_body,
        in_specs=[anywhere, anywhere],
        out_specs=anywhere,
        out_shape=jax.ShapeDtypeStruct((total, width), BF),
        scratch_shapes=[
            pltpu.VMEM((steps, plane, count, STEP), BF),
            pltpu.VMEM((steps, STEP, weights.shape[1]), BF),
            pltpu.VMEM((steps, total, STEP), BF),
            pltpu.SemaphoreType.DMA((2 * steps,)),
            pltpu.SemaphoreType.DMA((steps,)),
        ],
        compiler_params=pltpu.CompilerParams(vmem_limit_bytes=GRANT),
        cost_estimate=cost(5 << 29, 10 << 20),
    )(rows, weights)


def backward_body(x_ref, g_ref, w_ref, out_ref):
    hid = w_ref.shape[1] // 3
    x = x_ref[...].reshape(out_ref.shape)
    g = g_ref[...].reshape(out_ref.shape)
    projected = jnp.dot(x, w_ref[:, : 2 * hid], preferred_element_type=F32)
    d_hidden = jnp.dot(g, w_ref[:, 2 * hid :], preferred_element_type=F32)
    gate_part = projected[:, :hid]
    sig = jax.nn.sigmoid(gate_part)
    d_gate = d_hidden * projected[:, hid:] * sig * (1.0 + gate_part * (1.0 - sig))
    d_upper = d_hidden * gate_part * sig
    d_joined = jnp.concatenate([d_gate.astype(BF), d_upper.astype(BF)], axis=1)
    for j in range(0, out_ref.shape[1], STEP):
        out = lax.dot_general(d_joined, w_ref[j : j + STEP, : 2 * hid], LAST, preferred_element_type=F32)
        out_ref[:, j : j + STEP] = out.astype(BF)


def backward(rows, weights):
    plane, _, count, width = rows.shape
    total = plane * count

    def taken(which):
        return pl.BlockSpec((ROWS // count, None, count, width), lambda i: (i, which, 0, 0))

    return pl.pallas_call(
        backward_body,
        grid=(total // ROWS,),
        in_specs=[
            taken(0),
            taken(1),
            pl.BlockSpec(weights.shape, lambda i: (0, 0), pipeline_mode=pl.Buffered(1)),
        ],
        out_specs=pl.BlockSpec((ROWS, width), lambda i: (i, 0)),
        out_shape=jax.ShapeDtypeStruct((total, width), BF),
        compiler_params=pltpu.CompilerParams(vmem_limit_bytes=GRANT),
        cost_estimate=cost(7 << 29, 10 << 20),
    )(rows, rows, weights)


def combine_body(count, *refs):
    factors, rows, own_ref = refs[:count], refs[count][...], refs[count + 1]
    total = jnp.dot(factors[0][...], rows, preferred_element_type=F32)
    for f in factors[1:]:
        total = total + jnp.dot(f[...], rows, preferred_element_type=F32)
    m = own_ref.shape[0]
    own_ref[...] = total[:m]
    for s, ref in enumerate(refs[count + 2 :], 1):
        ref[...] = total[s * m : (s + 1) * m].astype(BF)


def combine(factors, rows):
    n, slots = factors[0].shape
    width = rows.shape[1]
    part = pl.BlockSpec((n // 4, STEP), lambda j: (0, j))
    return pl.pallas_call(
        functools.partial(combine_body, len(factors)),
        grid=(width // STEP,),
        in_specs=[pl.BlockSpec((n, slots), lambda j: (0, 0))] * len(factors)
        + [pl.BlockSpec((slots, STEP), lambda j: (0, j))],
        out_specs=[part] * 4,
        out_shape=[jax.ShapeDtypeStruct((n // 4, width), F32)]
        + [jax.ShapeDtypeStruct((n // 4, width), BF)] * 3,
        compiler_params=pltpu.CompilerParams(vmem_limit_bytes=16 << 20),
        cost_estimate=cost(1 << 28, 3 << 20),
    )(*factors, rows)


def in_plane(rows):
    return lax.all_to_all(rows, PLANE, 0, 0, tiled=True)


def local(hidden_in, cotangent, expert_ids, route_prob, swap_flags, gate_up, down_t):
    micro, tok, width = hidden_in.shape
    top = expert_ids.shape[2]
    hid = down_t.shape[2]
    nz = lax.axis_size("z")
    ny = lax.axis_size("y")
    plane = ny * lax.axis_size("x") * 2
    count = micro * nz * 2
    my_z = lax.axis_index("z")
    half = ny * lax.axis_size("x") * nz
    my_index = lax.axis_index(EXPERT)

    weights = jnp.concatenate([gate_up.reshape(-1, 2 * hid), down_t.reshape(-1, hid)], axis=1)
    weights = lax.all_gather(weights, "dp", axis=0, tiled=True)

    flag = jnp.sum(jnp.where(jnp.arange(half, dtype=jnp.int32) == my_index % half, swap_flags, 0))
    pairs = [(i, i ^ (ny // 2)) for i in range(ny)]

    high = lax.reduce_precision(route_prob, 8, 7)
    middle = lax.reduce_precision(route_prob - high, 8, 7)
    low = route_prob - high - middle
    facts = jnp.concatenate([expert_ids.astype(F32), high, middle, low], axis=2).astype(BF)
    facts = jnp.pad(facts.reshape(micro * tok, 4 * top), ((0, micro * tok), (0, MORE - 4 * top)))
    mine = jnp.concatenate([hidden_in, cotangent], axis=0).reshape(2 * micro * tok, width)
    mine = jnp.concatenate([mine, facts], axis=1)
    gate_own, down_own, mine = lax.optimization_barrier((gate_up, down_t, mine))
    other_gate = lax.ppermute(gate_own, "y", pairs)
    other_down = lax.ppermute(down_own, "y", pairs)
    up, down = along_z(mine, 1), along_z(mine, -1)
    split = micro * tok
    far = (along_z(down[:split], -1), along_z(up[split:], 1))

    place = jnp.full((1,), my_z, jnp.int32)
    pick, scale, back, w_high, w_low = route(place, mine, up, far[0], down, plane * count)
    rows = select(pick, mine, up, far[0], down, plane)
    rows = select(pick, mine, up, far[1], down, plane, scale, rows)
    rows, other_gate, other_down = lax.optimization_barrier((rows, other_gate, other_down))
    rows = in_plane(rows)

    expert_out = forward(rows, weights)
    back_out = in_plane(expert_out.reshape(plane, count, width)).reshape(plane * count, width)
    row_input = backward(rows, weights)
    back_out, row_input = lax.optimization_barrier((back_out, row_input))
    back_grad = in_plane(row_input.reshape(plane, count, width)).reshape(plane * count, width)
    resident_gate = jnp.where(flag == 1, other_gate, gate_up)
    resident_down = jnp.where(flag == 1, other_down, down_t)

    results = []
    for factors, moved in (((w_high, w_low), back_out), ((back,), back_grad)):
        own, *others = combine(factors, moved)
        for s, part in enumerate(others, 1):
            own = own + along_z(part, -s).astype(F32)
        results.append(own.astype(BF).reshape(micro, tok, width))
    return (results[0], results[1], resident_gate, resident_down)


def solution(mesh):
    devices = mesh.devices.reshape(4, 4, 4, 4, 2)
    fine = Mesh(devices, ("dp", "y", "x", "z", "c"))
    tokens = P(None, ("dp",) + EXPERT, None)
    placed = (
        tokens,
        tokens,
        tokens,
        tokens,
        P(),
        P(EXPERT, "dp", None, None),
        P(EXPERT, "dp", None),
    )
    return jax.shard_map(
        local,
        mesh=fine,
        in_specs=placed,
        out_specs=(tokens, tokens, P(EXPERT, "dp", None, None), P(EXPERT, "dp", None)),
        check_vma=False,
    )
```

time: 274 us -> 269 us (0.982)
  the two profiles are of different devices: /device:TPU:35 before, /device:TPU:64 now
where the time goes in v3:
time: 269 us; the launch traced here: 268 us
  waiting for transfers between devices  83.1 us (31%)
  starting transfers between devices  76 us (28%)
  blocking collectives  56.2 us (21%)
  Pallas kernels  25.5 us (9%)
  between operations  15.1 us (6%)
  other arithmetic  7.48 us (3%)
  local copies, waits for them, and re-layouts  5.08 us (2%)
    ppermute x10, starting transfers between devices, along_z(): lax.ppermute(value, 'z', [(i, (i + shift) % count) for i in range(count)])  60.4 us
    ppermute x10, waiting for transfers between devices, along_z(): lax.ppermute(value, 'z', [(i, (i + shift) % count) for i in range(count)])  56.3 us
    all_to_all x1, blocking collectives, in_plane(): return lax.all_to_all(rows, PLANE, 0, 0, tiled=True)  56.2 us
    all_to_all x2, waiting for transfers between devices, in_plane(): return lax.all_to_all(rows, PLANE, 0, 0, tiled=True)  26.8 us
    pallas_call x1, Pallas kernels, backward(): pl.pallas_call(backward_body, grid=(total // ROWS,), in_specs=[taken(0),...  8.77 us
    all_to_all x2, starting transfers between devices, in_plane(): return lax.all_to_all(rows, PLANE, 0, 0, tiled=True)  8.17 us
    pallas_call x1, Pallas kernels, forward(): pl.pallas_call(forward_body, in_specs=[anywhere, anywhere], out_specs=any...  6.92 us
    pallas_call x2, Pallas kernels, select(): pl.pallas_call(select_grads_body if which else select_tokens_body, grid=(...  6.06 us
  transfers between devices with their start and end apart: 15, of which 8 were waited for; matrix products, arithmetic and copies ran while one was open for 2% of the time, Pallas kernels for 7%

profile of v3, /device:TPU:64, one launch (start us, length us, event | category | flops | bytes accessed | tf_op | source)
XLA Modules:
  0.0 268.4 jit_solution(13619925898617649426)
XLA Ops:
  11.3 5.1 %collective-permute-start.4 = (bf16[1,512,2,384]{3,2,1,0:T(2,128)(2,1)S(1)}, bf16[1,512,2,384]{3,2,1,0:T(2,128)(2,1)}, u32[]{:S(2)}, u32[]{:S(2)}) collective-permute-start(bf16[1,512,2,384]{3,2,1,0:T(2,128)(2,1)S(1)} %copy-done.8), channel_id=1, source_target_pairs={{0,64},{32,96},{64,0},{96,32},{1,65},{33,97},{65,1},{97,33},{2,66}... | collective-permute-start | bytes 2359304 | tf_op jit(solution)/shard_map/ppermute | solution.py:273
  16.5 10.9 %collective-permute-start.1 = (bf16[64,2176]{1,0:T(8,128)(2,1)S(1)}, bf16[64,2176]{1,0:T(8,128)(2,1)S(1)}, u32[]{:S(2)}, u32[]{:S(2)}) collective-permute-start(bf16[64,2176]{1,0:T(8,128)(2,1)S(1)} %pad_maximum_fusion.1.f0.a0), channel_id=1, source_target_pairs={{0,6},{2,0},{4,2},{6,4},{1,7},{3,1},{5,3},{7,5},{8,14},{10,8},{12,... | collective-permute-start | bytes 835592 | tf_op jit(solution)/shard_map/ppermute | solution.py:23
  29.3 2.2 collective-permute-start.5
  31.6 33.4 %collective-permute-done.1.f3.a3 = bf16[64,2176]{1,0:T(8,128)(2,1)S(1)} collective-permute-done((bf16[64,2176]{1,0:T(8,128)(2,1)S(1)}, bf16[64,2176]{1,0:T(8,128)(2,1)S(1)}, u32[]{:S(2)}, u32[]{:S(2)}) %collective-permute-start.1) | collective-permute-done | bytes 278560 | tf_op jit(solution)/shard_map/ppermute | solution.py:23
  65.0 8.3 %collective-permute-start.2 = (bf16[32,2176]{1,0:T(8,128)(2,1)S(1)}, bf16[32,2176]{1,0:T(8,128)(2,1)S(1)}, u32[]{:S(2)}, u32[]{:S(2)}) collective-permute-start(bf16[32,2176]{1,0:T(8,128)(2,1)S(1)} %slice.8), channel_id=1, source_target_pairs={{0,6},{2,0},{4,2},{6,4},{1,7},{3,1},{5,3},{7,5},{8,14},{10,8},{12,... | collective-permute-start | bytes 417800 | tf_op jit(solution)/shard_map/ppermute | solution.py:23
  75.3 9.1 %collective-permute-done.2.f2.a2 = bf16[32,2176]{1,0:T(8,128)(2,1)S(1)} collective-permute-done((bf16[32,2176]{1,0:T(8,128)(2,1)S(1)}, bf16[32,2176]{1,0:T(8,128)(2,1)S(1)}, u32[]{:S(2)}, u32[]{:S(2)}) %collective-permute-start.2) | collective-permute-done | bytes 139296 | tf_op jit(solution)/shard_map/ppermute | solution.py:23
  86.9 3.0 %shard_map.103._ = bf16[32,2,16,2048]{3,2,1,0:T(8,128)(2,1)} custom-call(bf16[512,128]{1,0:T(8,128)(2,1)} %copy-done.6, bf16[64,2176]{1,0:T(8,128)(2,1)} %copy-done.2, bf16[64,2176]{1,0:T(8,128)(2,1)} %copy-done.4, bf16[32,2176]{1,0:T(8,128)(2,1)} %copy-done.5, bf16[64,2176]{1,0:T(8,128)(2,1)} %copy-done.3), custom_call_target="tpu_custom_call" | custom-call | flops 536870912 | bytes 3145728 | tf_op jit(solution)/shard_map/pallas_call | solution.py:109
  89.8 4.3 %collective-permute-done.3.a2 = bf16[32,2176]{1,0:T(8,128)(2,1)S(1)} collective-permute-done((bf16[32,2176]{1,0:T(8,128)(2,1)S(1)}, bf16[32,2176]{1,0:T(8,128)(2,1)S(1)}, u32[]{:S(2)}, u32[]{:S(2)}) %collective-permute-start.3) | collective-permute-done | bytes 139296 | tf_op jit(solution)/shard_map/ppermute | solution.py:23
  94.8 3.1 %shard_map.104 = bf16[32,2,16,2048]{3,2,1,0:T(8,128)(2,1)} custom-call(bf16[512,128]{1,0:T(8,128)(2,1)} %copy-done.6, f32[512,1]{1,0:T(8,128)} %copy-done.7, bf16[64,2176]{1,0:T(8,128)(2,1)} %copy-done.2, bf16[64,2176]{1,0:T(8,128)(2,1)} %copy-done.4, bf16[32,2176]{1,0:T(8,128)(2,1)} %copy-done.13, ...), custom_call_target="tpu_custom_call", output_to_operand_aliasing={{}: (6, {})} | custom-call | flops 536870912 | bytes 3145728 | tf_op jit(solution)/shard_map/pallas_call | solution.py:109
  97.9 56.2 %all_to_all.15.rows_hbm.x_ref.g_ref = bf16[32,2,16,2048]{3,2,1,0:T(8,128)(2,1)} all-to-all(bf16[32,2,16,2048]{3,2,1,0:T(8,128)(2,1)} %shard_map.104), channel_id=1, replica_groups=mesh['dp'=4,'y'=4,'x'=4,'z'=4,'c'=2] {'y','x','c'}, dimensions={0} | all-to-all | bytes 8388608 | tf_op jit(solution)/shard_map/all_to_all | solution.py:244
  154.1 6.9 %shard_map.105 = bf16[512,2048]{1,0:T(8,128)(2,1)} custom-call(bf16[32,2,16,2048]{3,2,1,0:T(8,128)(2,1)} %all_to_all.15.rows_hbm.x_ref.g_ref, bf16[2048,1152]{1,0:T(8,128)(2,1)} %all-gather.2.cloned.1.call-done.weights_hbm.w_ref), custom_call_target="tpu_custom_call" | custom-call | flops 2684354560 | bytes 10485760 | tf_op jit(solution)/shard_map/pallas_call | solution.py:160
  161.0 4.0 %all-to-all-start.1 = ((bf16[32,16,2048]{2,1,0:T(8,128)(2,1)}), bf16[32,16,2048]{2,1,0:T(8,128)(2,1)S(1)}, u32[]{:S(2)}, u32[]{:S(2)}) async-start(bf16[32,16,2048]{2,1,0:T(8,128)(2,1)} %bitcast.21), calls=%async_computation.1 | async-start | bytes 4194304 | tf_op jit(solution)/shard_map/all_to_all | solution.py:244
  165.0 8.8 %shard_map.106 = bf16[512,2048]{1,0:T(8,128)(2,1)} custom-call(bf16[32,2,16,2048]{3,2,1,0:T(8,128)(2,1)} %all_to_all.15.rows_hbm.x_ref.g_ref, bf16[32,2,16,2048]{3,2,1,0:T(8,128)(2,1)} %all_to_all.15.rows_hbm.x_ref.g_ref, bf16[2048,1152]{1,0:T(8,128)(2,1)} %all-gather.2.cloned.1.call-done.weights_hbm.w_ref), custom_call_target="tpu_custom_call" | custom-call | flops 3758096384 | bytes 10485760 | tf_op jit(solution)/shard_map/pallas_call | solution.py:200
  173.8 21.2 %all-to-all-done.1 = bf16[32,16,2048]{2,1,0:T(8,128)(2,1)S(1)} async-done(((bf16[32,16,2048]{2,1,0:T(8,128)(2,1)}), bf16[32,16,2048]{2,1,0:T(8,128)(2,1)S(1)}, u32[]{:S(2)}, u32[]{:S(2)}) %all-to-all-start.1) | async-done | bytes 2097184 | tf_op jit(solution)/shard_map/all_to_all | solution.py:244
  196.4 4.1 %all-to-all-start.2 = ((bf16[32,16,2048]{2,1,0:T(8,128)(2,1)}), bf16[32,16,2048]{2,1,0:T(8,128)(2,1)S(1)}, u32[]{:S(2)}, u32[]{:S(2)}) async-start(bf16[32,16,2048]{2,1,0:T(8,128)(2,1)} %bitcast.22), calls=%async_computation.2 | async-start | bytes 4194304 | tf_op jit(solution)/shard_map/all_to_all | solution.py:244
  201.9 2.3 broadcast_select_fusion
  205.7 7.5 %collective-permute-start.6 = (bf16[32,2048]{1,0:T(8,128)(2,1)S(1)}, bf16[32,2048]{1,0:T(8,128)(2,1)S(1)}, u32[]{:S(2)}, u32[]{:S(2)}) collective-permute-start(bf16[32,2048]{1,0:T(8,128)(2,1)S(1)} %get-tuple-element.35), channel_id=1, source_target_pairs={{0,6},{2,0},{4,2},{6,4},{1,7},{3,1},{5,3},{7,5},{8,14},{10,8},{12,... | collective-permute-start | bytes 393224 | tf_op jit(solution)/shard_map/ppermute | solution.py:23
  213.1 3.6 %collective-permute-start.7 = (bf16[32,2048]{1,0:T(8,128)(2,1)S(1)}, bf16[32,2048]{1,0:T(8,128)(2,1)S(1)}, u32[]{:S(2)}, u32[]{:S(2)}) collective-permute-start(bf16[32,2048]{1,0:T(8,128)(2,1)S(1)} %get-tuple-element.36), channel_id=1, source_target_pairs={{0,4},{2,6},{4,0},{6,2},{1,5},{3,7},{5,1},{7,3},{8,12},{10,14},{12... | collective-permute-start | bytes 393224 | tf_op jit(solution)/shard_map/ppermute | solution.py:23
  216.7 7.4 %collective-permute-start.8 = (bf16[32,2048]{1,0:T(8,128)(2,1)S(1)}, bf16[32,2048]{1,0:T(8,128)(2,1)S(1)}, u32[]{:S(2)}, u32[]{:S(2)}) collective-permute-start(bf16[32,2048]{1,0:T(8,128)(2,1)S(1)} %get-tuple-element.37), channel_id=1, source_target_pairs={{0,2},{2,4},{4,6},{6,0},{1,3},{3,5},{5,7},{7,1},{8,10},{10,12},{12... | collective-permute-start | bytes 393224 | tf_op jit(solution)/shard_map/ppermute | solution.py:23
  224.9 5.6 %all-to-all-done.2 = bf16[32,16,2048]{2,1,0:T(8,128)(2,1)S(1)} async-done(((bf16[32,16,2048]{2,1,0:T(8,128)(2,1)}), bf16[32,16,2048]{2,1,0:T(8,128)(2,1)S(1)}, u32[]{:S(2)}, u32[]{:S(2)}) %all-to-all-start.2) | async-done | bytes 2097184 | tf_op jit(solution)/shard_map/all_to_all | solution.py:244
  231.7 9.1 %collective-permute-start.10 = (bf16[32,2048]{1,0:T(8,128)(2,1)S(1)}, bf16[32,2048]{1,0:T(8,128)(2,1)S(1)}, u32[]{:S(2)}, u32[]{:S(2)}) collective-permute-start(bf16[32,2048]{1,0:T(8,128)(2,1)S(1)} %get-tuple-element.42), channel_id=1, source_target_pairs={{0,4},{2,6},{4,0},{6,2},{1,5},{3,7},{5,1},{7,3},{8,12},{10,14},{12... | collective-permute-start | bytes 393224 | tf_op jit(solution)/shard_map/ppermute | solution.py:23
  240.8 6.1 %collective-permute-start.11 = (bf16[32,2048]{1,0:T(8,128)(2,1)S(1)}, bf16[32,2048]{1,0:T(8,128)(2,1)S(1)}, u32[]{:S(2)}, u32[]{:S(2)}) collective-permute-start(bf16[32,2048]{1,0:T(8,128)(2,1)S(1)} %get-tuple-element.43), channel_id=1, source_target_pairs={{0,2},{2,4},{4,6},{6,0},{1,3},{3,5},{5,7},{7,1},{8,10},{10,12},{12... | collective-permute-start | bytes 393224 | tf_op jit(solution)/shard_map/ppermute | solution.py:23
  246.9 3.7 %collective-permute-start.9 = (bf16[32,2048]{1,0:T(8,128)(2,1)S(1)}, bf16[32,2048]{1,0:T(8,128)(2,1)S(1)}, u32[]{:S(2)}, u32[]{:S(2)}) collective-permute-start(bf16[32,2048]{1,0:T(8,128)(2,1)S(1)} %get-tuple-element.41), channel_id=1, source_target_pairs={{0,6},{2,0},{4,2},{6,4},{1,7},{3,1},{5,3},{7,5},{8,14},{10,8},{12,... | collective-permute-start | bytes 393224 | tf_op jit(solution)/shard_map/ppermute | solution.py:23
  251.4 7.9 %collective-permute-done.10 = bf16[32,2048]{1,0:T(8,128)(2,1)S(1)} collective-permute-done((bf16[32,2048]{1,0:T(8,128)(2,1)S(1)}, bf16[32,2048]{1,0:T(8,128)(2,1)S(1)}, u32[]{:S(2)}, u32[]{:S(2)}) %collective-permute-start.10) | collective-permute-done | bytes 131104 | tf_op jit(solution)/shard_map/ppermute | solution.py:23
  (71 shorter events, 19.5 us)
Async XLA Ops:
  7.2 146.9 %all-gather.2.cloned.1.call-start = ((), (), s32[]{:S(2)}) async-start(), calls=%async_computation.3 | async-start | bytes 5898240 | tf_op jit(solution)/shard_map/all_gather | solution.py:260
  8.5 2.8 %copy-start.8 = (bf16[1,512,2,384]{3,2,1,0:T(2,128)(2,1)S(1)}, bf16[1,512,2,384]{3,2,1,0:T(2,128)(2,1)}, u32[]{:S(2)}) copy-start(bf16[1,512,2,384]{3,2,1,0:T(2,128)(2,1)} %param.12) | copy-start | bytes 2359300
  8.5 20.8 %copy-start.9 = (bf16[1,512,384]{2,1,0:T(8,128)(2,1)S(1)}, bf16[1,512,384]{2,1,0:T(8,128)(2,1)}, u32[]{:S(2)}) copy-start(bf16[1,512,384]{2,1,0:T(8,128)(2,1)} %param.13) | copy-start | bytes 1179652
  11.3 75.5 %copy-start.2 = (bf16[64,2176]{1,0:T(8,128)(2,1)}, bf16[64,2176]{1,0:T(8,128)(2,1)S(1)}, u32[]{:S(2)}) copy-start(bf16[64,2176]{1,0:T(8,128)(2,1)S(1)} %pad_maximum_fusion.1.f0.a0) | copy-start | bytes 835588
  11.3 86.5 %collective-permute-start.4 = (bf16[1,512,2,384]{3,2,1,0:T(2,128)(2,1)S(1)}, bf16[1,512,2,384]{3,2,1,0:T(2,128)(2,1)}, u32[]{:S(2)}, u32[]{:S(2)}) collective-permute-start(bf16[1,512,2,384]{3,2,1,0:T(2,128)(2,1)S(1)} %copy-done.8), channel_id=1, source_target_pairs={{0,64},{32,96},{64,0},{96,32},{1,65},{33,97},{65,1},{97,33},{2,66}... | collective-permute-start | bytes 2359304 | tf_op jit(solution)/shard_map/ppermute | solution.py:273
  16.5 48.6 %collective-permute-start.1 = (bf16[64,2176]{1,0:T(8,128)(2,1)S(1)}, bf16[64,2176]{1,0:T(8,128)(2,1)S(1)}, u32[]{:S(2)}, u32[]{:S(2)}) collective-permute-start(bf16[64,2176]{1,0:T(8,128)(2,1)S(1)} %pad_maximum_fusion.1.f0.a0), channel_id=1, source_target_pairs={{0,6},{2,0},{4,2},{6,4},{1,7},{3,1},{5,3},{7,5},{8,14},{10,8},{12,... | collective-permute-start | bytes 835592 | tf_op jit(solution)/shard_map/ppermute | solution.py:23
  27.4 46.0 %collective-permute-start = (bf16[64,2176]{1,0:T(8,128)(2,1)S(1)}, bf16[64,2176]{1,0:T(8,128)(2,1)S(1)}, u32[]{:S(2)}, u32[]{:S(2)}) collective-permute-start(bf16[64,2176]{1,0:T(8,128)(2,1)S(1)} %pad_maximum_fusion.1.f0.a0), channel_id=1, source_target_pairs={{0,2},{2,4},{4,6},{6,0},{1,3},{3,5},{5,7},{7,1},{8,10},{10,12},{12... | collective-permute-start | bytes 835592 | tf_op jit(solution)/shard_map/ppermute | solution.py:23
  29.3 68.5 %collective-permute-start.5 = (bf16[1,512,384]{2,1,0:T(8,128)(2,1)S(1)}, bf16[1,512,384]{2,1,0:T(8,128)(2,1)S(1)}, u32[]{:S(2)}, u32[]{:S(2)}) collective-permute-start(bf16[1,512,384]{2,1,0:T(8,128)(2,1)S(1)} %copy-done.9), channel_id=1, source_target_pairs={{0,64},{32,96},{64,0},{96,32},{1,65},{33,97},{65,1},{97,33},{2,66}... | collective-permute-start | bytes 1179656 | tf_op jit(solution)/shard_map/ppermute | solution.py:274
  65.0 21.8 %copy-start.3 = (bf16[64,2176]{1,0:T(8,128)(2,1)}, bf16[64,2176]{1,0:T(8,128)(2,1)S(1)}, u32[]{:S(2)}) copy-start(bf16[64,2176]{1,0:T(8,128)(2,1)S(1)} %collective-permute-done.1.f3.a3) | copy-start | bytes 835588
  65.0 19.4 %collective-permute-start.2 = (bf16[32,2176]{1,0:T(8,128)(2,1)S(1)}, bf16[32,2176]{1,0:T(8,128)(2,1)S(1)}, u32[]{:S(2)}, u32[]{:S(2)}) collective-permute-start(bf16[32,2176]{1,0:T(8,128)(2,1)S(1)} %slice.8), channel_id=1, source_target_pairs={{0,6},{2,0},{4,2},{6,4},{1,7},{3,1},{5,3},{7,5},{8,14},{10,8},{12,... | collective-permute-start | bytes 417800 | tf_op jit(solution)/shard_map/ppermute | solution.py:23
  73.4 13.5 %copy-start.4 = (bf16[64,2176]{1,0:T(8,128)(2,1)}, bf16[64,2176]{1,0:T(8,128)(2,1)S(1)}, u32[]{:S(2)}) copy-start(bf16[64,2176]{1,0:T(8,128)(2,1)S(1)} %collective-permute-done.f1.a1) | copy-start | bytes 835588
  73.4 20.7 %collective-permute-start.3 = (bf16[32,2176]{1,0:T(8,128)(2,1)S(1)}, bf16[32,2176]{1,0:T(8,128)(2,1)S(1)}, u32[]{:S(2)}, u32[]{:S(2)}) collective-permute-start(bf16[32,2176]{1,0:T(8,128)(2,1)S(1)} %slice.9), channel_id=1, source_target_pairs={{0,2},{2,4},{4,6},{6,0},{1,3},{3,5},{5,7},{7,1},{8,10},{10,12},{12... | collective-permute-start | bytes 417800 | tf_op jit(solution)/shard_map/ppermute | solution.py:23
  97.9 56.2 %copy-start.11 = (bf16[1,512,384]{2,1,0:T(8,128)(2,1)}, bf16[1,512,384]{2,1,0:T(8,128)(2,1)S(1)}, u32[]{:S(2)}) copy-start(bf16[1,512,384]{2,1,0:T(8,128)(2,1)S(1)} %collective-permute-done.5) | copy-start | bytes 1179652
  161.0 34.0 %all-to-all-start.1 = ((bf16[32,16,2048]{2,1,0:T(8,128)(2,1)}), bf16[32,16,2048]{2,1,0:T(8,128)(2,1)S(1)}, u32[]{:S(2)}, u32[]{:S(2)}) async-start(bf16[32,16,2048]{2,1,0:T(8,128)(2,1)} %bitcast.21), calls=%async_computation.1 | async-start | bytes 4194304 | tf_op jit(solution)/shard_map/all_to_all | solution.py:244
  196.4 4.2 %copy-start.18 = (s32[64]{0:T(128)S(1)}, s32[64]{0:T(128)}, u32[]{:S(2)}) copy-start(s32[64]{0:T(128)} %param.11) | copy-start | bytes 772
  196.4 34.1 %all-to-all-start.2 = ((bf16[32,16,2048]{2,1,0:T(8,128)(2,1)}), bf16[32,16,2048]{2,1,0:T(8,128)(2,1)S(1)}, u32[]{:S(2)}, u32[]{:S(2)}) async-start(bf16[32,16,2048]{2,1,0:T(8,128)(2,1)} %bitcast.22), calls=%async_computation.2 | async-start | bytes 4194304 | tf_op jit(solution)/shard_map/all_to_all | solution.py:244
  201.8 22.3 %copy-start.10 = (bf16[1,512,384]{2,1,0:T(8,128)(2,1)S(1)}, bf16[1,512,384]{2,1,0:T(8,128)(2,1)}, u32[]{:S(2)}) copy-start(bf16[1,512,384]{2,1,0:T(8,128)(2,1)} %param.13) | copy-start | bytes 1179652
  201.9 22.3 %copy-start.12 = (bf16[1,512,384]{2,1,0:T(8,128)(2,1)S(1)}, bf16[1,512,384]{2,1,0:T(8,128)(2,1)}, u32[]{:S(2)}) copy-start(bf16[1,512,384]{2,1,0:T(8,128)(2,1)} %copy-done.11) | copy-start | bytes 1179652
  205.7 41.3 %collective-permute-start.6 = (bf16[32,2048]{1,0:T(8,128)(2,1)S(1)}, bf16[32,2048]{1,0:T(8,128)(2,1)S(1)}, u32[]{:S(2)}, u32[]{:S(2)}) collective-permute-start(bf16[32,2048]{1,0:T(8,128)(2,1)S(1)} %get-tuple-element.35), channel_id=1, source_target_pairs={{0,6},{2,0},{4,2},{6,4},{1,7},{3,1},{5,3},{7,5},{8,14},{10,8},{12,... | collective-permute-start | bytes 393224 | tf_op jit(solution)/shard_map/ppermute | solution.py:23
  213.1 37.5 %collective-permute-start.7 = (bf16[32,2048]{1,0:T(8,128)(2,1)S(1)}, bf16[32,2048]{1,0:T(8,128)(2,1)S(1)}, u32[]{:S(2)}, u32[]{:S(2)}) collective-permute-start(bf16[32,2048]{1,0:T(8,128)(2,1)S(1)} %get-tuple-element.36), channel_id=1, source_target_pairs={{0,4},{2,6},{4,0},{6,2},{1,5},{3,7},{5,1},{7,3},{8,12},{10,14},{12... | collective-permute-start | bytes 393224 | tf_op jit(solution)/shard_map/ppermute | solution.py:23
  216.7 33.9 %collective-permute-start.8 = (bf16[32,2048]{1,0:T(8,128)(2,1)S(1)}, bf16[32,2048]{1,0:T(8,128)(2,1)S(1)}, u32[]{:S(2)}, u32[]{:S(2)}) collective-permute-start(bf16[32,2048]{1,0:T(8,128)(2,1)S(1)} %get-tuple-element.37), channel_id=1, source_target_pairs={{0,2},{2,4},{4,6},{6,0},{1,3},{3,5},{5,7},{7,1},{8,10},{10,12},{12... | collective-permute-start | bytes 393224 | tf_op jit(solution)/shard_map/ppermute | solution.py:23
  231.7 27.5 %collective-permute-start.10 = (bf16[32,2048]{1,0:T(8,128)(2,1)S(1)}, bf16[32,2048]{1,0:T(8,128)(2,1)S(1)}, u32[]{:S(2)}, u32[]{:S(2)}) collective-permute-start(bf16[32,2048]{1,0:T(8,128)(2,1)S(1)} %get-tuple-element.42), channel_id=1, source_target_pairs={{0,4},{2,6},{4,0},{6,2},{1,5},{3,7},{5,1},{7,3},{8,12},{10,14},{12... | collective-permute-start | bytes 393224 | tf_op jit(solution)/shard_map/ppermute | solution.py:23
  240.8 19.8 %collective-permute-start.11 = (bf16[32,2048]{1,0:T(8,128)(2,1)S(1)}, bf16[32,2048]{1,0:T(8,128)(2,1)S(1)}, u32[]{:S(2)}, u32[]{:S(2)}) collective-permute-start(bf16[32,2048]{1,0:T(8,128)(2,1)S(1)} %get-tuple-element.43), channel_id=1, source_target_pairs={{0,2},{2,4},{4,6},{6,0},{1,3},{3,5},{5,7},{7,1},{8,10},{10,12},{12... | collective-permute-start | bytes 393224 | tf_op jit(solution)/shard_map/ppermute | solution.py:23
  246.9 13.9 %collective-permute-start.9 = (bf16[32,2048]{1,0:T(8,128)(2,1)S(1)}, bf16[32,2048]{1,0:T(8,128)(2,1)S(1)}, u32[]{:S(2)}, u32[]{:S(2)}) collective-permute-start(bf16[32,2048]{1,0:T(8,128)(2,1)S(1)} %get-tuple-element.41), channel_id=1, source_target_pairs={{0,6},{2,0},{4,2},{6,4},{1,7},{3,1},{5,3},{7,5},{8,14},{10,8},{12,... | collective-permute-start | bytes 393224 | tf_op jit(solution)/shard_map/ppermute | solution.py:23
  (10 other events, 18.5 us)
Sparse Core Ops, SparseCore 0:
  10.9 128.4 all-gather.1

commit v4 on v3

--- a/solution.py
+++ b/solution.py
@@ -270,7 +270,7 @@
     mine = jnp.concatenate([hidden_in, cotangent], axis=0).reshape(2 * micro * tok, width)
     mine = jnp.concatenate([mine, facts], axis=1)
     gate_own, down_own, mine = lax.optimization_barrier((gate_up, down_t, mine))
-    other_gate = lax.ppermute(gate_own, "y", pairs)
+    other_gate = [lax.ppermute(part, "y", pairs) for part in jnp.split(gate_own, 2, axis=1)]
     other_down = lax.ppermute(down_own, "y", pairs)
     up, down = along_z(mine, 1), along_z(mine, -1)
     split = micro * tok
@@ -281,6 +281,7 @@
     rows = select(pick, mine, up, far[0], down, plane)
     rows = select(pick, mine, up, far[1], down, plane, scale, rows)
     rows, other_gate, other_down = lax.optimization_barrier((rows, other_gate, other_down))
+    other_gate = jnp.concatenate(other_gate, axis=1)
     rows = in_plane(rows)
 
     expert_out = forward(rows, weights)

time: 269 us -> 266 us (0.989)
  the two profiles are of different devices: /device:TPU:64 before, /device:TPU:103 now
where the time goes in v4:
time: 266 us; the launch traced here: 265 us
  starting transfers between devices  88.9 us (33%)
  blocking collectives  60.7 us (23%)
  waiting for transfers between devices  59.9 us (23%)
  Pallas kernels  25.5 us (10%)
  between operations  15.1 us (6%)
  other arithmetic  8.57 us (3%)
  local copies, waits for them, and re-layouts  6.49 us (2%)
    ppermute x10, starting transfers between devices, along_z(): lax.ppermute(value, 'z', [(i, (i + shift) % count) for i in range(count)])  62.9 us
    all_to_all x1, blocking collectives, in_plane(): return lax.all_to_all(rows, PLANE, 0, 0, tiled=True)  60.7 us
    ppermute x10, waiting for transfers between devices, along_z(): lax.ppermute(value, 'z', [(i, (i + shift) % count) for i in range(count)])  28.3 us
    all_to_all x2, waiting for transfers between devices, in_plane(): return lax.all_to_all(rows, PLANE, 0, 0, tiled=True)  20.5 us
    all_to_all x2, starting transfers between devices, in_plane(): return lax.all_to_all(rows, PLANE, 0, 0, tiled=True)  14.3 us
    all_gather x1, waiting for transfers between devices, local(): weights = lax.all_gather(weights, 'dp', axis=0, tiled=True)  11.1 us
    pallas_call x1, Pallas kernels, backward(): pl.pallas_call(backward_body, grid=(total // ROWS,), in_specs=[taken(0),...  8.77 us
    pallas_call x1, Pallas kernels, forward(): pl.pallas_call(forward_body, in_specs=[anywhere, anywhere], out_specs=any...  6.98 us
  transfers between devices with their start and end apart: 16, of which 6 were waited for; matrix products, arithmetic and copies ran while one was open for 3% of the time, Pallas kernels for 7%

profile of v4, /device:TPU:103, one launch (start us, length us, event | category | flops | bytes accessed | tf_op | source)
XLA Modules:
  0.0 265.3 jit_solution(17328752664489827589)
XLA Ops:
  8.5 2.2 pad_maximum_fusion
  11.3 9.8 %collective-permute-start.1 = (bf16[64,2176]{1,0:T(8,128)(2,1)S(1)}, bf16[64,2176]{1,0:T(8,128)(2,1)S(1)}, u32[]{:S(2)}, u32[]{:S(2)}) collective-permute-start(bf16[64,2176]{1,0:T(8,128)(2,1)S(1)} %pad_maximum_fusion.1.f0.a0), channel_id=1, source_target_pairs={{0,6},{2,0},{4,2},{6,4},{1,7},{3,1},{5,3},{7,5},{8,14},{10,8},{12,... | collective-permute-start | bytes 835592 | tf_op jit(solution)/shard_map/ppermute | solution.py:23
  24.4 4.8 %collective-permute-start.4 = (bf16[1,256,2,384]{3,2,1,0:T(2,128)(2,1)}, bf16[1,256,2,384]{3,2,1,0:T(2,128)(2,1)S(1)}, u32[]{:S(2)}, u32[]{:S(2)}) collective-permute-start(bf16[1,256,2,384]{3,2,1,0:T(2,128)(2,1)} %get-tuple-element.49), channel_id=1, source_target_pairs={{0,64},{32,96},{64,0},{96,32},{1,65},{33,97},{65,1},{97,33},{2,66}... | collective-permute-start | bytes 1179656 | tf_op jit(solution)/shard_map/ppermute | solution.py:273
  31.2 4.8 %collective-permute-start.6 = (bf16[1,512,384]{2,1,0:T(8,128)(2,1)S(1)}, bf16[1,512,384]{2,1,0:T(8,128)(2,1)}, u32[]{:S(2)}, u32[]{:S(2)}) collective-permute-start(bf16[1,512,384]{2,1,0:T(8,128)(2,1)S(1)} %copy-done.9), channel_id=1, source_target_pairs={{0,64},{32,96},{64,0},{96,32},{1,65},{33,97},{65,1},{97,33},{2,66}... | collective-permute-start | bytes 1179656 | tf_op jit(solution)/shard_map/ppermute | solution.py:274
  36.1 12.3 %collective-permute-start.2 = (bf16[32,2176]{1,0:T(8,128)(2,1)S(1)}, bf16[32,2176]{1,0:T(8,128)(2,1)S(1)}, u32[]{:S(2)}, u32[]{:S(2)}) collective-permute-start(bf16[32,2176]{1,0:T(8,128)(2,1)S(1)} %slice.8), channel_id=1, source_target_pairs={{0,6},{2,0},{4,2},{6,4},{1,7},{3,1},{5,3},{7,5},{8,14},{10,8},{12,... | collective-permute-start | bytes 417800 | tf_op jit(solution)/shard_map/ppermute | solution.py:23
  50.4 6.9 %collective-permute-done.2.f2.a2 = bf16[32,2176]{1,0:T(8,128)(2,1)S(1)} collective-permute-done((bf16[32,2176]{1,0:T(8,128)(2,1)S(1)}, bf16[32,2176]{1,0:T(8,128)(2,1)S(1)}, u32[]{:S(2)}, u32[]{:S(2)}) %collective-permute-start.2) | collective-permute-done | bytes 139296 | tf_op jit(solution)/shard_map/ppermute | solution.py:23
  59.7 2.9 %shard_map.103._ = bf16[32,2,16,2048]{3,2,1,0:T(8,128)(2,1)} custom-call(bf16[512,128]{1,0:T(8,128)(2,1)} %copy-done.6, bf16[64,2176]{1,0:T(8,128)(2,1)} %copy-done.2, bf16[64,2176]{1,0:T(8,128)(2,1)} %copy-done.4, bf16[32,2176]{1,0:T(8,128)(2,1)} %copy-done.5, bf16[64,2176]{1,0:T(8,128)(2,1)} %copy-done.3), custom_call_target="tpu_custom_call" | custom-call | flops 536870912 | bytes 3145728 | tf_op jit(solution)/shard_map/pallas_call | solution.py:109
  63.3 3.1 %shard_map.104 = bf16[32,2,16,2048]{3,2,1,0:T(8,128)(2,1)} custom-call(bf16[512,128]{1,0:T(8,128)(2,1)} %copy-done.6, f32[512,1]{1,0:T(8,128)} %copy-done.7, bf16[64,2176]{1,0:T(8,128)(2,1)} %copy-done.2, bf16[64,2176]{1,0:T(8,128)(2,1)} %copy-done.4, bf16[32,2176]{1,0:T(8,128)(2,1)} %copy-done.12, ...), custom_call_target="tpu_custom_call", output_to_operand_aliasing={{}: (6, {})} | custom-call | flops 536870912 | bytes 3145728 | tf_op jit(solution)/shard_map/pallas_call | solution.py:109
  66.5 60.7 %all_to_all.15.rows_hbm.x_ref.g_ref = bf16[32,2,16,2048]{3,2,1,0:T(8,128)(2,1)} all-to-all(bf16[32,2,16,2048]{3,2,1,0:T(8,128)(2,1)} %shard_map.104), channel_id=1, replica_groups=mesh['dp'=4,'y'=4,'x'=4,'z'=4,'c'=2] {'y','x','c'}, dimensions={0} | all-to-all | bytes 8388608 | tf_op jit(solution)/shard_map/all_to_all | solution.py:244
  127.2 11.1 %all-gather.2.cloned.1.call-done.weights_hbm.w_ref = bf16[2048,1152]{1,0:T(8,128)(2,1)} async-done(((bf16[512,1152]{1,0:T(8,128)(2,1)}), bf16[2048,1152]{1,0:T(8,128)(2,1)}) %all-gather.2.cloned.1.call-update) | async-done | bytes 4718608 | tf_op jit(solution)/shard_map/all_gather | solution.py:260
  138.3 7.0 %shard_map.105 = bf16[512,2048]{1,0:T(8,128)(2,1)} custom-call(bf16[32,2,16,2048]{3,2,1,0:T(8,128)(2,1)} %all_to_all.15.rows_hbm.x_ref.g_ref, bf16[2048,1152]{1,0:T(8,128)(2,1)} %all-gather.2.cloned.1.call-done.weights_hbm.w_ref), custom_call_target="tpu_custom_call" | custom-call | flops 2684354560 | bytes 10485760 | tf_op jit(solution)/shard_map/pallas_call | solution.py:160
  145.3 7.7 %all-to-all-start.1 = ((bf16[32,16,2048]{2,1,0:T(8,128)(2,1)}), bf16[32,16,2048]{2,1,0:T(8,128)(2,1)S(1)}, u32[]{:S(2)}, u32[]{:S(2)}) async-start(bf16[32,16,2048]{2,1,0:T(8,128)(2,1)} %bitcast.18), calls=%async_computation.1 | async-start | bytes 4194304 | tf_op jit(solution)/shard_map/all_to_all | solution.py:244
  153.0 8.8 %shard_map.106 = bf16[512,2048]{1,0:T(8,128)(2,1)} custom-call(bf16[32,2,16,2048]{3,2,1,0:T(8,128)(2,1)} %all_to_all.15.rows_hbm.x_ref.g_ref, bf16[32,2,16,2048]{3,2,1,0:T(8,128)(2,1)} %all_to_all.15.rows_hbm.x_ref.g_ref, bf16[2048,1152]{1,0:T(8,128)(2,1)} %all-gather.2.cloned.1.call-done.weights_hbm.w_ref), custom_call_target="tpu_custom_call" | custom-call | flops 3758096384 | bytes 10485760 | tf_op jit(solution)/shard_map/pallas_call | solution.py:200
  161.7 18.6 %all-to-all-done.1 = bf16[32,16,2048]{2,1,0:T(8,128)(2,1)S(1)} async-done(((bf16[32,16,2048]{2,1,0:T(8,128)(2,1)}), bf16[32,16,2048]{2,1,0:T(8,128)(2,1)S(1)}, u32[]{:S(2)}, u32[]{:S(2)}) %all-to-all-start.1) | async-done | bytes 2097184 | tf_op jit(solution)/shard_map/all_to_all | solution.py:244
  181.7 6.7 %all-to-all-start.2 = ((bf16[32,16,2048]{2,1,0:T(8,128)(2,1)}), bf16[32,16,2048]{2,1,0:T(8,128)(2,1)S(1)}, u32[]{:S(2)}, u32[]{:S(2)}) async-start(bf16[32,16,2048]{2,1,0:T(8,128)(2,1)} %bitcast.19), calls=%async_computation.2 | async-start | bytes 4194304 | tf_op jit(solution)/shard_map/all_to_all | solution.py:244
  189.7 3.4 %broadcast_select_fusion = bf16[1,512,2,384]{3,2,1,0:T(2,128)(2,1)} fusion(bf16[1,512,2,384]{3,2,1,0:T(2,128)(2,1)S(1)} %copy-done.8, pred[]{:T(512)S(6)} %eq.14, bf16[1,256,2,384]{3,2,1,0:T(2,128)(2,1)} %collective-permute-done.5, bf16[1,256,2,384]{3,2,1,0:T(2,128)(2,1)} %copy-done.11), kind=kLoop, calls=%fused_computation | loop fusion | flops 786432 | bytes 2359297 | tf_op jit(solution)/shard_map/jit(_where)/select_n | solution.py:292
  194.6 7.2 %collective-permute-start.7 = (bf16[32,2048]{1,0:T(8,128)(2,1)S(1)}, bf16[32,2048]{1,0:T(8,128)(2,1)S(1)}, u32[]{:S(2)}, u32[]{:S(2)}) collective-permute-start(bf16[32,2048]{1,0:T(8,128)(2,1)S(1)} %get-tuple-element.36), channel_id=1, source_target_pairs={{0,6},{2,0},{4,2},{6,4},{1,7},{3,1},{5,3},{7,5},{8,14},{10,8},{12,... | collective-permute-start | bytes 393224 | tf_op jit(solution)/shard_map/ppermute | solution.py:23
  201.8 5.1 %collective-permute-start.8 = (bf16[32,2048]{1,0:T(8,128)(2,1)S(1)}, bf16[32,2048]{1,0:T(8,128)(2,1)S(1)}, u32[]{:S(2)}, u32[]{:S(2)}) collective-permute-start(bf16[32,2048]{1,0:T(8,128)(2,1)S(1)} %get-tuple-element.37), channel_id=1, source_target_pairs={{0,4},{2,6},{4,0},{6,2},{1,5},{3,7},{5,1},{7,3},{8,12},{10,14},{12... | collective-permute-start | bytes 393224 | tf_op jit(solution)/shard_map/ppermute | solution.py:23
  206.9 6.2 %collective-permute-start.9 = (bf16[32,2048]{1,0:T(8,128)(2,1)S(1)}, bf16[32,2048]{1,0:T(8,128)(2,1)S(1)}, u32[]{:S(2)}, u32[]{:S(2)}) collective-permute-start(bf16[32,2048]{1,0:T(8,128)(2,1)S(1)} %get-tuple-element.38), channel_id=1, source_target_pairs={{0,2},{2,4},{4,6},{6,0},{1,3},{3,5},{5,7},{7,1},{8,10},{10,12},{12... | collective-permute-start | bytes 393224 | tf_op jit(solution)/shard_map/ppermute | solution.py:23
  217.0 7.5 %collective-permute-start.10 = (bf16[32,2048]{1,0:T(8,128)(2,1)S(1)}, bf16[32,2048]{1,0:T(8,128)(2,1)S(1)}, u32[]{:S(2)}, u32[]{:S(2)}) collective-permute-start(bf16[32,2048]{1,0:T(8,128)(2,1)S(1)} %get-tuple-element.42), channel_id=1, source_target_pairs={{0,6},{2,0},{4,2},{6,4},{1,7},{3,1},{5,3},{7,5},{8,14},{10,8},{12,... | collective-permute-start | bytes 393224 | tf_op jit(solution)/shard_map/ppermute | solution.py:23
  224.6 5.1 %collective-permute-start.11 = (bf16[32,2048]{1,0:T(8,128)(2,1)S(1)}, bf16[32,2048]{1,0:T(8,128)(2,1)S(1)}, u32[]{:S(2)}, u32[]{:S(2)}) collective-permute-start(bf16[32,2048]{1,0:T(8,128)(2,1)S(1)} %get-tuple-element.43), channel_id=1, source_target_pairs={{0,4},{2,6},{4,0},{6,2},{1,5},{3,7},{5,1},{7,3},{8,12},{10,14},{12... | collective-permute-start | bytes 393224 | tf_op jit(solution)/shard_map/ppermute | solution.py:23
  229.7 5.9 %collective-permute-start.12 = (bf16[32,2048]{1,0:T(8,128)(2,1)S(1)}, bf16[32,2048]{1,0:T(8,128)(2,1)S(1)}, u32[]{:S(2)}, u32[]{:S(2)}) collective-permute-start(bf16[32,2048]{1,0:T(8,128)(2,1)S(1)} %get-tuple-element.44), channel_id=1, source_target_pairs={{0,2},{2,4},{4,6},{6,0},{1,3},{3,5},{5,7},{7,1},{8,10},{10,12},{12... | collective-permute-start | bytes 393224 | tf_op jit(solution)/shard_map/ppermute | solution.py:23
  236.3 6.0 %collective-permute-done.11 = bf16[32,2048]{1,0:T(8,128)(2,1)S(1)} collective-permute-done((bf16[32,2048]{1,0:T(8,128)(2,1)S(1)}, bf16[32,2048]{1,0:T(8,128)(2,1)S(1)}, u32[]{:S(2)}, u32[]{:S(2)}) %collective-permute-start.11) | collective-permute-done | bytes 131104 | tf_op jit(solution)/shard_map/ppermute | solution.py:23
  242.3 15.4 %collective-permute-done.12 = bf16[32,2048]{1,0:T(8,128)(2,1)S(1)} collective-permute-done((bf16[32,2048]{1,0:T(8,128)(2,1)S(1)}, bf16[32,2048]{1,0:T(8,128)(2,1)S(1)}, u32[]{:S(2)}, u32[]{:S(2)}) %collective-permute-start.12) | collective-permute-done | bytes 131104 | tf_op jit(solution)/shard_map/ppermute | solution.py:23
  (72 shorter events, 21.0 us)
Async XLA Ops:
  7.2 131.1 %all-gather.2.cloned.1.call-start = ((), (), s32[]{:S(2)}) async-start(), calls=%async_computation.3 | async-start | bytes 5898240 | tf_op jit(solution)/shard_map/all_gather | solution.py:260
  8.5 14.5 %copy-start.8 = (bf16[1,512,2,384]{3,2,1,0:T(2,128)(2,1)S(1)}, bf16[1,512,2,384]{3,2,1,0:T(2,128)(2,1)}, u32[]{:S(2)}) copy-start(bf16[1,512,2,384]{3,2,1,0:T(2,128)(2,1)} %param.12) | copy-start | bytes 2359300
  10.7 20.5 %copy-start.9 = (bf16[1,512,384]{2,1,0:T(8,128)(2,1)S(1)}, bf16[1,512,384]{2,1,0:T(8,128)(2,1)}, u32[]{:S(2)}) copy-start(bf16[1,512,384]{2,1,0:T(8,128)(2,1)} %param.13) | copy-start | bytes 1179652
  11.3 48.4 %copy-start.2 = (bf16[64,2176]{1,0:T(8,128)(2,1)}, bf16[64,2176]{1,0:T(8,128)(2,1)S(1)}, u32[]{:S(2)}) copy-start(bf16[64,2176]{1,0:T(8,128)(2,1)S(1)} %pad_maximum_fusion.1.f0.a0) | copy-start | bytes 835588
  11.3 24.8 %collective-permute-start.1 = (bf16[64,2176]{1,0:T(8,128)(2,1)S(1)}, bf16[64,2176]{1,0:T(8,128)(2,1)S(1)}, u32[]{:S(2)}, u32[]{:S(2)}) collective-permute-start(bf16[64,2176]{1,0:T(8,128)(2,1)S(1)} %pad_maximum_fusion.1.f0.a0), channel_id=1, source_target_pairs={{0,6},{2,0},{4,2},{6,4},{1,7},{3,1},{5,3},{7,5},{8,14},{10,8},{12,... | collective-permute-start | bytes 835592 | tf_op jit(solution)/shard_map/ppermute | solution.py:23
  21.1 27.3 %collective-permute-start = (bf16[64,2176]{1,0:T(8,128)(2,1)S(1)}, bf16[64,2176]{1,0:T(8,128)(2,1)S(1)}, u32[]{:S(2)}, u32[]{:S(2)}) collective-permute-start(bf16[64,2176]{1,0:T(8,128)(2,1)S(1)} %pad_maximum_fusion.1.f0.a0), channel_id=1, source_target_pairs={{0,2},{2,4},{4,6},{6,0},{1,3},{3,5},{5,7},{7,1},{8,10},{10,12},{12... | collective-permute-start | bytes 835592 | tf_op jit(solution)/shard_map/ppermute | solution.py:23
  24.4 42.0 %collective-permute-start.4 = (bf16[1,256,2,384]{3,2,1,0:T(2,128)(2,1)}, bf16[1,256,2,384]{3,2,1,0:T(2,128)(2,1)S(1)}, u32[]{:S(2)}, u32[]{:S(2)}) collective-permute-start(bf16[1,256,2,384]{3,2,1,0:T(2,128)(2,1)} %get-tuple-element.49), channel_id=1, source_target_pairs={{0,64},{32,96},{64,0},{96,32},{1,65},{33,97},{65,1},{97,33},{2,66}... | collective-permute-start | bytes 1179656 | tf_op jit(solution)/shard_map/ppermute | solution.py:273
  29.2 37.2 %collective-permute-start.5 = (bf16[1,256,2,384]{3,2,1,0:T(2,128)(2,1)}, bf16[1,256,2,384]{3,2,1,0:T(2,128)(2,1)}, u32[]{:S(2)}, u32[]{:S(2)}) collective-permute-start(bf16[1,256,2,384]{3,2,1,0:T(2,128)(2,1)} %get-tuple-element.48), channel_id=1, source_target_pairs={{0,64},{32,96},{64,0},{96,32},{1,65},{33,97},{65,1},{97,33},{2,66}... | collective-permute-start | bytes 1179656 | tf_op jit(solution)/shard_map/ppermute | solution.py:273
  31.2 35.2 %collective-permute-start.6 = (bf16[1,512,384]{2,1,0:T(8,128)(2,1)S(1)}, bf16[1,512,384]{2,1,0:T(8,128)(2,1)}, u32[]{:S(2)}, u32[]{:S(2)}) collective-permute-start(bf16[1,512,384]{2,1,0:T(8,128)(2,1)S(1)} %copy-done.9), channel_id=1, source_target_pairs={{0,64},{32,96},{64,0},{96,32},{1,65},{33,97},{65,1},{97,33},{2,66}... | collective-permute-start | bytes 1179656 | tf_op jit(solution)/shard_map/ppermute | solution.py:274
  36.1 23.7 %copy-start.3 = (bf16[64,2176]{1,0:T(8,128)(2,1)}, bf16[64,2176]{1,0:T(8,128)(2,1)S(1)}, u32[]{:S(2)}) copy-start(bf16[64,2176]{1,0:T(8,128)(2,1)S(1)} %collective-permute-done.1.f3.a3) | copy-start | bytes 835588
  36.1 21.2 %collective-permute-start.2 = (bf16[32,2176]{1,0:T(8,128)(2,1)S(1)}, bf16[32,2176]{1,0:T(8,128)(2,1)S(1)}, u32[]{:S(2)}, u32[]{:S(2)}) collective-permute-start(bf16[32,2176]{1,0:T(8,128)(2,1)S(1)} %slice.8), channel_id=1, source_target_pairs={{0,6},{2,0},{4,2},{6,4},{1,7},{3,1},{5,3},{7,5},{8,14},{10,8},{12,... | collective-permute-start | bytes 417800 | tf_op jit(solution)/shard_map/ppermute | solution.py:23
  48.4 11.3 %copy-start.4 = (bf16[64,2176]{1,0:T(8,128)(2,1)}, bf16[64,2176]{1,0:T(8,128)(2,1)S(1)}, u32[]{:S(2)}) copy-start(bf16[64,2176]{1,0:T(8,128)(2,1)S(1)} %collective-permute-done.f1.a1) | copy-start | bytes 835588
  48.4 14.3 %collective-permute-start.3 = (bf16[32,2176]{1,0:T(8,128)(2,1)S(1)}, bf16[32,2176]{1,0:T(8,128)(2,1)S(1)}, u32[]{:S(2)}, u32[]{:S(2)}) collective-permute-start(bf16[32,2176]{1,0:T(8,128)(2,1)S(1)} %slice.9), channel_id=1, source_target_pairs={{0,2},{2,4},{4,6},{6,0},{1,3},{3,5},{5,7},{7,1},{8,10},{10,12},{12... | collective-permute-start | bytes 417800 | tf_op jit(solution)/shard_map/ppermute | solution.py:23
  66.4 78.8 %copy-start.11 = (bf16[1,256,2,384]{3,2,1,0:T(2,128)(2,1)}, bf16[1,256,2,384]{3,2,1,0:T(2,128)(2,1)S(1)}, u32[]{:S(2)}) copy-start(bf16[1,256,2,384]{3,2,1,0:T(2,128)(2,1)S(1)} %collective-permute-done.4) | copy-start | bytes 1179652
  145.3 35.0 %all-to-all-start.1 = ((bf16[32,16,2048]{2,1,0:T(8,128)(2,1)}), bf16[32,16,2048]{2,1,0:T(8,128)(2,1)S(1)}, u32[]{:S(2)}, u32[]{:S(2)}) async-start(bf16[32,16,2048]{2,1,0:T(8,128)(2,1)} %bitcast.18), calls=%async_computation.1 | async-start | bytes 4194304 | tf_op jit(solution)/shard_map/all_to_all | solution.py:244
  181.7 6.7 %copy-start.17 = (s32[64]{0:T(128)S(1)}, s32[64]{0:T(128)}, u32[]{:S(2)}) copy-start(s32[64]{0:T(128)} %param.11) | copy-start | bytes 772
  181.7 34.1 %all-to-all-start.2 = ((bf16[32,16,2048]{2,1,0:T(8,128)(2,1)}), bf16[32,16,2048]{2,1,0:T(8,128)(2,1)S(1)}, u32[]{:S(2)}, u32[]{:S(2)}) async-start(bf16[32,16,2048]{2,1,0:T(8,128)(2,1)} %bitcast.19), calls=%async_computation.2 | async-start | bytes 4194304 | tf_op jit(solution)/shard_map/all_to_all | solution.py:244
  189.7 23.4 %copy-start.10 = (bf16[1,512,384]{2,1,0:T(8,128)(2,1)S(1)}, bf16[1,512,384]{2,1,0:T(8,128)(2,1)}, u32[]{:S(2)}) copy-start(bf16[1,512,384]{2,1,0:T(8,128)(2,1)} %param.13) | copy-start | bytes 1179652
  194.6 35.1 %collective-permute-start.7 = (bf16[32,2048]{1,0:T(8,128)(2,1)S(1)}, bf16[32,2048]{1,0:T(8,128)(2,1)S(1)}, u32[]{:S(2)}, u32[]{:S(2)}) collective-permute-start(bf16[32,2048]{1,0:T(8,128)(2,1)S(1)} %get-tuple-element.36), channel_id=1, source_target_pairs={{0,6},{2,0},{4,2},{6,4},{1,7},{3,1},{5,3},{7,5},{8,14},{10,8},{12,... | collective-permute-start | bytes 393224 | tf_op jit(solution)/shard_map/ppermute | solution.py:23
  201.8 33.8 %collective-permute-start.8 = (bf16[32,2048]{1,0:T(8,128)(2,1)S(1)}, bf16[32,2048]{1,0:T(8,128)(2,1)S(1)}, u32[]{:S(2)}, u32[]{:S(2)}) collective-permute-start(bf16[32,2048]{1,0:T(8,128)(2,1)S(1)} %get-tuple-element.37), channel_id=1, source_target_pairs={{0,4},{2,6},{4,0},{6,2},{1,5},{3,7},{5,1},{7,3},{8,12},{10,14},{12... | collective-permute-start | bytes 393224 | tf_op jit(solution)/shard_map/ppermute | solution.py:23
  206.9 28.7 %collective-permute-start.9 = (bf16[32,2048]{1,0:T(8,128)(2,1)S(1)}, bf16[32,2048]{1,0:T(8,128)(2,1)S(1)}, u32[]{:S(2)}, u32[]{:S(2)}) collective-permute-start(bf16[32,2048]{1,0:T(8,128)(2,1)S(1)} %get-tuple-element.38), channel_id=1, source_target_pairs={{0,2},{2,4},{4,6},{6,0},{1,3},{3,5},{5,7},{7,1},{8,10},{10,12},{12... | collective-permute-start | bytes 393224 | tf_op jit(solution)/shard_map/ppermute | solution.py:23
  217.0 19.3 %collective-permute-start.10 = (bf16[32,2048]{1,0:T(8,128)(2,1)S(1)}, bf16[32,2048]{1,0:T(8,128)(2,1)S(1)}, u32[]{:S(2)}, u32[]{:S(2)}) collective-permute-start(bf16[32,2048]{1,0:T(8,128)(2,1)S(1)} %get-tuple-element.42), channel_id=1, source_target_pairs={{0,6},{2,0},{4,2},{6,4},{1,7},{3,1},{5,3},{7,5},{8,14},{10,8},{12,... | collective-permute-start | bytes 393224 | tf_op jit(solution)/shard_map/ppermute | solution.py:23
  224.6 17.7 %collective-permute-start.11 = (bf16[32,2048]{1,0:T(8,128)(2,1)S(1)}, bf16[32,2048]{1,0:T(8,128)(2,1)S(1)}, u32[]{:S(2)}, u32[]{:S(2)}) collective-permute-start(bf16[32,2048]{1,0:T(8,128)(2,1)S(1)} %get-tuple-element.43), channel_id=1, source_target_pairs={{0,4},{2,6},{4,0},{6,2},{1,5},{3,7},{5,1},{7,3},{8,12},{10,14},{12... | collective-permute-start | bytes 393224 | tf_op jit(solution)/shard_map/ppermute | solution.py:23
  229.7 28.1 %collective-permute-start.12 = (bf16[32,2048]{1,0:T(8,128)(2,1)S(1)}, bf16[32,2048]{1,0:T(8,128)(2,1)S(1)}, u32[]{:S(2)}, u32[]{:S(2)}) collective-permute-start(bf16[32,2048]{1,0:T(8,128)(2,1)S(1)} %get-tuple-element.44), channel_id=1, source_target_pairs={{0,2},{2,4},{4,6},{6,0},{1,3},{3,5},{5,7},{7,1},{8,10},{10,12},{12... | collective-permute-start | bytes 393224 | tf_op jit(solution)/shard_map/ppermute | solution.py:23
  (10 other events, 19.5 us)
Sparse Core Ops, SparseCore 0:
  10.9 127.3 all-gather.1

commit v5 on v4

--- a/solution.py
+++ b/solution.py
@@ -295,8 +295,9 @@
     results = []
     for factors, moved in (((w_high, w_low), back_out), ((back,), back_grad)):
         own, *others = combine(factors, moved)
-        for s, part in enumerate(others, 1):
-            own = own + along_z(part, -s).astype(F32)
+        came = [along_z(others[s - 1], -s) for s in (2, 1, 3)]
+        for part in came:
+            own = own + part.astype(F32)
         results.append(own.astype(BF).reshape(micro, tok, width))
     return (results[0], results[1], resident_gate, resident_down)
 

time: 266 us -> 266 us (level)
  the two profiles are of different devices: /device:TPU:103 before, /device:TPU:61 now
where the time goes in v5:
time: 266 us; the launch traced here: 265 us
  starting transfers between devices  83.1 us (31%)
  waiting for transfers between devices  64.5 us (24%)
  blocking collectives  62 us (23%)
  Pallas kernels  25.5 us (10%)
  between operations  15.1 us (6%)
  other arithmetic  8.57 us (3%)
  local copies, waits for them, and re-layouts  6.49 us (2%)
    all_to_all x1, blocking collectives, in_plane(): return lax.all_to_all(rows, PLANE, 0, 0, tiled=True)  62 us
    ppermute x10, starting transfers between devices, along_z(): lax.ppermute(value, 'z', [(i, (i + shift) % count) for i in range(count)])  55.8 us
    ppermute x10, waiting for transfers between devices, along_z(): lax.ppermute(value, 'z', [(i, (i + shift) % count) for i in range(count)])  46.7 us
    all_to_all x2, waiting for transfers between devices, in_plane(): return lax.all_to_all(rows, PLANE, 0, 0, tiled=True)  17.8 us
    all_to_all x2, starting transfers between devices, in_plane(): return lax.all_to_all(rows, PLANE, 0, 0, tiled=True)  17.6 us
    pallas_call x1, Pallas kernels, backward(): pl.pallas_call(backward_body, grid=(total // ROWS,), in_specs=[taken(0),...  8.77 us
    pallas_call x1, Pallas kernels, forward(): pl.pallas_call(forward_body, in_specs=[anywhere, anywhere], out_specs=any...  6.98 us
    ppermute x2, starting transfers between devices, local(): lax.ppermute(part, 'y', pairs)  6.78 us
  transfers between devices with their start and end apart: 16, of which 9 were waited for; matrix products, arithmetic and copies ran while one was open for 3% of the time, Pallas kernels for 7%

profile of v5, /device:TPU:61, one launch (start us, length us, event | category | flops | bytes accessed | tf_op | source)
XLA Modules:
  0.0 265.4 jit_solution(15592338365704668572)
XLA Ops:
  11.3 11.6 %collective-permute-start.1 = (bf16[64,2176]{1,0:T(8,128)(2,1)S(1)}, bf16[64,2176]{1,0:T(8,128)(2,1)S(1)}, u32[]{:S(2)}, u32[]{:S(2)}) collective-permute-start(bf16[64,2176]{1,0:T(8,128)(2,1)S(1)} %pad_maximum_fusion.1.f0.a0), channel_id=1, source_target_pairs={{0,6},{2,0},{4,2},{6,4},{1,7},{3,1},{5,3},{7,5},{8,14},{10,8},{12,... | collective-permute-start | bytes 835592 | tf_op jit(solution)/shard_map/ppermute | solution.py:23
  26.2 2.9 %collective-permute-start.4 = (bf16[1,256,2,384]{3,2,1,0:T(2,128)(2,1)}, bf16[1,256,2,384]{3,2,1,0:T(2,128)(2,1)S(1)}, u32[]{:S(2)}, u32[]{:S(2)}) collective-permute-start(bf16[1,256,2,384]{3,2,1,0:T(2,128)(2,1)} %get-tuple-element.49), channel_id=1, source_target_pairs={{0,64},{32,96},{64,0},{96,32},{1,65},{33,97},{65,1},{97,33},{2,66}... | collective-permute-start | bytes 1179656 | tf_op jit(solution)/shard_map/ppermute | solution.py:273
  29.1 3.9 %collective-permute-start.5 = (bf16[1,256,2,384]{3,2,1,0:T(2,128)(2,1)}, bf16[1,256,2,384]{3,2,1,0:T(2,128)(2,1)}, u32[]{:S(2)}, u32[]{:S(2)}) collective-permute-start(bf16[1,256,2,384]{3,2,1,0:T(2,128)(2,1)} %get-tuple-element.48), channel_id=1, source_target_pairs={{0,64},{32,96},{64,0},{96,32},{1,65},{33,97},{65,1},{97,33},{2,66}... | collective-permute-start | bytes 1179656 | tf_op jit(solution)/shard_map/ppermute | solution.py:273
  33.0 2.9 %collective-permute-start.6 = (bf16[1,512,384]{2,1,0:T(8,128)(2,1)S(1)}, bf16[1,512,384]{2,1,0:T(8,128)(2,1)}, u32[]{:S(2)}, u32[]{:S(2)}) collective-permute-start(bf16[1,512,384]{2,1,0:T(8,128)(2,1)S(1)} %copy-done.9), channel_id=1, source_target_pairs={{0,64},{32,96},{64,0},{96,32},{1,65},{33,97},{65,1},{97,33},{2,66}... | collective-permute-start | bytes 1179656 | tf_op jit(solution)/shard_map/ppermute | solution.py:274
  35.9 13.7 %collective-permute-done.1.f3.a3 = bf16[64,2176]{1,0:T(8,128)(2,1)S(1)} collective-permute-done((bf16[64,2176]{1,0:T(8,128)(2,1)S(1)}, bf16[64,2176]{1,0:T(8,128)(2,1)S(1)}, u32[]{:S(2)}, u32[]{:S(2)}) %collective-permute-start.1) | collective-permute-done | bytes 278560 | tf_op jit(solution)/shard_map/ppermute | solution.py:23
  49.6 9.0 %collective-permute-start.2 = (bf16[32,2176]{1,0:T(8,128)(2,1)S(1)}, bf16[32,2176]{1,0:T(8,128)(2,1)S(1)}, u32[]{:S(2)}, u32[]{:S(2)}) collective-permute-start(bf16[32,2176]{1,0:T(8,128)(2,1)S(1)} %slice.8), channel_id=1, source_target_pairs={{0,6},{2,0},{4,2},{6,4},{1,7},{3,1},{5,3},{7,5},{8,14},{10,8},{12,... | collective-permute-start | bytes 417800 | tf_op jit(solution)/shard_map/ppermute | solution.py:23
  58.6 3.0 %collective-permute-done.f1.a1 = bf16[64,2176]{1,0:T(8,128)(2,1)S(1)} collective-permute-done((bf16[64,2176]{1,0:T(8,128)(2,1)S(1)}, bf16[64,2176]{1,0:T(8,128)(2,1)S(1)}, u32[]{:S(2)}, u32[]{:S(2)}) %collective-permute-start) | collective-permute-done | bytes 278560 | tf_op jit(solution)/shard_map/ppermute | solution.py:23
  63.5 8.0 %collective-permute-done.2.f2.a2 = bf16[32,2176]{1,0:T(8,128)(2,1)S(1)} collective-permute-done((bf16[32,2176]{1,0:T(8,128)(2,1)S(1)}, bf16[32,2176]{1,0:T(8,128)(2,1)S(1)}, u32[]{:S(2)}, u32[]{:S(2)}) %collective-permute-start.2) | collective-permute-done | bytes 139296 | tf_op jit(solution)/shard_map/ppermute | solution.py:23
  73.9 2.9 %shard_map.103._ = bf16[32,2,16,2048]{3,2,1,0:T(8,128)(2,1)} custom-call(bf16[512,128]{1,0:T(8,128)(2,1)} %copy-done.6, bf16[64,2176]{1,0:T(8,128)(2,1)} %copy-done.2, bf16[64,2176]{1,0:T(8,128)(2,1)} %copy-done.4, bf16[32,2176]{1,0:T(8,128)(2,1)} %copy-done.5, bf16[64,2176]{1,0:T(8,128)(2,1)} %copy-done.3), custom_call_target="tpu_custom_call" | custom-call | flops 536870912 | bytes 3145728 | tf_op jit(solution)/shard_map/pallas_call | solution.py:109
  76.9 4.8 %collective-permute-done.3.a2 = bf16[32,2176]{1,0:T(8,128)(2,1)S(1)} collective-permute-done((bf16[32,2176]{1,0:T(8,128)(2,1)S(1)}, bf16[32,2176]{1,0:T(8,128)(2,1)S(1)}, u32[]{:S(2)}, u32[]{:S(2)}) %collective-permute-start.3) | collective-permute-done | bytes 139296 | tf_op jit(solution)/shard_map/ppermute | solution.py:23
  82.4 3.1 %shard_map.104 = bf16[32,2,16,2048]{3,2,1,0:T(8,128)(2,1)} custom-call(bf16[512,128]{1,0:T(8,128)(2,1)} %copy-done.6, f32[512,1]{1,0:T(8,128)} %copy-done.7, bf16[64,2176]{1,0:T(8,128)(2,1)} %copy-done.2, bf16[64,2176]{1,0:T(8,128)(2,1)} %copy-done.4, bf16[32,2176]{1,0:T(8,128)(2,1)} %copy-done.12, ...), custom_call_target="tpu_custom_call", output_to_operand_aliasing={{}: (6, {})} | custom-call | flops 536870912 | bytes 3145728 | tf_op jit(solution)/shard_map/pallas_call | solution.py:109
  85.5 62.0 %all_to_all.15.rows_hbm.x_ref.g_ref = bf16[32,2,16,2048]{3,2,1,0:T(8,128)(2,1)} all-to-all(bf16[32,2,16,2048]{3,2,1,0:T(8,128)(2,1)} %shard_map.104), channel_id=1, replica_groups=mesh['dp'=4,'y'=4,'x'=4,'z'=4,'c'=2] {'y','x','c'}, dimensions={0} | all-to-all | bytes 8388608 | tf_op jit(solution)/shard_map/all_to_all | solution.py:244
  147.5 7.0 %shard_map.105 = bf16[512,2048]{1,0:T(8,128)(2,1)} custom-call(bf16[32,2,16,2048]{3,2,1,0:T(8,128)(2,1)} %all_to_all.15.rows_hbm.x_ref.g_ref, bf16[2048,1152]{1,0:T(8,128)(2,1)} %all-gather.2.cloned.1.call-done.weights_hbm.w_ref), custom_call_target="tpu_custom_call" | custom-call | flops 2684354560 | bytes 10485760 | tf_op jit(solution)/shard_map/pallas_call | solution.py:160
  154.5 8.1 %all-to-all-start.1 = ((bf16[32,16,2048]{2,1,0:T(8,128)(2,1)}), bf16[32,16,2048]{2,1,0:T(8,128)(2,1)S(1)}, u32[]{:S(2)}, u32[]{:S(2)}) async-start(bf16[32,16,2048]{2,1,0:T(8,128)(2,1)} %bitcast.18), calls=%async_computation.1 | async-start | bytes 4194304 | tf_op jit(solution)/shard_map/all_to_all | solution.py:244
  162.6 8.8 %shard_map.106 = bf16[512,2048]{1,0:T(8,128)(2,1)} custom-call(bf16[32,2,16,2048]{3,2,1,0:T(8,128)(2,1)} %all_to_all.15.rows_hbm.x_ref.g_ref, bf16[32,2,16,2048]{3,2,1,0:T(8,128)(2,1)} %all_to_all.15.rows_hbm.x_ref.g_ref, bf16[2048,1152]{1,0:T(8,128)(2,1)} %all-gather.2.cloned.1.call-done.weights_hbm.w_ref), custom_call_target="tpu_custom_call" | custom-call | flops 3758096384 | bytes 10485760 | tf_op jit(solution)/shard_map/pallas_call | solution.py:200
  171.3 15.8 %all-to-all-done.1 = bf16[32,16,2048]{2,1,0:T(8,128)(2,1)S(1)} async-done(((bf16[32,16,2048]{2,1,0:T(8,128)(2,1)}), bf16[32,16,2048]{2,1,0:T(8,128)(2,1)S(1)}, u32[]{:S(2)}, u32[]{:S(2)}) %all-to-all-start.1) | async-done | bytes 2097184 | tf_op jit(solution)/shard_map/all_to_all | solution.py:244
  188.5 9.6 %all-to-all-start.2 = ((bf16[32,16,2048]{2,1,0:T(8,128)(2,1)}), bf16[32,16,2048]{2,1,0:T(8,128)(2,1)S(1)}, u32[]{:S(2)}, u32[]{:S(2)}) async-start(bf16[32,16,2048]{2,1,0:T(8,128)(2,1)} %bitcast.19), calls=%async_computation.2 | async-start | bytes 4194304 | tf_op jit(solution)/shard_map/all_to_all | solution.py:244
  199.4 3.4 %broadcast_select_fusion = bf16[1,512,2,384]{3,2,1,0:T(2,128)(2,1)} fusion(bf16[1,512,2,384]{3,2,1,0:T(2,128)(2,1)S(1)} %copy-done.8, pred[]{:T(512)S(6)} %eq.14, bf16[1,256,2,384]{3,2,1,0:T(2,128)(2,1)} %collective-permute-done.5, bf16[1,256,2,384]{3,2,1,0:T(2,128)(2,1)} %copy-done.11), kind=kLoop, calls=%fused_computation | loop fusion | flops 786432 | bytes 2359297 | tf_op jit(solution)/shard_map/jit(_where)/select_n | solution.py:292
  204.3 6.5 %collective-permute-start.7 = (bf16[32,2048]{1,0:T(8,128)(2,1)S(1)}, bf16[32,2048]{1,0:T(8,128)(2,1)S(1)}, u32[]{:S(2)}, u32[]{:S(2)}) collective-permute-start(bf16[32,2048]{1,0:T(8,128)(2,1)S(1)} %get-tuple-element.36), channel_id=1, source_target_pairs={{0,4},{2,6},{4,0},{6,2},{1,5},{3,7},{5,1},{7,3},{8,12},{10,14},{12... | collective-permute-start | bytes 393224 | tf_op jit(solution)/shard_map/ppermute | solution.py:23
  212.7 7.3 %collective-permute-start.9 = (bf16[32,2048]{1,0:T(8,128)(2,1)S(1)}, bf16[32,2048]{1,0:T(8,128)(2,1)S(1)}, u32[]{:S(2)}, u32[]{:S(2)}) collective-permute-start(bf16[32,2048]{1,0:T(8,128)(2,1)S(1)} %get-tuple-element.38), channel_id=1, source_target_pairs={{0,2},{2,4},{4,6},{6,0},{1,3},{3,5},{5,7},{7,1},{8,10},{10,12},{12... | collective-permute-start | bytes 393224 | tf_op jit(solution)/shard_map/ppermute | solution.py:23
  224.1 6.5 %collective-permute-start.10 = (bf16[32,2048]{1,0:T(8,128)(2,1)S(1)}, bf16[32,2048]{1,0:T(8,128)(2,1)S(1)}, u32[]{:S(2)}, u32[]{:S(2)}) collective-permute-start(bf16[32,2048]{1,0:T(8,128)(2,1)S(1)} %get-tuple-element.42), channel_id=1, source_target_pairs={{0,4},{2,6},{4,0},{6,2},{1,5},{3,7},{5,1},{7,3},{8,12},{10,14},{12... | collective-permute-start | bytes 393224 | tf_op jit(solution)/shard_map/ppermute | solution.py:23
  230.6 5.0 %collective-permute-start.11 = (bf16[32,2048]{1,0:T(8,128)(2,1)S(1)}, bf16[32,2048]{1,0:T(8,128)(2,1)S(1)}, u32[]{:S(2)}, u32[]{:S(2)}) collective-permute-start(bf16[32,2048]{1,0:T(8,128)(2,1)S(1)} %get-tuple-element.43), channel_id=1, source_target_pairs={{0,6},{2,0},{4,2},{6,4},{1,7},{3,1},{5,3},{7,5},{8,14},{10,8},{12,... | collective-permute-start | bytes 393224 | tf_op jit(solution)/shard_map/ppermute | solution.py:23
  235.7 4.1 %collective-permute-start.12 = (bf16[32,2048]{1,0:T(8,128)(2,1)S(1)}, bf16[32,2048]{1,0:T(8,128)(2,1)S(1)}, u32[]{:S(2)}, u32[]{:S(2)}) collective-permute-start(bf16[32,2048]{1,0:T(8,128)(2,1)S(1)} %get-tuple-element.44), channel_id=1, source_target_pairs={{0,2},{2,4},{4,6},{6,0},{1,3},{3,5},{5,7},{7,1},{8,10},{10,12},{12... | collective-permute-start | bytes 393224 | tf_op jit(solution)/shard_map/ppermute | solution.py:23
  240.6 12.4 %collective-permute-done.10 = bf16[32,2048]{1,0:T(8,128)(2,1)S(1)} collective-permute-done((bf16[32,2048]{1,0:T(8,128)(2,1)S(1)}, bf16[32,2048]{1,0:T(8,128)(2,1)S(1)}, u32[]{:S(2)}, u32[]{:S(2)}) %collective-permute-start.10) | collective-permute-done | bytes 131104 | tf_op jit(solution)/shard_map/ppermute | solution.py:23
  (72 shorter events, 28.1 us)
Async XLA Ops:
  7.2 140.3 %all-gather.2.cloned.1.call-start = ((), (), s32[]{:S(2)}) async-start(), calls=%async_computation.3 | async-start | bytes 5898240 | tf_op jit(solution)/shard_map/all_gather | solution.py:260
  8.5 16.3 %copy-start.8 = (bf16[1,512,2,384]{3,2,1,0:T(2,128)(2,1)S(1)}, bf16[1,512,2,384]{3,2,1,0:T(2,128)(2,1)}, u32[]{:S(2)}) copy-start(bf16[1,512,2,384]{3,2,1,0:T(2,128)(2,1)} %param.12) | copy-start | bytes 2359300
  10.7 22.3 %copy-start.9 = (bf16[1,512,384]{2,1,0:T(8,128)(2,1)S(1)}, bf16[1,512,384]{2,1,0:T(8,128)(2,1)}, u32[]{:S(2)}) copy-start(bf16[1,512,384]{2,1,0:T(8,128)(2,1)} %param.13) | copy-start | bytes 1179652
  11.3 62.6 %copy-start.2 = (bf16[64,2176]{1,0:T(8,128)(2,1)}, bf16[64,2176]{1,0:T(8,128)(2,1)S(1)}, u32[]{:S(2)}) copy-start(bf16[64,2176]{1,0:T(8,128)(2,1)S(1)} %pad_maximum_fusion.1.f0.a0) | copy-start | bytes 835588
  11.3 38.2 %collective-permute-start.1 = (bf16[64,2176]{1,0:T(8,128)(2,1)S(1)}, bf16[64,2176]{1,0:T(8,128)(2,1)S(1)}, u32[]{:S(2)}, u32[]{:S(2)}) collective-permute-start(bf16[64,2176]{1,0:T(8,128)(2,1)S(1)} %pad_maximum_fusion.1.f0.a0), channel_id=1, source_target_pairs={{0,6},{2,0},{4,2},{6,4},{1,7},{3,1},{5,3},{7,5},{8,14},{10,8},{12,... | collective-permute-start | bytes 835592 | tf_op jit(solution)/shard_map/ppermute | solution.py:23
  22.9 38.7 %collective-permute-start = (bf16[64,2176]{1,0:T(8,128)(2,1)S(1)}, bf16[64,2176]{1,0:T(8,128)(2,1)S(1)}, u32[]{:S(2)}, u32[]{:S(2)}) collective-permute-start(bf16[64,2176]{1,0:T(8,128)(2,1)S(1)} %pad_maximum_fusion.1.f0.a0), channel_id=1, source_target_pairs={{0,2},{2,4},{4,6},{6,0},{1,3},{3,5},{5,7},{7,1},{8,10},{10,12},{12... | collective-permute-start | bytes 835592 | tf_op jit(solution)/shard_map/ppermute | solution.py:23
  26.2 59.2 %collective-permute-start.4 = (bf16[1,256,2,384]{3,2,1,0:T(2,128)(2,1)}, bf16[1,256,2,384]{3,2,1,0:T(2,128)(2,1)S(1)}, u32[]{:S(2)}, u32[]{:S(2)}) collective-permute-start(bf16[1,256,2,384]{3,2,1,0:T(2,128)(2,1)} %get-tuple-element.49), channel_id=1, source_target_pairs={{0,64},{32,96},{64,0},{96,32},{1,65},{33,97},{65,1},{97,33},{2,66}... | collective-permute-start | bytes 1179656 | tf_op jit(solution)/shard_map/ppermute | solution.py:273
  29.1 56.4 %collective-permute-start.5 = (bf16[1,256,2,384]{3,2,1,0:T(2,128)(2,1)}, bf16[1,256,2,384]{3,2,1,0:T(2,128)(2,1)}, u32[]{:S(2)}, u32[]{:S(2)}) collective-permute-start(bf16[1,256,2,384]{3,2,1,0:T(2,128)(2,1)} %get-tuple-element.48), channel_id=1, source_target_pairs={{0,64},{32,96},{64,0},{96,32},{1,65},{33,97},{65,1},{97,33},{2,66}... | collective-permute-start | bytes 1179656 | tf_op jit(solution)/shard_map/ppermute | solution.py:273
  33.0 52.4 %collective-permute-start.6 = (bf16[1,512,384]{2,1,0:T(8,128)(2,1)S(1)}, bf16[1,512,384]{2,1,0:T(8,128)(2,1)}, u32[]{:S(2)}, u32[]{:S(2)}) collective-permute-start(bf16[1,512,384]{2,1,0:T(8,128)(2,1)S(1)} %copy-done.9), channel_id=1, source_target_pairs={{0,64},{32,96},{64,0},{96,32},{1,65},{33,97},{65,1},{97,33},{2,66}... | collective-permute-start | bytes 1179656 | tf_op jit(solution)/shard_map/ppermute | solution.py:274
  49.5 24.4 %copy-start.3 = (bf16[64,2176]{1,0:T(8,128)(2,1)}, bf16[64,2176]{1,0:T(8,128)(2,1)S(1)}, u32[]{:S(2)}) copy-start(bf16[64,2176]{1,0:T(8,128)(2,1)S(1)} %collective-permute-done.1.f3.a3) | copy-start | bytes 835588
  49.6 21.9 %collective-permute-start.2 = (bf16[32,2176]{1,0:T(8,128)(2,1)S(1)}, bf16[32,2176]{1,0:T(8,128)(2,1)S(1)}, u32[]{:S(2)}, u32[]{:S(2)}) collective-permute-start(bf16[32,2176]{1,0:T(8,128)(2,1)S(1)} %slice.8), channel_id=1, source_target_pairs={{0,6},{2,0},{4,2},{6,4},{1,7},{3,1},{5,3},{7,5},{8,14},{10,8},{12,... | collective-permute-start | bytes 417800 | tf_op jit(solution)/shard_map/ppermute | solution.py:23
  61.5 12.4 %copy-start.4 = (bf16[64,2176]{1,0:T(8,128)(2,1)}, bf16[64,2176]{1,0:T(8,128)(2,1)S(1)}, u32[]{:S(2)}) copy-start(bf16[64,2176]{1,0:T(8,128)(2,1)S(1)} %collective-permute-done.f1.a1) | copy-start | bytes 835588
  61.5 20.2 %collective-permute-start.3 = (bf16[32,2176]{1,0:T(8,128)(2,1)S(1)}, bf16[32,2176]{1,0:T(8,128)(2,1)S(1)}, u32[]{:S(2)}, u32[]{:S(2)}) collective-permute-start(bf16[32,2176]{1,0:T(8,128)(2,1)S(1)} %slice.9), channel_id=1, source_target_pairs={{0,2},{2,4},{4,6},{6,0},{1,3},{3,5},{5,7},{7,1},{8,10},{10,12},{12... | collective-permute-start | bytes 417800 | tf_op jit(solution)/shard_map/ppermute | solution.py:23
  85.4 69.0 %copy-start.11 = (bf16[1,256,2,384]{3,2,1,0:T(2,128)(2,1)}, bf16[1,256,2,384]{3,2,1,0:T(2,128)(2,1)S(1)}, u32[]{:S(2)}) copy-start(bf16[1,256,2,384]{3,2,1,0:T(2,128)(2,1)S(1)} %collective-permute-done.4) | copy-start | bytes 1179652
  154.5 32.6 %all-to-all-start.1 = ((bf16[32,16,2048]{2,1,0:T(8,128)(2,1)}), bf16[32,16,2048]{2,1,0:T(8,128)(2,1)S(1)}, u32[]{:S(2)}, u32[]{:S(2)}) async-start(bf16[32,16,2048]{2,1,0:T(8,128)(2,1)} %bitcast.18), calls=%async_computation.1 | async-start | bytes 4194304 | tf_op jit(solution)/shard_map/all_to_all | solution.py:244
  188.5 9.6 %copy-start.17 = (s32[64]{0:T(128)S(1)}, s32[64]{0:T(128)}, u32[]{:S(2)}) copy-start(s32[64]{0:T(128)} %param.11) | copy-start | bytes 772
  188.5 34.4 %all-to-all-start.2 = ((bf16[32,16,2048]{2,1,0:T(8,128)(2,1)}), bf16[32,16,2048]{2,1,0:T(8,128)(2,1)S(1)}, u32[]{:S(2)}, u32[]{:S(2)}) async-start(bf16[32,16,2048]{2,1,0:T(8,128)(2,1)} %bitcast.19), calls=%async_computation.2 | async-start | bytes 4194304 | tf_op jit(solution)/shard_map/all_to_all | solution.py:244
  199.4 20.6 %copy-start.10 = (bf16[1,512,384]{2,1,0:T(8,128)(2,1)S(1)}, bf16[1,512,384]{2,1,0:T(8,128)(2,1)}, u32[]{:S(2)}) copy-start(bf16[1,512,384]{2,1,0:T(8,128)(2,1)} %param.13) | copy-start | bytes 1179652
  204.3 31.4 %collective-permute-start.7 = (bf16[32,2048]{1,0:T(8,128)(2,1)S(1)}, bf16[32,2048]{1,0:T(8,128)(2,1)S(1)}, u32[]{:S(2)}, u32[]{:S(2)}) collective-permute-start(bf16[32,2048]{1,0:T(8,128)(2,1)S(1)} %get-tuple-element.36), channel_id=1, source_target_pairs={{0,4},{2,6},{4,0},{6,2},{1,5},{3,7},{5,1},{7,3},{8,12},{10,14},{12... | collective-permute-start | bytes 393224 | tf_op jit(solution)/shard_map/ppermute | solution.py:23
  210.8 29.0 %collective-permute-start.8 = (bf16[32,2048]{1,0:T(8,128)(2,1)S(1)}, bf16[32,2048]{1,0:T(8,128)(2,1)S(1)}, u32[]{:S(2)}, u32[]{:S(2)}) collective-permute-start(bf16[32,2048]{1,0:T(8,128)(2,1)S(1)} %get-tuple-element.37), channel_id=1, source_target_pairs={{0,6},{2,0},{4,2},{6,4},{1,7},{3,1},{5,3},{7,5},{8,14},{10,8},{12,... | collective-permute-start | bytes 393224 | tf_op jit(solution)/shard_map/ppermute | solution.py:23
  212.7 27.1 %collective-permute-start.9 = (bf16[32,2048]{1,0:T(8,128)(2,1)S(1)}, bf16[32,2048]{1,0:T(8,128)(2,1)S(1)}, u32[]{:S(2)}, u32[]{:S(2)}) collective-permute-start(bf16[32,2048]{1,0:T(8,128)(2,1)S(1)} %get-tuple-element.38), channel_id=1, source_target_pairs={{0,2},{2,4},{4,6},{6,0},{1,3},{3,5},{5,7},{7,1},{8,10},{10,12},{12... | collective-permute-start | bytes 393224 | tf_op jit(solution)/shard_map/ppermute | solution.py:23
  224.1 28.9 %collective-permute-start.10 = (bf16[32,2048]{1,0:T(8,128)(2,1)S(1)}, bf16[32,2048]{1,0:T(8,128)(2,1)S(1)}, u32[]{:S(2)}, u32[]{:S(2)}) collective-permute-start(bf16[32,2048]{1,0:T(8,128)(2,1)S(1)} %get-tuple-element.42), channel_id=1, source_target_pairs={{0,4},{2,6},{4,0},{6,2},{1,5},{3,7},{5,1},{7,3},{8,12},{10,14},{12... | collective-permute-start | bytes 393224 | tf_op jit(solution)/shard_map/ppermute | solution.py:23
  230.6 25.1 %collective-permute-start.11 = (bf16[32,2048]{1,0:T(8,128)(2,1)S(1)}, bf16[32,2048]{1,0:T(8,128)(2,1)S(1)}, u32[]{:S(2)}, u32[]{:S(2)}) collective-permute-start(bf16[32,2048]{1,0:T(8,128)(2,1)S(1)} %get-tuple-element.43), channel_id=1, source_target_pairs={{0,6},{2,0},{4,2},{6,4},{1,7},{3,1},{5,3},{7,5},{8,14},{10,8},{12,... | collective-permute-start | bytes 393224 | tf_op jit(solution)/shard_map/ppermute | solution.py:23
  235.7 22.2 %collective-permute-start.12 = (bf16[32,2048]{1,0:T(8,128)(2,1)S(1)}, bf16[32,2048]{1,0:T(8,128)(2,1)S(1)}, u32[]{:S(2)}, u32[]{:S(2)}) collective-permute-start(bf16[32,2048]{1,0:T(8,128)(2,1)S(1)} %get-tuple-element.44), channel_id=1, source_target_pairs={{0,2},{2,4},{4,6},{6,0},{1,3},{3,5},{5,7},{7,1},{8,10},{10,12},{12... | collective-permute-start | bytes 393224 | tf_op jit(solution)/shard_map/ppermute | solution.py:23
  (10 other events, 19.5 us)
Sparse Core Ops, SparseCore 0:
  10.9 125.1 all-gather.1

commit v6 on v5

--- a/solution.py
+++ b/solution.py
@@ -59,7 +59,7 @@
 
 
 def route(place, mine, up, far, down, slots):
-    tokens = mine.shape[0] // 2
+    tokens = mine.shape[0]
     n = tokens * 4
     last = mine.shape[1] // MORE - 1
     facts = pl.BlockSpec((tokens, MORE), lambda i: (0, last))
@@ -91,21 +91,19 @@
     rows_ref[...] = (rows * scale_ref[...]).astype(BF).reshape(rows_ref.shape)
 
 
-def select(pick, mine, up, far, down, plane, scale=None, rows=None):
+def select(pick, column, width, plane, scale=None, rows=None):
     slots, n = pick.shape
-    part, width = n // 4, mine.shape[1] - MORE
+    part = n // 4
     which = 0 if rows is None else 1
     step = 2 * STEP
-    near = pl.BlockSpec((part, step), lambda j: (which, j))
-    distant = pl.BlockSpec((part, step), lambda j: (0, j))
     whole = pl.BlockSpec((slots, n), lambda j: (0, 0))
-    specs = [near, near, distant, near]
+    specs = [pl.BlockSpec((part, step), lambda j: (0, j))] * 4
     if which:
         specs = [whole, pl.BlockSpec((slots, 1), lambda j: (0, 0)), *specs, pl.BlockSpec(memory_space=pl.ANY)]
-        operands = (pick, scale, mine, up, far, down, rows)
+        operands = (pick, scale, *column, rows)
     else:
         specs = [whole, *specs]
-        operands = (pick, mine, up, far, down)
+        operands = (pick, *column)
     return pl.pallas_call(
         select_grads_body if which else select_tokens_body,
         grid=(width // step,),
@@ -266,20 +264,20 @@
     middle = lax.reduce_precision(route_prob - high, 8, 7)
     low = route_prob - high - middle
     facts = jnp.concatenate([expert_ids.astype(F32), high, middle, low], axis=2).astype(BF)
-    facts = jnp.pad(facts.reshape(micro * tok, 4 * top), ((0, micro * tok), (0, MORE - 4 * top)))
-    mine = jnp.concatenate([hidden_in, cotangent], axis=0).reshape(2 * micro * tok, width)
-    mine = jnp.concatenate([mine, facts], axis=1)
+    facts = jnp.pad(facts.reshape(micro * tok, 4 * top), ((0, 0), (0, MORE - 4 * top)))
+    mine = jnp.concatenate([hidden_in.reshape(micro * tok, width), facts], axis=1)
+    mine_g = cotangent.reshape(micro * tok, width)
     gate_own, down_own, mine = lax.optimization_barrier((gate_up, down_t, mine))
     other_gate = [lax.ppermute(part, "y", pairs) for part in jnp.split(gate_own, 2, axis=1)]
     other_down = lax.ppermute(down_own, "y", pairs)
-    up, down = along_z(mine, 1), along_z(mine, -1)
-    split = micro * tok
-    far = (along_z(down[:split], -1), along_z(up[split:], 1))
+    down, up = along_z(mine, -1), along_z(mine, 1)
+    up_g, down_g = along_z(mine_g, 1), along_z(mine_g, -1)
+    far, far_g = along_z(down, -1), along_z(up_g, 1)
 
     place = jnp.full((1,), my_z, jnp.int32)
-    pick, scale, back, w_high, w_low = route(place, mine, up, far[0], down, plane * count)
-    rows = select(pick, mine, up, far[0], down, plane)
-    rows = select(pick, mine, up, far[1], down, plane, scale, rows)
+    pick, scale, back, w_high, w_low = route(place, mine, up, far, down, plane * count)
+    rows = select(pick, (mine, up, far, down), width, plane)
+    rows = select(pick, (mine_g, up_g, far_g, down_g), width, plane, scale, rows)
     rows, other_gate, other_down = lax.optimization_barrier((rows, other_gate, other_down))
     other_gate = jnp.concatenate(other_gate, axis=1)
     rows = in_plane(rows)

time: 266 us -> 272 us (1.023)
  the two profiles are of different devices: /device:TPU:61 before, /device:TPU:55 now
where the time goes in v6:
time: 272 us; the launch traced here: 271 us
  starting transfers between devices  95.6 us (35%)
  waiting for transfers between devices  64.3 us (24%)
  blocking collectives  55.9 us (21%)
  Pallas kernels  25.5 us (9%)
  between operations  15.1 us (6%)
  other arithmetic  8.56 us (3%)
  local copies, waits for them, and re-layouts  6.46 us (2%)
    ppermute x12, starting transfers between devices, along_z(): lax.ppermute(value, 'z', [(i, (i + shift) % count) for i in range(count)])  69.7 us
    all_to_all x1, blocking collectives, in_plane(): return lax.all_to_all(rows, PLANE, 0, 0, tiled=True)  55.9 us
    ppermute x12, waiting for transfers between devices, along_z(): lax.ppermute(value, 'z', [(i, (i + shift) % count) for i in range(count)])  48.1 us
    all_to_all x2, starting transfers between devices, in_plane(): return lax.all_to_all(rows, PLANE, 0, 0, tiled=True)  17.1 us
    all_to_all x2, waiting for transfers between devices, in_plane(): return lax.all_to_all(rows, PLANE, 0, 0, tiled=True)  16.2 us
    pallas_call x1, Pallas kernels, backward(): pl.pallas_call(backward_body, grid=(total // ROWS,), in_specs=[taken(0),...  8.78 us
    pallas_call x1, Pallas kernels, forward(): pl.pallas_call(forward_body, in_specs=[anywhere, anywhere], out_specs=any...  6.92 us
    ppermute x2, starting transfers between devices, local(): lax.ppermute(part, 'y', pairs)  6.77 us
  transfers between devices with their start and end apart: 18, of which 9 were waited for; matrix products, arithmetic and copies ran while one was open for 3% of the time, Pallas kernels for 7%

profile of v6, /device:TPU:55, one launch (start us, length us, event | category | flops | bytes accessed | tf_op | source)
XLA Modules:
  0.0 271.4 jit_solution(7420960437283832334)
XLA Ops:
  11.3 11.6 %collective-permute-start.1 = (bf16[32,2176]{1,0:T(8,128)(2,1)S(1)}, bf16[32,2176]{1,0:T(8,128)(2,1)S(1)}, u32[]{:S(2)}, u32[]{:S(2)}) collective-permute-start(bf16[32,2176]{1,0:T(8,128)(2,1)S(1)} %pad_maximum_fusion.1.f0.a0), channel_id=1, source_target_pairs={{0,6},{2,0},{4,2},{6,4},{1,7},{3,1},{5,3},{7,5},{8,14},{10,8},{12,... | collective-permute-start | bytes 417800 | tf_op jit(solution)/shard_map/ppermute | solution.py:23
  28.1 4.8 %collective-permute-start.7 = (bf16[1,256,2,384]{3,2,1,0:T(2,128)(2,1)}, bf16[1,256,2,384]{3,2,1,0:T(2,128)(2,1)S(1)}, u32[]{:S(2)}, u32[]{:S(2)}) collective-permute-start(bf16[1,256,2,384]{3,2,1,0:T(2,128)(2,1)} %get-tuple-element.48), channel_id=1, source_target_pairs={{0,64},{32,96},{64,0},{96,32},{1,65},{33,97},{65,1},{97,33},{2,66}... | collective-permute-start | bytes 1179656 | tf_op jit(solution)/shard_map/ppermute | solution.py:271
  35.0 3.6 %collective-permute-done.3.a1 = bf16[32,2048]{1,0:T(8,128)(2,1)S(1)} collective-permute-done((bf16[32,2048]{1,0:T(8,128)(2,1)S(1)}, bf16[32,2048]{1,0:T(8,128)(2,1)S(1)}, u32[]{:S(2)}, u32[]{:S(2)}) %collective-permute-start.3) | collective-permute-done | bytes 131104 | tf_op jit(solution)/shard_map/ppermute | solution.py:23
  40.6 7.3 %collective-permute-start.2 = (bf16[32,2176]{1,0:T(8,128)(2,1)S(1)}, bf16[32,2176]{1,0:T(8,128)(2,1)S(1)}, u32[]{:S(2)}, u32[]{:S(2)}) collective-permute-start(bf16[32,2176]{1,0:T(8,128)(2,1)S(1)} %collective-permute-done.1.f3.a3), channel_id=1, source_target_pairs={{0,6},{2,0},{4,2},{6,4},{1,7},{3,1},{5,3},{7,5},{8,14},{10,8},{12,... | collective-permute-start | bytes 417800 | tf_op jit(solution)/shard_map/ppermute | solution.py:23
  47.8 14.7 %collective-permute-done.f1.a1 = bf16[32,2176]{1,0:T(8,128)(2,1)S(1)} collective-permute-done((bf16[32,2176]{1,0:T(8,128)(2,1)S(1)}, bf16[32,2176]{1,0:T(8,128)(2,1)S(1)}, u32[]{:S(2)}, u32[]{:S(2)}) %collective-permute-start) | collective-permute-done | bytes 139296 | tf_op jit(solution)/shard_map/ppermute | solution.py:23
  62.5 6.5 %collective-permute-start.5 = (bf16[32,2048]{1,0:T(8,128)(2,1)S(1)}, bf16[32,2048]{1,0:T(8,128)(2,1)S(1)}, u32[]{:S(2)}, u32[]{:S(2)}) collective-permute-start(bf16[32,2048]{1,0:T(8,128)(2,1)S(1)} %bitcast.26), channel_id=1, source_target_pairs={{0,6},{2,0},{4,2},{6,4},{1,7},{3,1},{5,3},{7,5},{8,14},{10,8},{12,... | collective-permute-start | bytes 393224 | tf_op jit(solution)/shard_map/ppermute | solution.py:23
  69.0 6.0 %collective-permute-done.2.f2.a2 = bf16[32,2176]{1,0:T(8,128)(2,1)S(1)} collective-permute-done((bf16[32,2176]{1,0:T(8,128)(2,1)S(1)}, bf16[32,2176]{1,0:T(8,128)(2,1)S(1)}, u32[]{:S(2)}, u32[]{:S(2)}) %collective-permute-start.2) | collective-permute-done | bytes 139296 | tf_op jit(solution)/shard_map/ppermute | solution.py:23
  75.0 3.6 %collective-permute-start.4 = (bf16[32,2048]{1,0:T(8,128)(2,1)S(1)}, bf16[32,2048]{1,0:T(8,128)(2,1)S(1)}, u32[]{:S(2)}, u32[]{:S(2)}) collective-permute-start(bf16[32,2048]{1,0:T(8,128)(2,1)S(1)} %collective-permute-done.3.a1), channel_id=1, source_target_pairs={{0,2},{2,4},{4,6},{6,0},{1,3},{3,5},{5,7},{7,1},{8,10},{10,12},{12... | collective-permute-start | bytes 393224 | tf_op jit(solution)/shard_map/ppermute | solution.py:23
  86.9 6.7 %collective-permute-done.4.a2 = bf16[32,2048]{1,0:T(8,128)(2,1)S(1)} collective-permute-done((bf16[32,2048]{1,0:T(8,128)(2,1)S(1)}, bf16[32,2048]{1,0:T(8,128)(2,1)S(1)}, u32[]{:S(2)}, u32[]{:S(2)}) %collective-permute-start.4) | collective-permute-done | bytes 131104 | tf_op jit(solution)/shard_map/ppermute | solution.py:23
  97.3 55.9 %all_to_all.15.rows_hbm.x_ref.g_ref = bf16[32,2,16,2048]{3,2,1,0:T(8,128)(2,1)} all-to-all(bf16[32,2,16,2048]{3,2,1,0:T(8,128)(2,1)} %shard_map.104), channel_id=1, replica_groups=mesh['dp'=4,'y'=4,'x'=4,'z'=4,'c'=2] {'y','x','c'}, dimensions={0} | all-to-all | bytes 8388608 | tf_op jit(solution)/shard_map/all_to_all | solution.py:242
  153.2 6.9 %shard_map.105 = bf16[512,2048]{1,0:T(8,128)(2,1)} custom-call(bf16[32,2,16,2048]{3,2,1,0:T(8,128)(2,1)} %all_to_all.15.rows_hbm.x_ref.g_ref, bf16[2048,1152]{1,0:T(8,128)(2,1)} %all-gather.2.cloned.1.call-done.weights_hbm.w_ref), custom_call_target="tpu_custom_call" | custom-call | flops 2684354560 | bytes 10485760 | tf_op jit(solution)/shard_map/pallas_call | solution.py:158
  160.2 7.9 %all-to-all-start.1 = ((bf16[32,16,2048]{2,1,0:T(8,128)(2,1)}), bf16[32,16,2048]{2,1,0:T(8,128)(2,1)S(1)}, u32[]{:S(2)}, u32[]{:S(2)}) async-start(bf16[32,16,2048]{2,1,0:T(8,128)(2,1)} %bitcast.19), calls=%async_computation.1 | async-start | bytes 4194304 | tf_op jit(solution)/shard_map/all_to_all | solution.py:242
  168.1 8.8 %shard_map.106 = bf16[512,2048]{1,0:T(8,128)(2,1)} custom-call(bf16[32,2,16,2048]{3,2,1,0:T(8,128)(2,1)} %all_to_all.15.rows_hbm.x_ref.g_ref, bf16[32,2,16,2048]{3,2,1,0:T(8,128)(2,1)} %all_to_all.15.rows_hbm.x_ref.g_ref, bf16[2048,1152]{1,0:T(8,128)(2,1)} %all-gather.2.cloned.1.call-done.weights_hbm.w_ref), custom_call_target="tpu_custom_call" | custom-call | flops 3758096384 | bytes 10485760 | tf_op jit(solution)/shard_map/pallas_call | solution.py:198
  176.9 16.2 %all-to-all-done.1 = bf16[32,16,2048]{2,1,0:T(8,128)(2,1)S(1)} async-done(((bf16[32,16,2048]{2,1,0:T(8,128)(2,1)}), bf16[32,16,2048]{2,1,0:T(8,128)(2,1)S(1)}, u32[]{:S(2)}, u32[]{:S(2)}) %all-to-all-start.1) | async-done | bytes 2097184 | tf_op jit(solution)/shard_map/all_to_all | solution.py:242
  194.4 9.2 %all-to-all-start.2 = ((bf16[32,16,2048]{2,1,0:T(8,128)(2,1)}), bf16[32,16,2048]{2,1,0:T(8,128)(2,1)S(1)}, u32[]{:S(2)}, u32[]{:S(2)}) async-start(bf16[32,16,2048]{2,1,0:T(8,128)(2,1)} %bitcast.20), calls=%async_computation.2 | async-start | bytes 4194304 | tf_op jit(solution)/shard_map/all_to_all | solution.py:242
  204.9 3.4 %broadcast_select_fusion = bf16[1,512,2,384]{3,2,1,0:T(2,128)(2,1)} fusion(bf16[1,512,2,384]{3,2,1,0:T(2,128)(2,1)S(1)} %copy-done.8, pred[]{:T(512)S(6)} %eq.14, bf16[1,256,2,384]{3,2,1,0:T(2,128)(2,1)} %copy-done.12, bf16[1,256,2,384]{3,2,1,0:T(2,128)(2,1)} %copy-done.11), kind=kLoop, calls=%fused_computation | loop fusion | flops 786432 | bytes 2359297 | tf_op jit(solution)/shard_map/jit(_where)/select_n | solution.py:290
  209.8 7.6 %collective-permute-start.10 = (bf16[32,2048]{1,0:T(8,128)(2,1)S(1)}, bf16[32,2048]{1,0:T(8,128)(2,1)S(1)}, u32[]{:S(2)}, u32[]{:S(2)}) collective-permute-start(bf16[32,2048]{1,0:T(8,128)(2,1)S(1)} %get-tuple-element.37), channel_id=1, source_target_pairs={{0,6},{2,0},{4,2},{6,4},{1,7},{3,1},{5,3},{7,5},{8,14},{10,8},{12,... | collective-permute-start | bytes 393224 | tf_op jit(solution)/shard_map/ppermute | solution.py:23
  219.3 9.6 %collective-permute-start.9 = (bf16[32,2048]{1,0:T(8,128)(2,1)S(1)}, bf16[32,2048]{1,0:T(8,128)(2,1)S(1)}, u32[]{:S(2)}, u32[]{:S(2)}) collective-permute-start(bf16[32,2048]{1,0:T(8,128)(2,1)S(1)} %get-tuple-element.36), channel_id=1, source_target_pairs={{0,4},{2,6},{4,0},{6,2},{1,5},{3,7},{5,1},{7,3},{8,12},{10,14},{12... | collective-permute-start | bytes 393224 | tf_op jit(solution)/shard_map/ppermute | solution.py:23
  231.0 8.7 %collective-permute-start.12 = (bf16[32,2048]{1,0:T(8,128)(2,1)S(1)}, bf16[32,2048]{1,0:T(8,128)(2,1)S(1)}, u32[]{:S(2)}, u32[]{:S(2)}) collective-permute-start(bf16[32,2048]{1,0:T(8,128)(2,1)S(1)} %get-tuple-element.42), channel_id=1, source_target_pairs={{0,4},{2,6},{4,0},{6,2},{1,5},{3,7},{5,1},{7,3},{8,12},{10,14},{12... | collective-permute-start | bytes 393224 | tf_op jit(solution)/shard_map/ppermute | solution.py:23
  239.7 3.4 %collective-permute-start.13 = (bf16[32,2048]{1,0:T(8,128)(2,1)S(1)}, bf16[32,2048]{1,0:T(8,128)(2,1)S(1)}, u32[]{:S(2)}, u32[]{:S(2)}) collective-permute-start(bf16[32,2048]{1,0:T(8,128)(2,1)S(1)} %get-tuple-element.43), channel_id=1, source_target_pairs={{0,6},{2,0},{4,2},{6,4},{1,7},{3,1},{5,3},{7,5},{8,14},{10,8},{12,... | collective-permute-start | bytes 393224 | tf_op jit(solution)/shard_map/ppermute | solution.py:23
  243.1 5.8 %collective-permute-start.14 = (bf16[32,2048]{1,0:T(8,128)(2,1)S(1)}, bf16[32,2048]{1,0:T(8,128)(2,1)S(1)}, u32[]{:S(2)}, u32[]{:S(2)}) collective-permute-start(bf16[32,2048]{1,0:T(8,128)(2,1)S(1)} %get-tuple-element.44), channel_id=1, source_target_pairs={{0,2},{2,4},{4,6},{6,0},{1,3},{3,5},{5,7},{7,1},{8,10},{10,12},{12... | collective-permute-start | bytes 393224 | tf_op jit(solution)/shard_map/ppermute | solution.py:23
  249.6 3.3 %collective-permute-done.12 = bf16[32,2048]{1,0:T(8,128)(2,1)S(1)} collective-permute-done((bf16[32,2048]{1,0:T(8,128)(2,1)S(1)}, bf16[32,2048]{1,0:T(8,128)(2,1)S(1)}, u32[]{:S(2)}, u32[]{:S(2)}) %collective-permute-start.12) | collective-permute-done | bytes 131104 | tf_op jit(solution)/shard_map/ppermute | solution.py:23
  252.9 6.9 %collective-permute-done.13 = bf16[32,2048]{1,0:T(8,128)(2,1)S(1)} collective-permute-done((bf16[32,2048]{1,0:T(8,128)(2,1)S(1)}, bf16[32,2048]{1,0:T(8,128)(2,1)S(1)}, u32[]{:S(2)}, u32[]{:S(2)}) %collective-permute-start.13) | collective-permute-done | bytes 131104 | tf_op jit(solution)/shard_map/ppermute | solution.py:23
  259.9 4.0 %collective-permute-done.14 = bf16[32,2048]{1,0:T(8,128)(2,1)S(1)} collective-permute-done((bf16[32,2048]{1,0:T(8,128)(2,1)S(1)}, bf16[32,2048]{1,0:T(8,128)(2,1)S(1)}, u32[]{:S(2)}, u32[]{:S(2)}) %collective-permute-start.14) | collective-permute-done | bytes 131104 | tf_op jit(solution)/shard_map/ppermute | solution.py:23
  (79 shorter events, 34.1 us)
Async XLA Ops:
  7.2 146.1 %all-gather.2.cloned.1.call-start = ((), (), s32[]{:S(2)}) async-start(), calls=%async_computation.3 | async-start | bytes 5898240 | tf_op jit(solution)/shard_map/all_gather | solution.py:258
  11.3 69.8 %copy-start.2 = (bf16[32,2176]{1,0:T(8,128)(2,1)}, bf16[32,2176]{1,0:T(8,128)(2,1)S(1)}, u32[]{:S(2)}) copy-start(bf16[32,2176]{1,0:T(8,128)(2,1)S(1)} %pad_maximum_fusion.1.f0.a0) | copy-start | bytes 417796
  11.3 29.3 %collective-permute-start.1 = (bf16[32,2176]{1,0:T(8,128)(2,1)S(1)}, bf16[32,2176]{1,0:T(8,128)(2,1)S(1)}, u32[]{:S(2)}, u32[]{:S(2)}) collective-permute-start(bf16[32,2176]{1,0:T(8,128)(2,1)S(1)} %pad_maximum_fusion.1.f0.a0), channel_id=1, source_target_pairs={{0,6},{2,0},{4,2},{6,4},{1,7},{3,1},{5,3},{7,5},{8,14},{10,8},{12,... | collective-permute-start | bytes 417800 | tf_op jit(solution)/shard_map/ppermute | solution.py:23
  22.8 15.8 %collective-permute-start.3 = (bf16[32,2048]{1,0:T(8,128)(2,1)S(1)}, bf16[32,2048]{1,0:T(8,128)(2,1)S(1)}, u32[]{:S(2)}, u32[]{:S(2)}) collective-permute-start(bf16[32,2048]{1,0:T(8,128)(2,1)S(1)} %bitcast.25), channel_id=1, source_target_pairs={{0,2},{2,4},{4,6},{6,0},{1,3},{3,5},{5,7},{7,1},{8,10},{10,12},{12... | collective-permute-start | bytes 393224 | tf_op jit(solution)/shard_map/ppermute | solution.py:23
  26.2 71.1 %collective-permute-start.6 = (bf16[1,256,2,384]{3,2,1,0:T(2,128)(2,1)}, bf16[1,256,2,384]{3,2,1,0:T(2,128)(2,1)S(1)}, u32[]{:S(2)}, u32[]{:S(2)}) collective-permute-start(bf16[1,256,2,384]{3,2,1,0:T(2,128)(2,1)} %get-tuple-element.49), channel_id=1, source_target_pairs={{0,64},{32,96},{64,0},{96,32},{1,65},{33,97},{65,1},{97,33},{2,66}... | collective-permute-start | bytes 1179656 | tf_op jit(solution)/shard_map/ppermute | solution.py:271
  28.1 69.1 %collective-permute-start.7 = (bf16[1,256,2,384]{3,2,1,0:T(2,128)(2,1)}, bf16[1,256,2,384]{3,2,1,0:T(2,128)(2,1)S(1)}, u32[]{:S(2)}, u32[]{:S(2)}) collective-permute-start(bf16[1,256,2,384]{3,2,1,0:T(2,128)(2,1)} %get-tuple-element.48), channel_id=1, source_target_pairs={{0,64},{32,96},{64,0},{96,32},{1,65},{33,97},{65,1},{97,33},{2,66}... | collective-permute-start | bytes 1179656 | tf_op jit(solution)/shard_map/ppermute | solution.py:271
  33.0 64.3 %collective-permute-start.8 = (bf16[1,512,384]{2,1,0:T(8,128)(2,1)S(1)}, bf16[1,512,384]{2,1,0:T(8,128)(2,1)}, u32[]{:S(2)}, u32[]{:S(2)}) collective-permute-start(bf16[1,512,384]{2,1,0:T(8,128)(2,1)S(1)} %copy-done.9), channel_id=1, source_target_pairs={{0,64},{32,96},{64,0},{96,32},{1,65},{33,97},{65,1},{97,33},{2,66}... | collective-permute-start | bytes 1179656 | tf_op jit(solution)/shard_map/ppermute | solution.py:272
  38.6 45.4 %copy-start.14 = (bf16[32,2048]{1,0:T(8,128)(2,1)}, bf16[32,2048]{1,0:T(8,128)(2,1)S(1)}, u32[]{:S(2)}) copy-start(bf16[32,2048]{1,0:T(8,128)(2,1)S(1)} %collective-permute-done.3.a1) | copy-start | bytes 393220
  38.6 23.9 %collective-permute-start = (bf16[32,2176]{1,0:T(8,128)(2,1)S(1)}, bf16[32,2176]{1,0:T(8,128)(2,1)S(1)}, u32[]{:S(2)}, u32[]{:S(2)}) collective-permute-start(bf16[32,2176]{1,0:T(8,128)(2,1)S(1)} %pad_maximum_fusion.1.f0.a0), channel_id=1, source_target_pairs={{0,2},{2,4},{4,6},{6,0},{1,3},{3,5},{5,7},{7,1},{8,10},{10,12},{12... | collective-permute-start | bytes 417800 | tf_op jit(solution)/shard_map/ppermute | solution.py:23
  40.5 40.5 %copy-start.3 = (bf16[32,2176]{1,0:T(8,128)(2,1)}, bf16[32,2176]{1,0:T(8,128)(2,1)S(1)}, u32[]{:S(2)}) copy-start(bf16[32,2176]{1,0:T(8,128)(2,1)S(1)} %collective-permute-done.1.f3.a3) | copy-start | bytes 417796
  40.6 34.5 %collective-permute-start.2 = (bf16[32,2176]{1,0:T(8,128)(2,1)S(1)}, bf16[32,2176]{1,0:T(8,128)(2,1)S(1)}, u32[]{:S(2)}, u32[]{:S(2)}) collective-permute-start(bf16[32,2176]{1,0:T(8,128)(2,1)S(1)} %collective-permute-done.1.f3.a3), channel_id=1, source_target_pairs={{0,6},{2,0},{4,2},{6,4},{1,7},{3,1},{5,3},{7,5},{8,14},{10,8},{12,... | collective-permute-start | bytes 417800 | tf_op jit(solution)/shard_map/ppermute | solution.py:23
  62.5 24.4 %collective-permute-start.5 = (bf16[32,2048]{1,0:T(8,128)(2,1)S(1)}, bf16[32,2048]{1,0:T(8,128)(2,1)S(1)}, u32[]{:S(2)}, u32[]{:S(2)}) collective-permute-start(bf16[32,2048]{1,0:T(8,128)(2,1)S(1)} %bitcast.26), channel_id=1, source_target_pairs={{0,6},{2,0},{4,2},{6,4},{1,7},{3,1},{5,3},{7,5},{8,14},{10,8},{12,... | collective-permute-start | bytes 393224 | tf_op jit(solution)/shard_map/ppermute | solution.py:23
  75.0 18.5 %collective-permute-start.4 = (bf16[32,2048]{1,0:T(8,128)(2,1)S(1)}, bf16[32,2048]{1,0:T(8,128)(2,1)S(1)}, u32[]{:S(2)}, u32[]{:S(2)}) collective-permute-start(bf16[32,2048]{1,0:T(8,128)(2,1)S(1)} %collective-permute-done.3.a1), channel_id=1, source_target_pairs={{0,2},{2,4},{4,6},{6,0},{1,3},{3,5},{5,7},{7,1},{8,10},{10,12},{12... | collective-permute-start | bytes 393224 | tf_op jit(solution)/shard_map/ppermute | solution.py:23
  97.3 62.9 %copy-start.11 = (bf16[1,256,2,384]{3,2,1,0:T(2,128)(2,1)}, bf16[1,256,2,384]{3,2,1,0:T(2,128)(2,1)S(1)}, u32[]{:S(2)}) copy-start(bf16[1,256,2,384]{3,2,1,0:T(2,128)(2,1)S(1)} %collective-permute-done.6) | copy-start | bytes 1179652
  97.3 62.9 %copy-start.12 = (bf16[1,256,2,384]{3,2,1,0:T(2,128)(2,1)}, bf16[1,256,2,384]{3,2,1,0:T(2,128)(2,1)S(1)}, u32[]{:S(2)}) copy-start(bf16[1,256,2,384]{3,2,1,0:T(2,128)(2,1)S(1)} %collective-permute-done.7) | copy-start | bytes 1179652
  160.2 32.9 %all-to-all-start.1 = ((bf16[32,16,2048]{2,1,0:T(8,128)(2,1)}), bf16[32,16,2048]{2,1,0:T(8,128)(2,1)S(1)}, u32[]{:S(2)}, u32[]{:S(2)}) async-start(bf16[32,16,2048]{2,1,0:T(8,128)(2,1)} %bitcast.19), calls=%async_computation.1 | async-start | bytes 4194304 | tf_op jit(solution)/shard_map/all_to_all | solution.py:242
  194.4 35.4 %all-to-all-start.2 = ((bf16[32,16,2048]{2,1,0:T(8,128)(2,1)}), bf16[32,16,2048]{2,1,0:T(8,128)(2,1)S(1)}, u32[]{:S(2)}, u32[]{:S(2)}) async-start(bf16[32,16,2048]{2,1,0:T(8,128)(2,1)} %bitcast.20), calls=%async_computation.2 | async-start | bytes 4194304 | tf_op jit(solution)/shard_map/all_to_all | solution.py:242
  204.9 24.0 %copy-start.10 = (bf16[1,512,384]{2,1,0:T(8,128)(2,1)S(1)}, bf16[1,512,384]{2,1,0:T(8,128)(2,1)}, u32[]{:S(2)}) copy-start(bf16[1,512,384]{2,1,0:T(8,128)(2,1)} %param.13) | copy-start | bytes 1179652
  209.8 33.3 %collective-permute-start.10 = (bf16[32,2048]{1,0:T(8,128)(2,1)S(1)}, bf16[32,2048]{1,0:T(8,128)(2,1)S(1)}, u32[]{:S(2)}, u32[]{:S(2)}) collective-permute-start(bf16[32,2048]{1,0:T(8,128)(2,1)S(1)} %get-tuple-element.37), channel_id=1, source_target_pairs={{0,6},{2,0},{4,2},{6,4},{1,7},{3,1},{5,3},{7,5},{8,14},{10,8},{12,... | collective-permute-start | bytes 393224 | tf_op jit(solution)/shard_map/ppermute | solution.py:23
  217.4 31.5 %collective-permute-start.11 = (bf16[32,2048]{1,0:T(8,128)(2,1)S(1)}, bf16[32,2048]{1,0:T(8,128)(2,1)S(1)}, u32[]{:S(2)}, u32[]{:S(2)}) collective-permute-start(bf16[32,2048]{1,0:T(8,128)(2,1)S(1)} %get-tuple-element.38), channel_id=1, source_target_pairs={{0,2},{2,4},{4,6},{6,0},{1,3},{3,5},{5,7},{7,1},{8,10},{10,12},{12... | collective-permute-start | bytes 393224 | tf_op jit(solution)/shard_map/ppermute | solution.py:23
  219.3 29.6 %collective-permute-start.9 = (bf16[32,2048]{1,0:T(8,128)(2,1)S(1)}, bf16[32,2048]{1,0:T(8,128)(2,1)S(1)}, u32[]{:S(2)}, u32[]{:S(2)}) collective-permute-start(bf16[32,2048]{1,0:T(8,128)(2,1)S(1)} %get-tuple-element.36), channel_id=1, source_target_pairs={{0,4},{2,6},{4,0},{6,2},{1,5},{3,7},{5,1},{7,3},{8,12},{10,14},{12... | collective-permute-start | bytes 393224 | tf_op jit(solution)/shard_map/ppermute | solution.py:23
  231.0 21.9 %collective-permute-start.12 = (bf16[32,2048]{1,0:T(8,128)(2,1)S(1)}, bf16[32,2048]{1,0:T(8,128)(2,1)S(1)}, u32[]{:S(2)}, u32[]{:S(2)}) collective-permute-start(bf16[32,2048]{1,0:T(8,128)(2,1)S(1)} %get-tuple-element.42), channel_id=1, source_target_pairs={{0,4},{2,6},{4,0},{6,2},{1,5},{3,7},{5,1},{7,3},{8,12},{10,14},{12... | collective-permute-start | bytes 393224 | tf_op jit(solution)/shard_map/ppermute | solution.py:23
  239.7 20.2 %collective-permute-start.13 = (bf16[32,2048]{1,0:T(8,128)(2,1)S(1)}, bf16[32,2048]{1,0:T(8,128)(2,1)S(1)}, u32[]{:S(2)}, u32[]{:S(2)}) collective-permute-start(bf16[32,2048]{1,0:T(8,128)(2,1)S(1)} %get-tuple-element.43), channel_id=1, source_target_pairs={{0,6},{2,0},{4,2},{6,4},{1,7},{3,1},{5,3},{7,5},{8,14},{10,8},{12,... | collective-permute-start | bytes 393224 | tf_op jit(solution)/shard_map/ppermute | solution.py:23
  243.1 20.8 %collective-permute-start.14 = (bf16[32,2048]{1,0:T(8,128)(2,1)S(1)}, bf16[32,2048]{1,0:T(8,128)(2,1)S(1)}, u32[]{:S(2)}, u32[]{:S(2)}) collective-permute-start(bf16[32,2048]{1,0:T(8,128)(2,1)S(1)} %get-tuple-element.44), channel_id=1, source_target_pairs={{0,2},{2,4},{4,6},{6,0},{1,3},{3,5},{5,7},{7,1},{8,10},{10,12},{12... | collective-permute-start | bytes 393224 | tf_op jit(solution)/shard_map/ppermute | solution.py:23
  (15 other events, 107.6 us)
Sparse Core Ops, SparseCore 0:
  10.9 126.0 all-gather.1
